TPU v7x, 32 devices: a whole 2x2x4 slice. The times are simulated.
32 devices in a mesh: grp: 2 (over x), vir: 16 (over z, y, core).
Axes of the slice: x: 2, y: 2, z: 4, core: 2. Of those that a mesh axis runs over, the one named last changes fastest.
Arguments:
- amplitudes: bfloat16 [256, 1024, 1024], P(('grp', 'vir')), parts along dimension 0, may hold values from -0.0625 to 0.0625
- integrals: bfloat16 [2, 128, 1024, 1024], P('grp', None, 'vir'), parts along dimension 0, may hold values from -6 to 6
- pair_energy: float32 [2], P('grp'), parts along dimension 0, may hold values from -3 to -0.5
- vir_energy: float32 [2048], P('grp'), parts along dimension 0, may hold values from 0.25 to 3
Outputs:
- update: float32 [2048, 1, 1024], P(('grp', 'vir')), parts along dimension 0
There are 2 independent parts, one for each index of `grp`. A program takes and returns all parts, laid end to end along the dimension named above; each array names one. Nothing has to cross between parts.
All inputs are finite; a program needn't handle non-finite values.
Results may differ from a plain program's by a relative error of at most 0.0003.
Values may be sent and summed in bfloat16 or wider, within the bound.
No kernel may reach another device: no remote copies, remote signals or barrier semaphores. Data moves between devices by JAX's collectives and lax.ppermute only.
A program may use at most 128 MiB of HBM per device.

v0:
```python
import jax
import jax.numpy as jnp
from jax import lax
from jax.sharding import PartitionSpec as P


def body(amplitudes, integrals, pair_energy, vir_energy):
    local_row_block = lax.all_to_all(integrals, "vir", split_axis=1, concat_axis=2, tiled=True)
    slab_rows = local_row_block.shape[2] // lax.axis_size("vir")
    cycle_part = lax.psum_scatter(
        jnp.einsum(
            "lgif,gfh->ilh", local_row_block, amplitudes, preferred_element_type=jnp.float32
        ),
        "vir",
        scatter_dimension=0,
        tiled=True,
    )
    swapped_term = lax.all_to_all(cycle_part, "vir", split_axis=2, concat_axis=0, tiled=True)
    symmetric_total = cycle_part + jnp.transpose(swapped_term, (2, 1, 0))
    start_row = lax.axis_index("vir") * slab_rows
    block_orbital_energy = lax.dynamic_slice_in_dim(vir_energy, start_row, slab_rows, 0)
    energy_denominator = (
        pair_energy[None, :, None] - vir_energy[None, None, :] - block_orbital_energy[:, None, None]
    )
    return symmetric_total / energy_denominator


def solution(mesh):
    in_specs = (P(("grp", "vir"), None, None), P("grp", None, "vir", None), P("grp"), P("grp"))
    out_specs = P(("grp", "vir"), None, None)
    return jax.shard_map(body, mesh=mesh, in_specs=in_specs, out_specs=out_specs, check_vma=False)
```

profile of v0, /device:TPU:0, one launch (start us, length us, event | category | flops | bytes accessed | tf_op | source)
XLA Modules:
  0.0 554.9 jit_solution(5251866372057170928)
XLA Ops:
  6.5 0.0 all-reduce.3.cloned.1.call-start
  6.5 369.3 %all_to_all.33 = bf16[1,128,64,1024]{3,2,0,1:T(8,128)(2,1)S(1)} all-to-all(bf16[1,128,64,1024]{3,2,0,1:T(8,128)(2,1)} %bitcast.30), channel_id=1, replica_groups=mesh['grp'=2,'vir'=16] {'vir'}, dimensions={1} | all-to-all | bytes 33554432 | tf_op jit(solution)/shard_map/all_to_all | solution.py:8
  375.8 2.2 copy.10
  378.0 0.0 copy-start.1
  378.1 0.0 copy-start
  378.1 22.3 %convolution_bitcast_fusion = f32[1024,1,1024]{0,2,1:T(8,128)} fusion(bf16[8,1024,1024]{2,1,0:T(8,128)(2,1)} %param.4, bf16[8,1024,1024]{2,1,0:T(8,128)(2,1)S(1)} %bitcast.31), kind=kOutput, calls=%fused_computation | convolution fusion | flops 17179869184 | bytes 37748736 | tf_op jit(solution)/shard_map/lgif,gfh->ilh/dot_general | solution.py:11
  400.4 11.0 %copy.12 = f32[1024,1,1024]{2,1,0:T(1,128)} copy(f32[1024,1,1024]{0,2,1:T(8,128)} %convolution_bitcast_fusion) | data formatting | bytes 8388608 | tf_op jit(solution)/shard_map/lgif,gfh->ilh/transpose | solution.py:11
  411.4 0.0 all-reduce.3.cloned.1.call-update
  411.4 0.0 copy-done.1
  411.4 0.6 dynamic-slice
  412.7 112.1 %all-reduce.3.cloned.1.call-done = f32[1024,1,1024]{2,1,0:T(1,128)} async-done(((f32[1024,1,1024]{2,1,0:T(1,128)}), f32[1024,1,1024]{2,1,0:T(1,128)}) %all-reduce.3.cloned.1.call-update) | async-done | bytes 4194320
  524.8 1.0 constant_dynamic-slice_fusion
  525.8 0.3 copy.13
  526.1 0.5 broadcast.36
  526.6 2.0 reduce
  528.6 1.0 reshape.56
  529.6 3.6 all-to-all-start.1
  533.9 0.0 copy-done
  533.9 0.1 dynamic_slice.3
  534.0 9.3 %all-to-all-done.1 = f32[16,1,4096]{2,1,0:T(1,128)S(1)} async-done(((f32[16,1,4096]{2,1,0:T(1,128)}), f32[16,1,4096]{2,1,0:T(1,128)S(1)}, u32[]{:S(2)}, u32[]{:S(2)}) %all-to-all-start.1) | async-done | bytes 262176 | tf_op jit(solution)/shard_map/all_to_all | solution.py:18
  543.3 1.3 reduce.1
  544.6 0.7 reshape.57
  545.3 0.3 copy.17
  545.6 0.3 all_to_all.30
  545.9 2.2 fusion
  (1 shorter events, 0.0 us)
Async XLA Ops:
  6.5 518.2 %all-reduce.3.cloned.1.call-start = ((), (), s32[]{:S(2)}) async-start(), calls=%async_computation.2 | async-start | bytes 8388608
  378.0 33.4 %copy-start.1 = (u32[32]{0:T(128)S(1)}, u32[32]{0:T(128)}, u32[]{:S(2)}) copy-start(u32[32]{0:T(128)} %constant.15) | copy-start | bytes 388
  378.1 155.9 %copy-start = (f32[1024]{0:T(1024)S(1)}, f32[1024]{0:T(1024)}, u32[]{:S(2)}) copy-start(f32[1024]{0:T(1024)} %param.7) | copy-start | bytes 12292
  529.6 13.7 %all-to-all-start.1 = ((f32[16,1,4096]{2,1,0:T(1,128)}), f32[16,1,4096]{2,1,0:T(1,128)S(1)}, u32[]{:S(2)}, u32[]{:S(2)}) async-start(f32[16,1,4096]{2,1,0:T(1,128)} %reshape.56), calls=%async_computation.1 | async-start | bytes 524288 | tf_op jit(solution)/shard_map/all_to_all | solution.py:18
Sparse Core Ops, SparseCore 0:
  411.5 113.1 all-reduce.2
where the time goes:
time: 556 us; the launch traced here: 555 us
  blocking collectives  369 us (66%)
  waiting for transfers between devices  121 us (22%)
  matrix products  22.3 us (4%)
  local copies, waits for them, and re-layouts  18 us (3%)
  between operations  14.8 us (3%)
    all_to_all x1, blocking collectives, body(): lax.all_to_all(integrals, 'vir', split_axis=1, concat_axis=2, tiled=True)  369 us
    unnamed x2, waiting for transfers between devices  112 us
    dot_general x1, matrix products, body(): jnp.einsum('lgif,gfh->ilh', local_row_block, amplitudes, preferred_elemen...  22.3 us
  transfers between devices with their start and end apart: 2, of which 2 were waited for; matrix products, arithmetic and copies ran while one was open for 0% of the time, Pallas kernels for 0%

commit v1 on v0

v1 whole, which is shorter than its diff:
```python
import jax
import jax.numpy as jnp
from jax import lax
from jax.sharding import PartitionSpec as P

AXIS = "vir"
IN_FLIGHT = 4


def denominator(pair_energy, vir_energy, start, rows):
    mine = lax.dynamic_slice_in_dim(vir_energy, start, rows, 0)
    return pair_energy[None, :, None] - vir_energy[None, None, :] - mine[:, None, None]


def gathered_body(amplitudes, integrals, pair_energy, vir_energy):
    blocks = lax.all_to_all(integrals, AXIS, split_axis=1, concat_axis=2, tiled=True)
    rows = blocks.shape[2] // lax.axis_size(AXIS)
    part = jnp.einsum("lgif,gfh->ilh", blocks, amplitudes, preferred_element_type=jnp.float32)
    cycle = lax.psum_scatter(part, AXIS, scatter_dimension=0, tiled=True)
    swapped = lax.all_to_all(cycle, AXIS, split_axis=2, concat_axis=0, tiled=True)
    paired = cycle + jnp.transpose(swapped, (2, 1, 0))
    return paired / denominator(pair_energy, vir_energy, lax.axis_index(AXIS) * rows, rows)


def paired_with(n, s):
    return [(i, i ^ s) for i in range(n)]


def after(x, *deps):
    deps = [d for d in deps if d is not None]
    if not deps:
        return x
    return lax.optimization_barrier((x, *deps))[0]


def exchanged_body(amplitudes, integrals, pair_energy, vir_energy):
    n = lax.axis_size(AXIS)
    half = n // 2
    me = lax.axis_index(AXIS)
    own, e, a = amplitudes.shape
    rows = integrals.shape[2]
    source = integrals.reshape(integrals.shape[1:])
    chunks = 4
    r = rows // chunks

    order = []
    for k in range(half):
        order.append(half + k)
        if k + 1 < half:
            order.append(k + 1)

    def piece(s, start, size, *deps):
        src = after(source, *deps)
        return lax.dynamic_slice(src, ((me ^ s) * own, start, 0), (own, size, e))

    flight = []
    sums = None
    stage = None
    cycle_rows = []
    for q in range(chunks):
        got = {0: lax.dynamic_slice(source, (me * own, q * r, 0), (own, r, e))}
        pending = stage or []
        for k, s in enumerate(order):
            deps = [flight[-IN_FLIGHT]] if len(flight) >= IN_FLIGHT else []
            if pending and k % 3 == 2:
                deps.append(pending.pop(0)())
            out = lax.ppermute(piece(s, q * r, r, *deps), AXIS, paired_with(n, s))
            flight.append(out)
            got[s] = out
        while pending:
            pending.pop(0)()
        lhs = jnp.concatenate([got[s] for s in range(n)], axis=1)

        state = {}

        def multiply(lhs=lhs, state=state):
            state["x"] = jnp.einsum(
                "mre,mea->ra", lhs, amplitudes, preferred_element_type=jnp.float32
            ).reshape(n, r, a)
            return state["x"]

        def halve(bit, state=state):
            x = state["x"].reshape(-1, 2, r, a)
            moved = lax.ppermute(x[:, 1], AXIS, paired_with(n, bit))
            state["x"] = x[:, 0] + moved
            return state["x"]

        def last(state=state):
            x = state["x"]
            moved = lax.ppermute(x[1], AXIS, paired_with(n, half))
            state["x"] = x[0] + moved
            cycle_rows.append(state["x"])
            return state["x"]

        stage = [multiply]
        bit = 1
        while bit < half:
            stage.append(lambda bit=bit, halve=halve: halve(bit))
            bit *= 2
        stage.append(last)
    for step in stage:
        step()
    cycle = jnp.concatenate(cycle_rows, axis=0)
    swapped = lax.all_to_all(
        cycle.reshape(rows, n, a // n).transpose(1, 0, 2), AXIS, split_axis=0, concat_axis=0, tiled=True
    )
    paired = cycle + swapped.reshape(n * rows, a // n).T
    return paired[:, None, :] / denominator(pair_energy, vir_energy, me * rows, rows)


def solution(mesh):
    n = mesh.shape[AXIS]
    body = exchanged_body if n & (n - 1) == 0 and n <= 16 else gathered_body
    in_specs = (P(("grp", AXIS), None, None), P("grp", None, AXIS, None), P("grp"), P("grp"))
    out_specs = P(("grp", AXIS), None, None)
    return jax.shard_map(body, mesh=mesh, in_specs=in_specs, out_specs=out_specs, check_vma=False)
```

time: 556 us -> 476 us (0.86)
  blocking collectives: 369 us -> 0 us
  starting transfers between devices: 3.63 us -> 140 us
  waiting for transfers between devices: 121 us -> 251 us
  local copies, waits for them, and re-layouts: 18 us -> 43.8 us
  matrix products: 22.3 us -> 36.1 us
  between operations: 14.8 us -> 1.86 us
    all_to_all x1 -> x0, blocking collectives: 369 us -> none  [body(): lax.all_to_all(integrals, 'vir', split_axis=1, concat_axis=2, tiled=True)]
    ppermute x0 -> x76, waiting for transfers between devices: none -> 242 us  [the longest x60 179 us: exchanged_body(): out = lax.ppermute(piece(s, q * r, r, *deps), AXIS, paired_with(n, s))]
    ppermute x0 -> x76, starting transfers between devices: none -> 137 us  [the longest x60 125 us: exchanged_body(): out = lax.ppermute(piece(s, q * r, r, *deps), AXIS, paired_with(n, s))]
    unnamed x2 -> x0, waiting for transfers between devices: 112 us -> none
    unnamed x9 -> x73, local copies, waits for them, and re-layouts: 3.8 us -> 25.9 us
    dot_general x1 -> x4, matrix products: 22.3 us -> 36.1 us  [multiply(): jnp.einsum('mre,mea->ra', lhs, amplitudes, preferred_element_type=jnp.flo...]
    dynamic_slice x1 -> x58, local copies, waits for them, and re-layouts: 0.08 us -> 13.9 us  [the longest x57 13.8 us: piece(): return lax.dynamic_slice(src, ((me ^ s) * own, start, 0), (own, size, e))]
    transpose x1 -> x0, local copies, waits for them, and re-layouts: 11 us -> none  [body(): jnp.einsum('lgif,gfh->ilh', local_row_block, amplitudes, preferred_elemen...]
  transfers between devices with their start and end apart: 2 -> 77, of which waited for: 2 -> 38; matrix products, arithmetic and copies ran while one was open for 0% -> 14% of each run, Pallas kernels for 0% -> 0%
where the time goes in v1:
time: 476 us; the launch traced here: 475 us
  waiting for transfers between devices  251 us (53%)
  starting transfers between devices  140 us (29%)
  local copies, waits for them, and re-layouts  43.8 us (9%)
  matrix products  36.1 us (8%)
    ppermute x60, waiting for transfers between devices, exchanged_body(): out = lax.ppermute(piece(s, q * r, r, *deps), AXIS, paired_with(n, s))  179 us
    ppermute x60, starting transfers between devices, exchanged_body(): out = lax.ppermute(piece(s, q * r, r, *deps), AXIS, paired_with(n, s))  125 us
    dot_general x4, matrix products, multiply(): jnp.einsum('mre,mea->ra', lhs, amplitudes, preferred_element_type=jnp.flo...  36.1 us
    ppermute x4, waiting for transfers between devices, last(): moved = lax.ppermute(x[1], AXIS, paired_with(n, half))  34 us
    ppermute x12, waiting for transfers between devices, halve(): moved = lax.ppermute(x[:, 1], AXIS, paired_with(n, bit))  28.9 us
    unnamed x73, local copies, waits for them, and re-layouts  25.9 us
    dynamic_slice x57, local copies, waits for them, and re-layouts, piece(): return lax.dynamic_slice(src, ((me ^ s) * own, start, 0), (own, size, e))  13.8 us
  transfers between devices with their start and end apart: 77, of which 38 were waited for; matrix products, arithmetic and copies ran while one was open for 14% of the time, Pallas kernels for 0%

profile of v1, /device:TPU:0, one launch (start us, length us, event | category | flops | bytes accessed | tf_op | source)
XLA Modules:
  0.0 475.3 jit_solution(11438915568430341378)
XLA Ops:
  1.8 2.6 collective-permute-start.1
  4.4 2.6 collective-permute-start.7
  7.0 2.3 bitcast_dynamic-update-slice_fusion.1
  12.3 1.9 collective-permute-start.3
  14.1 11.5 %collective-permute-done.7 = bf16[8,16,1024]{2,1,0:T(8,128)(2,1)S(1)} collective-permute-done((bf16[8,16,1024]{2,1,0:T(8,128)(2,1)S(1)}, bf16[8,16,1024]{2,1,0:T(8,128)(2,1)S(1)}, u32[]{:S(2)}, u32[]{:S(2)}) %collective-permute-start.7) | collective-permute-done | bytes 262176 | tf_op jit(solution)/shard_map/ppermute | solution.py:67
  26.7 3.0 collective-permute-done.8
  33.3 13.0 %collective-permute-start.4 = (bf16[8,16,1024]{2,1,0:T(8,128)(2,1)S(1)}, bf16[8,16,1024]{2,1,0:T(8,128)(2,1)S(1)}, u32[]{:S(2)}, u32[]{:S(2)}) collective-permute-start(bf16[8,16,1024]{2,1,0:T(8,128)(2,1)S(1)} %constant_dynamic-slice_fusion.53), channel_id=1, source_target_pairs={{0,5},{1,4},{2,7},{3,6},{4,1},{5,0},{6,3},{7,2},{8,13},{9,12},{10,... | collective-permute-start | bytes 786440 | tf_op jit(solution)/shard_map/ppermute | solution.py:67
  49.4 2.7 collective-permute-start.11
  53.0 4.2 collective-permute-start.12
  59.7 7.9 %collective-permute-done.11 = bf16[8,16,1024]{2,1,0:T(8,128)(2,1)S(1)} collective-permute-done((bf16[8,16,1024]{2,1,0:T(8,128)(2,1)S(1)}, bf16[8,16,1024]{2,1,0:T(8,128)(2,1)S(1)}, u32[]{:S(2)}, u32[]{:S(2)}) %collective-permute-start.11) | collective-permute-done | bytes 262176 | tf_op jit(solution)/shard_map/ppermute | solution.py:67
  68.6 1.9 collective-permute-start.13
  70.5 2.1 collective-permute-done.12
  73.5 1.9 collective-permute-start.14
  76.4 4.2 collective-permute-start.26
  88.2 2.0 collective-permute-done.14
  90.9 9.6 %fusion.18 = f32[256,1024,1]{1,0,2:T(8,128)S(1)} fusion(bf16[8,256,1024]{2,1,0:T(8,128)(2,1)} %constant_dynamic-update-slice_fusion, bf16[8,1024,1024]{2,1,0:T(8,128)(2,1)} %param.4), kind=kOutput, calls=%fused_computation.177 | convolution fusion | flops 4294967296 | bytes 22020096 | tf_op jit(solution)/shard_map/mre,mea->ra/dot_general | solution.py:77
  101.6 16.4 %collective-permute-start.27 = (bf16[8,16,1024]{2,1,0:T(8,128)(2,1)S(1)}, bf16[8,16,1024]{2,1,0:T(8,128)(2,1)S(1)}, u32[]{:S(2)}, u32[]{:S(2)}) collective-permute-start(bf16[8,16,1024]{2,1,0:T(8,128)(2,1)S(1)} %constant_dynamic-slice_fusion.36), channel_id=1, source_target_pairs={{0,9},{1,8},{2,11},{3,10},{4,13},{5,12},{6,15},{7,14},{8,1},{9,0},... | collective-permute-start | bytes 786440 | tf_op jit(solution)/shard_map/ppermute | solution.py:67
  120.1 15.5 %collective-permute-done.27 = bf16[8,16,1024]{2,1,0:T(8,128)(2,1)S(1)} collective-permute-done((bf16[8,16,1024]{2,1,0:T(8,128)(2,1)S(1)}, bf16[8,16,1024]{2,1,0:T(8,128)(2,1)S(1)}, u32[]{:S(2)}, u32[]{:S(2)}) %collective-permute-start.27) | collective-permute-done | bytes 262176 | tf_op jit(solution)/shard_map/ppermute | solution.py:67
  135.8 2.6 collective-permute-start.22
  140.4 12.4 %collective-permute-done.29 = bf16[8,16,1024]{2,1,0:T(8,128)(2,1)S(1)} collective-permute-done((bf16[8,16,1024]{2,1,0:T(8,128)(2,1)S(1)}, bf16[8,16,1024]{2,1,0:T(8,128)(2,1)S(1)}, u32[]{:S(2)}, u32[]{:S(2)}) %collective-permute-start.29) | collective-permute-done | bytes 262176 | tf_op jit(solution)/shard_map/ppermute | solution.py:67
  156.3 4.4 collective-permute-done.21
  161.0 5.3 %collective-permute-done.17 = f32[2,16,1024]{2,1,0:T(8,128)S(1)} collective-permute-done((f32[2,16,1024]{2,1,0:T(8,128)S(1)}, f32[2,16,1024]{2,1,0:T(8,128)S(1)}, u32[]{:S(2)}, u32[]{:S(2)}) %collective-permute-start.17) | collective-permute-done | bytes 131104 | tf_op jit(solution)/shard_map/ppermute | solution.py:84
  167.3 2.3 collective-permute-start.24
  169.6 9.6 %collective-permute-done.18 = f32[16,1024]{1,0:T(8,128)S(1)} collective-permute-done((f32[16,1024]{1,0:T(8,128)S(1)}, f32[16,1024]{1,0:T(8,128)S(1)}, u32[]{:S(2)}, u32[]{:S(2)}) %collective-permute-start.18) | collective-permute-done | bytes 65568 | tf_op jit(solution)/shard_map/ppermute | solution.py:90
  179.3 2.3 collective-permute-start.33
  181.7 2.8 collective-permute-start.32
  185.2 2.3 collective-permute-start.45
  187.5 3.4 collective-permute-done.33
  191.9 7.2 %collective-permute-done.25 = bf16[8,16,1024]{2,1,0:T(8,128)(2,1)S(1)} collective-permute-done((bf16[8,16,1024]{2,1,0:T(8,128)(2,1)S(1)}, bf16[8,16,1024]{2,1,0:T(8,128)(2,1)S(1)}, u32[]{:S(2)}, u32[]{:S(2)}) %collective-permute-start.25) | collective-permute-done | bytes 262176 | tf_op jit(solution)/shard_map/ppermute | solution.py:67
  199.3 6.8 %collective-permute-done.32 = bf16[8,16,1024]{2,1,0:T(8,128)(2,1)S(1)} collective-permute-done((bf16[8,16,1024]{2,1,0:T(8,128)(2,1)S(1)}, bf16[8,16,1024]{2,1,0:T(8,128)(2,1)S(1)}, u32[]{:S(2)}, u32[]{:S(2)}) %collective-permute-start.32) | collective-permute-done | bytes 262176 | tf_op jit(solution)/shard_map/ppermute | solution.py:67
  206.1 8.4 %fusion.19 = f32[256,1024,1]{1,0,2:T(8,128)S(1)} fusion(bf16[8,256,1024]{2,1,0:T(8,128)(2,1)S(1)} %constant_dynamic-update-slice_fusion.15, bf16[8,1024,1024]{2,1,0:T(8,128)(2,1)} %param.4), kind=kOutput, calls=%fused_computation.178 | convolution fusion | flops 4294967296 | bytes 22020096 | tf_op jit(solution)/shard_map/mre,mea->ra/dot_general | solution.py:77
  214.7 12.0 %collective-permute-start.46 = (bf16[8,16,1024]{2,1,0:T(8,128)(2,1)S(1)}, bf16[8,16,1024]{2,1,0:T(8,128)(2,1)S(1)}, u32[]{:S(2)}, u32[]{:S(2)}) collective-permute-start(bf16[8,16,1024]{2,1,0:T(8,128)(2,1)S(1)} %constant_dynamic-slice_fusion.21), channel_id=1, source_target_pairs={{0,9},{1,8},{2,11},{3,10},{4,13},{5,12},{6,15},{7,14},{8,1},{9,0},... | collective-permute-start | bytes 786440 | tf_op jit(solution)/shard_map/ppermute | solution.py:67
  228.7 15.9 %collective-permute-done.46 = bf16[8,16,1024]{2,1,0:T(8,128)(2,1)S(1)} collective-permute-done((bf16[8,16,1024]{2,1,0:T(8,128)(2,1)S(1)}, bf16[8,16,1024]{2,1,0:T(8,128)(2,1)S(1)}, u32[]{:S(2)}, u32[]{:S(2)}) %collective-permute-start.46) | collective-permute-done | bytes 262176 | tf_op jit(solution)/shard_map/ppermute | solution.py:67
  247.1 14.6 %collective-permute-done.48 = bf16[8,16,1024]{2,1,0:T(8,128)(2,1)S(1)} collective-permute-done((bf16[8,16,1024]{2,1,0:T(8,128)(2,1)S(1)}, bf16[8,16,1024]{2,1,0:T(8,128)(2,1)S(1)}, u32[]{:S(2)}, u32[]{:S(2)}) %collective-permute-start.48) | collective-permute-done | bytes 262176 | tf_op jit(solution)/shard_map/ppermute | solution.py:67
  263.8 6.5 %collective-permute-done.40 = bf16[8,16,1024]{2,1,0:T(8,128)(2,1)S(1)} collective-permute-done((bf16[8,16,1024]{2,1,0:T(8,128)(2,1)S(1)}, bf16[8,16,1024]{2,1,0:T(8,128)(2,1)S(1)}, u32[]{:S(2)}, u32[]{:S(2)}) %collective-permute-start.40) | collective-permute-done | bytes 262176 | tf_op jit(solution)/shard_map/ppermute | solution.py:67
  270.5 3.1 collective-permute-start.49
  277.4 11.8 %collective-permute-done.37 = f32[16,1024]{1,0:T(8,128)S(1)} collective-permute-done((f32[16,1024]{1,0:T(8,128)S(1)}, f32[16,1024]{1,0:T(8,128)S(1)}, u32[]{:S(2)}, u32[]{:S(2)}) %collective-permute-start.37) | collective-permute-done | bytes 65568 | tf_op jit(solution)/shard_map/ppermute | solution.py:90
  291.2 2.3 collective-permute-start.51
  294.3 3.5 collective-permute-start.64
  298.6 2.2 collective-permute-done.52
  302.2 4.1 collective-permute-done.44
  311.5 4.8 %collective-permute-done.51 = bf16[8,16,1024]{2,1,0:T(8,128)(2,1)S(1)} collective-permute-done((bf16[8,16,1024]{2,1,0:T(8,128)(2,1)S(1)}, bf16[8,16,1024]{2,1,0:T(8,128)(2,1)S(1)}, u32[]{:S(2)}, u32[]{:S(2)}) %collective-permute-start.51) | collective-permute-done | bytes 262176 | tf_op jit(solution)/shard_map/ppermute | solution.py:67
  317.8 9.5 %fusion.20 = f32[256,1024,1]{1,0,2:T(8,128)S(1)} fusion(bf16[8,256,1024]{2,1,0:T(8,128)(2,1)} %constant_dynamic-update-slice_fusion.30, bf16[8,1024,1024]{2,1,0:T(8,128)(2,1)} %param.4), kind=kOutput, calls=%fused_computation.179 | convolution fusion | flops 4294967296 | bytes 22020096 | tf_op jit(solution)/shard_map/mre,mea->ra/dot_general | solution.py:77
  327.5 8.6 %collective-permute-start.65 = (bf16[8,16,1024]{2,1,0:T(8,128)(2,1)S(1)}, bf16[8,16,1024]{2,1,0:T(8,128)(2,1)S(1)}, u32[]{:S(2)}, u32[]{:S(2)}) collective-permute-start(bf16[8,16,1024]{2,1,0:T(8,128)(2,1)S(1)} %constant_dynamic-slice_fusion.6), channel_id=1, source_target_pairs={{0,9},{1,8},{2,11},{3,10},{4,13},{5,12},{6,15},{7,14},{8,1},{9,0},... | collective-permute-start | bytes 786440 | tf_op jit(solution)/shard_map/ppermute | solution.py:67
  336.8 2.4 collective-permute-start.60
  339.2 14.8 %collective-permute-done.65 = bf16[8,16,1024]{2,1,0:T(8,128)(2,1)S(1)} collective-permute-done((bf16[8,16,1024]{2,1,0:T(8,128)(2,1)S(1)}, bf16[8,16,1024]{2,1,0:T(8,128)(2,1)S(1)}, u32[]{:S(2)}, u32[]{:S(2)}) %collective-permute-start.65) | collective-permute-done | bytes 262176 | tf_op jit(solution)/shard_map/ppermute | solution.py:67
  356.3 14.4 %collective-permute-done.67 = bf16[8,16,1024]{2,1,0:T(8,128)(2,1)S(1)} collective-permute-done((bf16[8,16,1024]{2,1,0:T(8,128)(2,1)S(1)}, bf16[8,16,1024]{2,1,0:T(8,128)(2,1)S(1)}, u32[]{:S(2)}, u32[]{:S(2)}) %collective-permute-start.67) | collective-permute-done | bytes 262176 | tf_op jit(solution)/shard_map/ppermute | solution.py:67
  372.6 2.2 collective-permute-start.68
  374.8 1.9 collective-permute-done.59
  376.9 7.8 %collective-permute-done.55 = f32[2,16,1024]{2,1,0:T(8,128)S(1)} collective-permute-done((f32[2,16,1024]{2,1,0:T(8,128)S(1)}, f32[2,16,1024]{2,1,0:T(8,128)S(1)}, u32[]{:S(2)}, u32[]{:S(2)}) %collective-permute-start.55) | collective-permute-done | bytes 131104 | tf_op jit(solution)/shard_map/ppermute | solution.py:84
  385.2 3.3 collective-permute-start.62
  388.5 9.4 %collective-permute-done.56 = f32[16,1024]{1,0:T(8,128)S(1)} collective-permute-done((f32[16,1024]{1,0:T(8,128)S(1)}, f32[16,1024]{1,0:T(8,128)S(1)}, u32[]{:S(2)}, u32[]{:S(2)}) %collective-permute-start.56) | collective-permute-done | bytes 65568 | tf_op jit(solution)/shard_map/ppermute | solution.py:90
  399.5 3.4 collective-permute-start.70
  403.6 11.5 %collective-permute-done.63 = bf16[8,16,1024]{2,1,0:T(8,128)(2,1)S(1)} collective-permute-done((bf16[8,16,1024]{2,1,0:T(8,128)(2,1)S(1)}, bf16[8,16,1024]{2,1,0:T(8,128)(2,1)S(1)}, u32[]{:S(2)}, u32[]{:S(2)}) %collective-permute-start.63) | collective-permute-done | bytes 262176 | tf_op jit(solution)/shard_map/ppermute | solution.py:67
  415.3 10.1 %collective-permute-done.70 = bf16[8,16,1024]{2,1,0:T(8,128)(2,1)S(1)} collective-permute-done((bf16[8,16,1024]{2,1,0:T(8,128)(2,1)S(1)}, bf16[8,16,1024]{2,1,0:T(8,128)(2,1)S(1)}, u32[]{:S(2)}, u32[]{:S(2)}) %collective-permute-start.70) | collective-permute-done | bytes 262176 | tf_op jit(solution)/shard_map/ppermute | solution.py:67
  425.5 8.6 %fusion.21 = f32[256,1024,1]{1,0,2:T(8,128)S(1)} fusion(bf16[8,256,1024]{2,1,0:T(8,128)(2,1)S(1)} %constant_dynamic-update-slice_fusion.45, bf16[8,1024,1024]{2,1,0:T(8,128)(2,1)} %param.4), kind=kOutput, calls=%fused_computation.180 | convolution fusion | flops 4294967296 | bytes 22020096 | tf_op jit(solution)/shard_map/mre,mea->ra/dot_general | solution.py:77
  434.2 1.9 collective-permute-done.72
  436.3 8.3 %collective-permute-done.73 = f32[4,16,1024]{2,1,0:T(8,128)S(1)} collective-permute-done((f32[4,16,1024]{2,1,0:T(8,128)S(1)}, f32[4,16,1024]{2,1,0:T(8,128)S(1)}, u32[]{:S(2)}, u32[]{:S(2)}) %collective-permute-start.73) | collective-permute-done | bytes 262176 | tf_op jit(solution)/shard_map/ppermute | solution.py:84
  444.7 3.9 collective-permute-start.74
  448.6 3.0 collective-permute-done.74
  451.6 2.0 collective-permute-start.75
  453.6 3.2 collective-permute-done.75
  458.1 3.5 all-to-all-start
  462.4 9.3 %all-to-all-done = f32[16,1,4096]{2,1,0:T(1,128)S(1)} async-done(((f32[16,1,4096]{2,1,0:T(1,128)}), f32[16,1,4096]{2,1,0:T(1,128)S(1)}, u32[]{:S(2)}, u32[]{:S(2)}) %all-to-all-start) | async-done | bytes 262176 | tf_op jit(solution)/shard_map/all_to_all | solution.py:104
  (271 shorter events, 74.8 us)
Async XLA Ops:
  4.4 21.3 %collective-permute-start.7 = (bf16[8,16,1024]{2,1,0:T(8,128)(2,1)S(1)}, bf16[8,16,1024]{2,1,0:T(8,128)(2,1)S(1)}, u32[]{:S(2)}, u32[]{:S(2)}) collective-permute-start(bf16[8,16,1024]{2,1,0:T(8,128)(2,1)S(1)} %get-tuple-element.121), channel_id=1, source_target_pairs={{0,8},{1,9},{2,10},{3,11},{4,12},{5,13},{6,14},{7,15},{8,0},{9,1},... | collective-permute-start | bytes 786440 | tf_op jit(solution)/shard_map/ppermute | solution.py:67
  7.0 22.8 %collective-permute-start.8 = (bf16[8,16,1024]{2,1,0:T(8,128)(2,1)S(1)}, bf16[8,16,1024]{2,1,0:T(8,128)(2,1)S(1)}, u32[]{:S(2)}, u32[]{:S(2)}) collective-permute-start(bf16[8,16,1024]{2,1,0:T(8,128)(2,1)S(1)} %get-tuple-element.122), channel_id=1, source_target_pairs={{0,9},{1,8},{2,11},{3,10},{4,13},{5,12},{6,15},{7,14},{8,1},{9,0},... | collective-permute-start | bytes 786440 | tf_op jit(solution)/shard_map/ppermute | solution.py:67
  10.2 22.1 %collective-permute-start.2 = (bf16[8,16,1024]{2,1,0:T(8,128)(2,1)S(1)}, bf16[8,16,1024]{2,1,0:T(8,128)(2,1)S(1)}, u32[]{:S(2)}, u32[]{:S(2)}) collective-permute-start(bf16[8,16,1024]{2,1,0:T(8,128)(2,1)S(1)} %constant_dynamic-slice_fusion.55), channel_id=1, source_target_pairs={{0,3},{1,2},{2,1},{3,0},{4,7},{5,6},{6,5},{7,4},{8,11},{9,10},{10,... | collective-permute-start | bytes 786440 | tf_op jit(solution)/shard_map/ppermute | solution.py:67
  12.3 34.0 %collective-permute-start.3 = (bf16[8,16,1024]{2,1,0:T(8,128)(2,1)S(1)}, bf16[8,16,1024]{2,1,0:T(8,128)(2,1)S(1)}, u32[]{:S(2)}, u32[]{:S(2)}) collective-permute-start(bf16[8,16,1024]{2,1,0:T(8,128)(2,1)S(1)} %constant_dynamic-slice_fusion.54), channel_id=1, source_target_pairs={{0,4},{1,5},{2,6},{3,7},{4,0},{5,1},{6,2},{7,3},{8,12},{9,13},{10,... | collective-permute-start | bytes 786440 | tf_op jit(solution)/shard_map/ppermute | solution.py:67
  26.6 21.8 %collective-permute-start.9 = (bf16[8,16,1024]{2,1,0:T(8,128)(2,1)S(1)}, bf16[8,16,1024]{2,1,0:T(8,128)(2,1)S(1)}, u32[]{:S(2)}, u32[]{:S(2)}) collective-permute-start(bf16[8,16,1024]{2,1,0:T(8,128)(2,1)S(1)} %constant_dynamic-slice_fusion.50), channel_id=1, source_target_pairs={{0,10},{1,11},{2,8},{3,9},{4,14},{5,15},{6,12},{7,13},{8,2},{9,3},... | collective-permute-start | bytes 786440 | tf_op jit(solution)/shard_map/ppermute | solution.py:67
  30.7 21.3 %collective-permute-start.10 = (bf16[8,16,1024]{2,1,0:T(8,128)(2,1)S(1)}, bf16[8,16,1024]{2,1,0:T(8,128)(2,1)S(1)}, u32[]{:S(2)}, u32[]{:S(2)}) collective-permute-start(bf16[8,16,1024]{2,1,0:T(8,128)(2,1)S(1)} %constant_dynamic-slice_fusion.49), channel_id=1, source_target_pairs={{0,11},{1,10},{2,9},{3,8},{4,15},{5,14},{6,13},{7,12},{8,3},{9,2},... | collective-permute-start | bytes 786440 | tf_op jit(solution)/shard_map/ppermute | solution.py:67
  33.3 25.4 %collective-permute-start.4 = (bf16[8,16,1024]{2,1,0:T(8,128)(2,1)S(1)}, bf16[8,16,1024]{2,1,0:T(8,128)(2,1)S(1)}, u32[]{:S(2)}, u32[]{:S(2)}) collective-permute-start(bf16[8,16,1024]{2,1,0:T(8,128)(2,1)S(1)} %constant_dynamic-slice_fusion.53), channel_id=1, source_target_pairs={{0,5},{1,4},{2,7},{3,6},{4,1},{5,0},{6,3},{7,2},{8,13},{9,12},{10,... | collective-permute-start | bytes 786440 | tf_op jit(solution)/shard_map/ppermute | solution.py:67
  47.2 28.2 %collective-permute-start.5 = (bf16[8,16,1024]{2,1,0:T(8,128)(2,1)S(1)}, bf16[8,16,1024]{2,1,0:T(8,128)(2,1)S(1)}, u32[]{:S(2)}, u32[]{:S(2)}) collective-permute-start(bf16[8,16,1024]{2,1,0:T(8,128)(2,1)S(1)} %constant_dynamic-slice_fusion.52), channel_id=1, source_target_pairs={{0,6},{1,7},{2,4},{3,5},{4,2},{5,3},{6,0},{7,1},{8,14},{9,15},{10,... | collective-permute-start | bytes 786440 | tf_op jit(solution)/shard_map/ppermute | solution.py:67
  49.4 18.2 %collective-permute-start.11 = (bf16[8,16,1024]{2,1,0:T(8,128)(2,1)S(1)}, bf16[8,16,1024]{2,1,0:T(8,128)(2,1)S(1)}, u32[]{:S(2)}, u32[]{:S(2)}) collective-permute-start(bf16[8,16,1024]{2,1,0:T(8,128)(2,1)S(1)} %constant_dynamic-slice_fusion.48), channel_id=1, source_target_pairs={{0,12},{1,13},{2,14},{3,15},{4,8},{5,9},{6,10},{7,11},{8,4},{9,5},... | collective-permute-start | bytes 786440 | tf_op jit(solution)/shard_map/ppermute | solution.py:67
  53.0 19.5 %collective-permute-start.12 = (bf16[8,16,1024]{2,1,0:T(8,128)(2,1)S(1)}, bf16[8,16,1024]{2,1,0:T(8,128)(2,1)S(1)}, u32[]{:S(2)}, u32[]{:S(2)}) collective-permute-start(bf16[8,16,1024]{2,1,0:T(8,128)(2,1)S(1)} %constant_dynamic-slice_fusion.47), channel_id=1, source_target_pairs={{0,13},{1,12},{2,15},{3,14},{4,9},{5,8},{6,11},{7,10},{8,5},{9,4},... | collective-permute-start | bytes 786440 | tf_op jit(solution)/shard_map/ppermute | solution.py:67
  59.7 22.5 %collective-permute-start.6 = (bf16[8,16,1024]{2,1,0:T(8,128)(2,1)S(1)}, bf16[8,16,1024]{2,1,0:T(8,128)(2,1)S(1)}, u32[]{:S(2)}, u32[]{:S(2)}) collective-permute-start(bf16[8,16,1024]{2,1,0:T(8,128)(2,1)S(1)} %constant_dynamic-slice_fusion.51), channel_id=1, source_target_pairs={{0,7},{1,6},{2,5},{3,4},{4,3},{5,2},{6,1},{7,0},{8,15},{9,14},{10,... | collective-permute-start | bytes 786440 | tf_op jit(solution)/shard_map/ppermute | solution.py:67
  68.6 18.9 %collective-permute-start.13 = (bf16[8,16,1024]{2,1,0:T(8,128)(2,1)S(1)}, bf16[8,16,1024]{2,1,0:T(8,128)(2,1)S(1)}, u32[]{:S(2)}, u32[]{:S(2)}) collective-permute-start(bf16[8,16,1024]{2,1,0:T(8,128)(2,1)S(1)} %constant_dynamic-slice_fusion.46), channel_id=1, source_target_pairs={{0,14},{1,15},{2,12},{3,13},{4,10},{5,11},{6,8},{7,9},{8,6},{9,7},... | collective-permute-start | bytes 786440 | tf_op jit(solution)/shard_map/ppermute | solution.py:67
  73.5 16.7 %collective-permute-start.14 = (bf16[8,16,1024]{2,1,0:T(8,128)(2,1)S(1)}, bf16[8,16,1024]{2,1,0:T(8,128)(2,1)S(1)}, u32[]{:S(2)}, u32[]{:S(2)}) collective-permute-start(bf16[8,16,1024]{2,1,0:T(8,128)(2,1)S(1)} %constant_dynamic-slice_fusion.45), channel_id=1, source_target_pairs={{0,15},{1,14},{2,13},{3,12},{4,11},{5,10},{6,9},{7,8},{8,7},{9,6},... | collective-permute-start | bytes 786440 | tf_op jit(solution)/shard_map/ppermute | solution.py:67
  76.4 42.7 %collective-permute-start.26 = (bf16[8,16,1024]{2,1,0:T(8,128)(2,1)S(1)}, bf16[8,16,1024]{2,1,0:T(8,128)(2,1)S(1)}, u32[]{:S(2)}, u32[]{:S(2)}) collective-permute-start(bf16[8,16,1024]{2,1,0:T(8,128)(2,1)S(1)} %constant_dynamic-slice_fusion.37), channel_id=1, source_target_pairs={{0,8},{1,9},{2,10},{3,11},{4,12},{5,13},{6,14},{7,15},{8,0},{9,1},... | collective-permute-start | bytes 786440 | tf_op jit(solution)/shard_map/ppermute | solution.py:67
  100.7 37.7 %collective-permute-start.15 = (f32[8,16,1024]{2,1,0:T(8,128)S(1)}, f32[8,16,1024]{2,1,0:T(8,128)S(1)}, u32[]{:S(2)}, u32[]{:S(2)}) collective-permute-start(f32[8,16,1024]{2,1,0:T(8,128)S(1)} %slice_bitcast_fusion.6), channel_id=1, source_target_pairs={{0,1},{1,0},{2,3},{3,2},{4,5},{5,4},{6,7},{7,6},{8,9},{9,8},{10,11... | collective-permute-start | bytes 1572872 | tf_op jit(solution)/shard_map/ppermute | solution.py:84
  101.6 34.0 %collective-permute-start.27 = (bf16[8,16,1024]{2,1,0:T(8,128)(2,1)S(1)}, bf16[8,16,1024]{2,1,0:T(8,128)(2,1)S(1)}, u32[]{:S(2)}, u32[]{:S(2)}) collective-permute-start(bf16[8,16,1024]{2,1,0:T(8,128)(2,1)S(1)} %constant_dynamic-slice_fusion.36), channel_id=1, source_target_pairs={{0,9},{1,8},{2,11},{3,10},{4,13},{5,12},{6,15},{7,14},{8,1},{9,0},... | collective-permute-start | bytes 786440 | tf_op jit(solution)/shard_map/ppermute | solution.py:67
  118.0 17.7 %collective-permute-start.20 = (bf16[8,16,1024]{2,1,0:T(8,128)(2,1)S(1)}, bf16[8,16,1024]{2,1,0:T(8,128)(2,1)S(1)}, u32[]{:S(2)}, u32[]{:S(2)}) collective-permute-start(bf16[8,16,1024]{2,1,0:T(8,128)(2,1)S(1)} %constant_dynamic-slice_fusion.43), channel_id=1, source_target_pairs={{0,2},{1,3},{2,0},{3,1},{4,6},{5,7},{6,4},{7,5},{8,10},{9,11},{10,... | collective-permute-start | bytes 786440 | tf_op jit(solution)/shard_map/ppermute | solution.py:67
  118.9 19.4 %collective-permute-start.19 = (bf16[8,16,1024]{2,1,0:T(8,128)(2,1)S(1)}, bf16[8,16,1024]{2,1,0:T(8,128)(2,1)S(1)}, u32[]{:S(2)}, u32[]{:S(2)}) collective-permute-start(bf16[8,16,1024]{2,1,0:T(8,128)(2,1)S(1)} %constant_dynamic-slice_fusion.44), channel_id=1, source_target_pairs={{0,1},{1,0},{2,3},{3,2},{4,5},{5,4},{6,7},{7,6},{8,9},{9,8},{10,11... | collective-permute-start | bytes 786440 | tf_op jit(solution)/shard_map/ppermute | solution.py:67
  119.1 41.7 %collective-permute-start.28 = (bf16[8,16,1024]{2,1,0:T(8,128)(2,1)S(1)}, bf16[8,16,1024]{2,1,0:T(8,128)(2,1)S(1)}, u32[]{:S(2)}, u32[]{:S(2)}) collective-permute-start(bf16[8,16,1024]{2,1,0:T(8,128)(2,1)S(1)} %constant_dynamic-slice_fusion.35), channel_id=1, source_target_pairs={{0,10},{1,11},{2,8},{3,9},{4,14},{5,15},{6,12},{7,13},{8,2},{9,3},... | collective-permute-start | bytes 786440 | tf_op jit(solution)/shard_map/ppermute | solution.py:67
  135.6 17.2 %collective-permute-start.29 = (bf16[8,16,1024]{2,1,0:T(8,128)(2,1)S(1)}, bf16[8,16,1024]{2,1,0:T(8,128)(2,1)S(1)}, u32[]{:S(2)}, u32[]{:S(2)}) collective-permute-start(bf16[8,16,1024]{2,1,0:T(8,128)(2,1)S(1)} %constant_dynamic-slice_fusion.34), channel_id=1, source_target_pairs={{0,11},{1,10},{2,9},{3,8},{4,15},{5,14},{6,13},{7,12},{8,3},{9,2},... | collective-permute-start | bytes 786440 | tf_op jit(solution)/shard_map/ppermute | solution.py:67
  135.8 25.2 %collective-permute-start.22 = (bf16[8,16,1024]{2,1,0:T(8,128)(2,1)S(1)}, bf16[8,16,1024]{2,1,0:T(8,128)(2,1)S(1)}, u32[]{:S(2)}, u32[]{:S(2)}) collective-permute-start(bf16[8,16,1024]{2,1,0:T(8,128)(2,1)S(1)} %constant_dynamic-slice_fusion.41), channel_id=1, source_target_pairs={{0,4},{1,5},{2,6},{3,7},{4,0},{5,1},{6,2},{7,3},{8,12},{9,13},{10,... | collective-permute-start | bytes 786440 | tf_op jit(solution)/shard_map/ppermute | solution.py:67
  138.5 17.7 %collective-permute-start.16 = (f32[4,16,1024]{2,1,0:T(8,128)S(1)}, f32[4,16,1024]{2,1,0:T(8,128)S(1)}, u32[]{:S(2)}, u32[]{:S(2)}) collective-permute-start(f32[4,16,1024]{2,1,0:T(8,128)S(1)} %slice_bitcast_fusion.14), channel_id=1, source_target_pairs={{0,2},{1,3},{2,0},{3,1},{4,6},{5,7},{6,4},{7,5},{8,10},{9,11},{10,... | collective-permute-start | bytes 786440 | tf_op jit(solution)/shard_map/ppermute | solution.py:84
  139.6 21.1 %collective-permute-start.21 = (bf16[8,16,1024]{2,1,0:T(8,128)(2,1)S(1)}, bf16[8,16,1024]{2,1,0:T(8,128)(2,1)S(1)}, u32[]{:S(2)}, u32[]{:S(2)}) collective-permute-start(bf16[8,16,1024]{2,1,0:T(8,128)(2,1)S(1)} %constant_dynamic-slice_fusion.42), channel_id=1, source_target_pairs={{0,3},{1,2},{2,1},{3,0},{4,7},{5,6},{6,5},{7,4},{8,11},{9,10},{10,... | collective-permute-start | bytes 786440 | tf_op jit(solution)/shard_map/ppermute | solution.py:67
  152.8 26.4 %collective-permute-start.31 = (bf16[8,16,1024]{2,1,0:T(8,128)(2,1)S(1)}, bf16[8,16,1024]{2,1,0:T(8,128)(2,1)S(1)}, u32[]{:S(2)}, u32[]{:S(2)}) collective-permute-start(bf16[8,16,1024]{2,1,0:T(8,128)(2,1)S(1)} %constant_dynamic-slice_fusion.32), channel_id=1, source_target_pairs={{0,13},{1,12},{2,15},{3,14},{4,9},{5,8},{6,11},{7,10},{8,5},{9,4},... | collective-permute-start | bytes 786440 | tf_op jit(solution)/shard_map/ppermute | solution.py:67
  160.7 20.9 %collective-permute-start.23 = (bf16[8,16,1024]{2,1,0:T(8,128)(2,1)S(1)}, bf16[8,16,1024]{2,1,0:T(8,128)(2,1)S(1)}, u32[]{:S(2)}, u32[]{:S(2)}) collective-permute-start(bf16[8,16,1024]{2,1,0:T(8,128)(2,1)S(1)} %constant_dynamic-slice_fusion.40), channel_id=1, source_target_pairs={{0,5},{1,4},{2,7},{3,6},{4,1},{5,0},{6,3},{7,2},{8,13},{9,12},{10,... | collective-permute-start | bytes 786440 | tf_op jit(solution)/shard_map/ppermute | solution.py:67
  160.8 20.8 %collective-permute-start.30 = (bf16[8,16,1024]{2,1,0:T(8,128)(2,1)S(1)}, bf16[8,16,1024]{2,1,0:T(8,128)(2,1)S(1)}, u32[]{:S(2)}, u32[]{:S(2)}) collective-permute-start(bf16[8,16,1024]{2,1,0:T(8,128)(2,1)S(1)} %constant_dynamic-slice_fusion.33), channel_id=1, source_target_pairs={{0,12},{1,13},{2,14},{3,15},{4,8},{5,9},{6,10},{7,11},{8,4},{9,5},... | collective-permute-start | bytes 786440 | tf_op jit(solution)/shard_map/ppermute | solution.py:67
  167.3 17.8 %collective-permute-start.24 = (bf16[8,16,1024]{2,1,0:T(8,128)(2,1)S(1)}, bf16[8,16,1024]{2,1,0:T(8,128)(2,1)S(1)}, u32[]{:S(2)}, u32[]{:S(2)}) collective-permute-start(bf16[8,16,1024]{2,1,0:T(8,128)(2,1)S(1)} %constant_dynamic-slice_fusion.39), channel_id=1, source_target_pairs={{0,6},{1,7},{2,4},{3,5},{4,2},{5,3},{6,0},{7,1},{8,14},{9,15},{10,... | collective-permute-start | bytes 786440 | tf_op jit(solution)/shard_map/ppermute | solution.py:67
  181.6 17.5 %collective-permute-start.25 = (bf16[8,16,1024]{2,1,0:T(8,128)(2,1)S(1)}, bf16[8,16,1024]{2,1,0:T(8,128)(2,1)S(1)}, u32[]{:S(2)}, u32[]{:S(2)}) collective-permute-start(bf16[8,16,1024]{2,1,0:T(8,128)(2,1)S(1)} %constant_dynamic-slice_fusion.38), channel_id=1, source_target_pairs={{0,7},{1,6},{2,5},{3,4},{4,3},{5,2},{6,1},{7,0},{8,15},{9,14},{10,... | collective-permute-start | bytes 786440 | tf_op jit(solution)/shard_map/ppermute | solution.py:67
  181.7 24.3 %collective-permute-start.32 = (bf16[8,16,1024]{2,1,0:T(8,128)(2,1)S(1)}, bf16[8,16,1024]{2,1,0:T(8,128)(2,1)S(1)}, u32[]{:S(2)}, u32[]{:S(2)}) collective-permute-start(bf16[8,16,1024]{2,1,0:T(8,128)(2,1)S(1)} %constant_dynamic-slice_fusion.31), channel_id=1, source_target_pairs={{0,14},{1,15},{2,12},{3,13},{4,10},{5,11},{6,8},{7,9},{8,6},{9,7},... | collective-permute-start | bytes 786440 | tf_op jit(solution)/shard_map/ppermute | solution.py:67
  185.2 41.6 %collective-permute-start.45 = (bf16[8,16,1024]{2,1,0:T(8,128)(2,1)S(1)}, bf16[8,16,1024]{2,1,0:T(8,128)(2,1)S(1)}, u32[]{:S(2)}, u32[]{:S(2)}) collective-permute-start(bf16[8,16,1024]{2,1,0:T(8,128)(2,1)S(1)} %constant_dynamic-slice_fusion.22), channel_id=1, source_target_pairs={{0,8},{1,9},{2,10},{3,11},{4,12},{5,13},{6,14},{7,15},{8,0},{9,1},... | collective-permute-start | bytes 786440 | tf_op jit(solution)/shard_map/ppermute | solution.py:67
  190.9 36.6 %collective-permute-start.39 = (bf16[8,16,1024]{2,1,0:T(8,128)(2,1)S(1)}, bf16[8,16,1024]{2,1,0:T(8,128)(2,1)S(1)}, u32[]{:S(2)}, u32[]{:S(2)}) collective-permute-start(bf16[8,16,1024]{2,1,0:T(8,128)(2,1)S(1)} %constant_dynamic-slice_fusion.28), channel_id=1, source_target_pairs={{0,2},{1,3},{2,0},{3,1},{4,6},{5,7},{6,4},{7,5},{8,10},{9,11},{10,... | collective-permute-start | bytes 786440 | tf_op jit(solution)/shard_map/ppermute | solution.py:67
  214.6 30.9 %collective-permute-start.34 = (f32[8,16,1024]{2,1,0:T(8,128)S(1)}, f32[8,16,1024]{2,1,0:T(8,128)S(1)}, u32[]{:S(2)}, u32[]{:S(2)}) collective-permute-start(f32[8,16,1024]{2,1,0:T(8,128)S(1)} %slice_bitcast_fusion.4), channel_id=1, source_target_pairs={{0,1},{1,0},{2,3},{3,2},{4,5},{5,4},{6,7},{7,6},{8,9},{9,8},{10,11... | collective-permute-start | bytes 1572872 | tf_op jit(solution)/shard_map/ppermute | solution.py:84
  214.7 29.9 %collective-permute-start.46 = (bf16[8,16,1024]{2,1,0:T(8,128)(2,1)S(1)}, bf16[8,16,1024]{2,1,0:T(8,128)(2,1)S(1)}, u32[]{:S(2)}, u32[]{:S(2)}) collective-permute-start(bf16[8,16,1024]{2,1,0:T(8,128)(2,1)S(1)} %constant_dynamic-slice_fusion.21), channel_id=1, source_target_pairs={{0,9},{1,8},{2,11},{3,10},{4,13},{5,12},{6,15},{7,14},{8,1},{9,0},... | collective-permute-start | bytes 786440 | tf_op jit(solution)/shard_map/ppermute | solution.py:67
  226.7 18.0 %collective-permute-start.38 = (bf16[8,16,1024]{2,1,0:T(8,128)(2,1)S(1)}, bf16[8,16,1024]{2,1,0:T(8,128)(2,1)S(1)}, u32[]{:S(2)}, u32[]{:S(2)}) collective-permute-start(bf16[8,16,1024]{2,1,0:T(8,128)(2,1)S(1)} %constant_dynamic-slice_fusion.29), channel_id=1, source_target_pairs={{0,1},{1,0},{2,3},{3,2},{4,5},{5,4},{6,7},{7,6},{8,9},{9,8},{10,11... | collective-permute-start | bytes 786440 | tf_op jit(solution)/shard_map/ppermute | solution.py:67
  226.8 43.6 %collective-permute-start.47 = (bf16[8,16,1024]{2,1,0:T(8,128)(2,1)S(1)}, bf16[8,16,1024]{2,1,0:T(8,128)(2,1)S(1)}, u32[]{:S(2)}, u32[]{:S(2)}) collective-permute-start(bf16[8,16,1024]{2,1,0:T(8,128)(2,1)S(1)} %constant_dynamic-slice_fusion.20), channel_id=1, source_target_pairs={{0,10},{1,11},{2,8},{3,9},{4,14},{5,15},{6,12},{7,13},{8,2},{9,3},... | collective-permute-start | bytes 786440 | tf_op jit(solution)/shard_map/ppermute | solution.py:67
  227.5 46.8 %collective-permute-start.41 = (bf16[8,16,1024]{2,1,0:T(8,128)(2,1)S(1)}, bf16[8,16,1024]{2,1,0:T(8,128)(2,1)S(1)}, u32[]{:S(2)}, u32[]{:S(2)}) collective-permute-start(bf16[8,16,1024]{2,1,0:T(8,128)(2,1)S(1)} %constant_dynamic-slice_fusion.26), channel_id=1, source_target_pairs={{0,4},{1,5},{2,6},{3,7},{4,0},{5,1},{6,2},{7,3},{8,12},{9,13},{10,... | collective-permute-start | bytes 786440 | tf_op jit(solution)/shard_map/ppermute | solution.py:67
  244.6 17.1 %collective-permute-start.48 = (bf16[8,16,1024]{2,1,0:T(8,128)(2,1)S(1)}, bf16[8,16,1024]{2,1,0:T(8,128)(2,1)S(1)}, u32[]{:S(2)}, u32[]{:S(2)}) collective-permute-start(bf16[8,16,1024]{2,1,0:T(8,128)(2,1)S(1)} %constant_dynamic-slice_fusion.19), channel_id=1, source_target_pairs={{0,11},{1,10},{2,9},{3,8},{4,15},{5,14},{6,13},{7,12},{8,3},{9,2},... | collective-permute-start | bytes 786440 | tf_op jit(solution)/shard_map/ppermute | solution.py:67
  245.5 18.2 %collective-permute-start.35 = (f32[4,16,1024]{2,1,0:T(8,128)S(1)}, f32[4,16,1024]{2,1,0:T(8,128)S(1)}, u32[]{:S(2)}, u32[]{:S(2)}) collective-permute-start(f32[4,16,1024]{2,1,0:T(8,128)S(1)} %slice_bitcast_fusion.12), channel_id=1, source_target_pairs={{0,2},{1,3},{2,0},{3,1},{4,6},{5,7},{6,4},{7,5},{8,10},{9,11},{10,... | collective-permute-start | bytes 786440 | tf_op jit(solution)/shard_map/ppermute | solution.py:84
  261.8 27.5 %collective-permute-start.50 = (bf16[8,16,1024]{2,1,0:T(8,128)(2,1)S(1)}, bf16[8,16,1024]{2,1,0:T(8,128)(2,1)S(1)}, u32[]{:S(2)}, u32[]{:S(2)}) collective-permute-start(bf16[8,16,1024]{2,1,0:T(8,128)(2,1)S(1)} %constant_dynamic-slice_fusion.17), channel_id=1, source_target_pairs={{0,13},{1,12},{2,15},{3,14},{4,9},{5,8},{6,11},{7,10},{8,5},{9,4},... | collective-permute-start | bytes 786440 | tf_op jit(solution)/shard_map/ppermute | solution.py:67
  270.3 20.8 %collective-permute-start.42 = (bf16[8,16,1024]{2,1,0:T(8,128)(2,1)S(1)}, bf16[8,16,1024]{2,1,0:T(8,128)(2,1)S(1)}, u32[]{:S(2)}, u32[]{:S(2)}) collective-permute-start(bf16[8,16,1024]{2,1,0:T(8,128)(2,1)S(1)} %constant_dynamic-slice_fusion.25), channel_id=1, source_target_pairs={{0,5},{1,4},{2,7},{3,6},{4,1},{5,0},{6,3},{7,2},{8,13},{9,12},{10,... | collective-permute-start | bytes 786440 | tf_op jit(solution)/shard_map/ppermute | solution.py:67
  270.5 20.7 %collective-permute-start.49 = (bf16[8,16,1024]{2,1,0:T(8,128)(2,1)S(1)}, bf16[8,16,1024]{2,1,0:T(8,128)(2,1)S(1)}, u32[]{:S(2)}, u32[]{:S(2)}) collective-permute-start(bf16[8,16,1024]{2,1,0:T(8,128)(2,1)S(1)} %constant_dynamic-slice_fusion.18), channel_id=1, source_target_pairs={{0,12},{1,13},{2,14},{3,15},{4,8},{5,9},{6,10},{7,11},{8,4},{9,5},... | collective-permute-start | bytes 786440 | tf_op jit(solution)/shard_map/ppermute | solution.py:67
  275.3 14.0 %collective-permute-start.37 = (f32[16,1024]{1,0:T(8,128)S(1)}, f32[16,1024]{1,0:T(8,128)S(1)}, u32[]{:S(2)}, u32[]{:S(2)}) collective-permute-start(f32[16,1024]{1,0:T(8,128)S(1)} %slice_bitcast_fusion.28), channel_id=1, source_target_pairs={{0,8},{1,9},{2,10},{3,11},{4,12},{5,13},{6,14},{7,15},{8,0},{9,1},... | collective-permute-start | bytes 196616 | tf_op jit(solution)/shard_map/ppermute | solution.py:90
  276.1 18.2 %collective-permute-start.43 = (bf16[8,16,1024]{2,1,0:T(8,128)(2,1)S(1)}, bf16[8,16,1024]{2,1,0:T(8,128)(2,1)S(1)}, u32[]{:S(2)}, u32[]{:S(2)}) collective-permute-start(bf16[8,16,1024]{2,1,0:T(8,128)(2,1)S(1)} %constant_dynamic-slice_fusion.24), channel_id=1, source_target_pairs={{0,6},{1,7},{2,4},{3,5},{4,2},{5,3},{6,0},{7,1},{8,14},{9,15},{10,... | collective-permute-start | bytes 786440 | tf_op jit(solution)/shard_map/ppermute | solution.py:67
  291.1 15.1 %collective-permute-start.44 = (bf16[8,16,1024]{2,1,0:T(8,128)(2,1)S(1)}, bf16[8,16,1024]{2,1,0:T(8,128)(2,1)S(1)}, u32[]{:S(2)}, u32[]{:S(2)}) collective-permute-start(bf16[8,16,1024]{2,1,0:T(8,128)(2,1)S(1)} %constant_dynamic-slice_fusion.23), channel_id=1, source_target_pairs={{0,7},{1,6},{2,5},{3,4},{4,3},{5,2},{6,1},{7,0},{8,15},{9,14},{10,... | collective-permute-start | bytes 786440 | tf_op jit(solution)/shard_map/ppermute | solution.py:67
  291.2 25.1 %collective-permute-start.51 = (bf16[8,16,1024]{2,1,0:T(8,128)(2,1)S(1)}, bf16[8,16,1024]{2,1,0:T(8,128)(2,1)S(1)}, u32[]{:S(2)}, u32[]{:S(2)}) collective-permute-start(bf16[8,16,1024]{2,1,0:T(8,128)(2,1)S(1)} %constant_dynamic-slice_fusion.16), channel_id=1, source_target_pairs={{0,14},{1,15},{2,12},{3,13},{4,10},{5,11},{6,8},{7,9},{8,6},{9,7},... | collective-permute-start | bytes 786440 | tf_op jit(solution)/shard_map/ppermute | solution.py:67
  294.3 41.9 %collective-permute-start.64 = (bf16[8,16,1024]{2,1,0:T(8,128)(2,1)S(1)}, bf16[8,16,1024]{2,1,0:T(8,128)(2,1)S(1)}, u32[]{:S(2)}, u32[]{:S(2)}) collective-permute-start(bf16[8,16,1024]{2,1,0:T(8,128)(2,1)S(1)} %constant_dynamic-slice_fusion.7), channel_id=1, source_target_pairs={{0,8},{1,9},{2,10},{3,11},{4,12},{5,13},{6,14},{7,15},{8,0},{9,1},... | collective-permute-start | bytes 786440 | tf_op jit(solution)/shard_map/ppermute | solution.py:67
  300.8 35.9 %collective-permute-start.58 = (bf16[8,16,1024]{2,1,0:T(8,128)(2,1)S(1)}, bf16[8,16,1024]{2,1,0:T(8,128)(2,1)S(1)}, u32[]{:S(2)}, u32[]{:S(2)}) collective-permute-start(bf16[8,16,1024]{2,1,0:T(8,128)(2,1)S(1)} %constant_dynamic-slice_fusion.13), channel_id=1, source_target_pairs={{0,2},{1,3},{2,0},{3,1},{4,6},{5,7},{6,4},{7,5},{8,10},{9,11},{10,... | collective-permute-start | bytes 786440 | tf_op jit(solution)/shard_map/ppermute | solution.py:67
  327.4 26.8 %collective-permute-start.53 = (f32[8,16,1024]{2,1,0:T(8,128)S(1)}, f32[8,16,1024]{2,1,0:T(8,128)S(1)}, u32[]{:S(2)}, u32[]{:S(2)}) collective-permute-start(f32[8,16,1024]{2,1,0:T(8,128)S(1)} %slice_bitcast_fusion.2), channel_id=1, source_target_pairs={{0,1},{1,0},{2,3},{3,2},{4,5},{5,4},{6,7},{7,6},{8,9},{9,8},{10,11... | collective-permute-start | bytes 1572872 | tf_op jit(solution)/shard_map/ppermute | solution.py:84
  327.5 26.5 %collective-permute-start.65 = (bf16[8,16,1024]{2,1,0:T(8,128)(2,1)S(1)}, bf16[8,16,1024]{2,1,0:T(8,128)(2,1)S(1)}, u32[]{:S(2)}, u32[]{:S(2)}) collective-permute-start(bf16[8,16,1024]{2,1,0:T(8,128)(2,1)S(1)} %constant_dynamic-slice_fusion.6), channel_id=1, source_target_pairs={{0,9},{1,8},{2,11},{3,10},{4,13},{5,12},{6,15},{7,14},{8,1},{9,0},... | collective-permute-start | bytes 786440 | tf_op jit(solution)/shard_map/ppermute | solution.py:67
  336.1 18.0 %collective-permute-start.57 = (bf16[8,16,1024]{2,1,0:T(8,128)(2,1)S(1)}, bf16[8,16,1024]{2,1,0:T(8,128)(2,1)S(1)}, u32[]{:S(2)}, u32[]{:S(2)}) collective-permute-start(bf16[8,16,1024]{2,1,0:T(8,128)(2,1)S(1)} %constant_dynamic-slice_fusion.14), channel_id=1, source_target_pairs={{0,1},{1,0},{2,3},{3,2},{4,5},{5,4},{6,7},{7,6},{8,9},{9,8},{10,11... | collective-permute-start | bytes 786440 | tf_op jit(solution)/shard_map/ppermute | solution.py:67
  336.2 36.4 %collective-permute-start.66 = (bf16[8,16,1024]{2,1,0:T(8,128)(2,1)S(1)}, bf16[8,16,1024]{2,1,0:T(8,128)(2,1)S(1)}, u32[]{:S(2)}, u32[]{:S(2)}) collective-permute-start(bf16[8,16,1024]{2,1,0:T(8,128)(2,1)S(1)} %constant_dynamic-slice_fusion.5), channel_id=1, source_target_pairs={{0,10},{1,11},{2,8},{3,9},{4,14},{5,15},{6,12},{7,13},{8,2},{9,3},... | collective-permute-start | bytes 786440 | tf_op jit(solution)/shard_map/ppermute | solution.py:67
  336.8 40.0 %collective-permute-start.60 = (bf16[8,16,1024]{2,1,0:T(8,128)(2,1)S(1)}, bf16[8,16,1024]{2,1,0:T(8,128)(2,1)S(1)}, u32[]{:S(2)}, u32[]{:S(2)}) collective-permute-start(bf16[8,16,1024]{2,1,0:T(8,128)(2,1)S(1)} %constant_dynamic-slice_fusion.11), channel_id=1, source_target_pairs={{0,4},{1,5},{2,6},{3,7},{4,0},{5,1},{6,2},{7,3},{8,12},{9,13},{10,... | collective-permute-start | bytes 786440 | tf_op jit(solution)/shard_map/ppermute | solution.py:67
  354.0 16.6 %collective-permute-start.67 = (bf16[8,16,1024]{2,1,0:T(8,128)(2,1)S(1)}, bf16[8,16,1024]{2,1,0:T(8,128)(2,1)S(1)}, u32[]{:S(2)}, u32[]{:S(2)}) collective-permute-start(bf16[8,16,1024]{2,1,0:T(8,128)(2,1)S(1)} %constant_dynamic-slice_fusion.4), channel_id=1, source_target_pairs={{0,11},{1,10},{2,9},{3,8},{4,15},{5,14},{6,13},{7,12},{8,3},{9,2},... | collective-permute-start | bytes 786440 | tf_op jit(solution)/shard_map/ppermute | solution.py:67
  354.2 18.3 %collective-permute-start.54 = (f32[4,16,1024]{2,1,0:T(8,128)S(1)}, f32[4,16,1024]{2,1,0:T(8,128)S(1)}, u32[]{:S(2)}, u32[]{:S(2)}) collective-permute-start(f32[4,16,1024]{2,1,0:T(8,128)S(1)} %slice_bitcast_fusion.10), channel_id=1, source_target_pairs={{0,2},{1,3},{2,0},{3,1},{4,6},{5,7},{6,4},{7,5},{8,10},{9,11},{10,... | collective-permute-start | bytes 786440 | tf_op jit(solution)/shard_map/ppermute | solution.py:84
  355.0 21.7 %collective-permute-start.59 = (bf16[8,16,1024]{2,1,0:T(8,128)(2,1)S(1)}, bf16[8,16,1024]{2,1,0:T(8,128)(2,1)S(1)}, u32[]{:S(2)}, u32[]{:S(2)}) collective-permute-start(bf16[8,16,1024]{2,1,0:T(8,128)(2,1)S(1)} %constant_dynamic-slice_fusion.12), channel_id=1, source_target_pairs={{0,3},{1,2},{2,1},{3,0},{4,7},{5,6},{6,5},{7,4},{8,11},{9,10},{10,... | collective-permute-start | bytes 786440 | tf_op jit(solution)/shard_map/ppermute | solution.py:67
  370.6 27.3 %collective-permute-start.69 = (bf16[8,16,1024]{2,1,0:T(8,128)(2,1)S(1)}, bf16[8,16,1024]{2,1,0:T(8,128)(2,1)S(1)}, u32[]{:S(2)}, u32[]{:S(2)}) collective-permute-start(bf16[8,16,1024]{2,1,0:T(8,128)(2,1)S(1)} %constant_dynamic-slice_fusion.2), channel_id=1, source_target_pairs={{0,13},{1,12},{2,15},{3,14},{4,9},{5,8},{6,11},{7,10},{8,5},{9,4},... | collective-permute-start | bytes 786440 | tf_op jit(solution)/shard_map/ppermute | solution.py:67
  372.6 26.8 %collective-permute-start.68 = (bf16[8,16,1024]{2,1,0:T(8,128)(2,1)S(1)}, bf16[8,16,1024]{2,1,0:T(8,128)(2,1)S(1)}, u32[]{:S(2)}, u32[]{:S(2)}) collective-permute-start(bf16[8,16,1024]{2,1,0:T(8,128)(2,1)S(1)} %constant_dynamic-slice_fusion.3), channel_id=1, source_target_pairs={{0,12},{1,13},{2,14},{3,15},{4,8},{5,9},{6,10},{7,11},{8,4},{9,5},... | collective-permute-start | bytes 786440 | tf_op jit(solution)/shard_map/ppermute | solution.py:67
  376.7 21.6 %collective-permute-start.61 = (bf16[8,16,1024]{2,1,0:T(8,128)(2,1)S(1)}, bf16[8,16,1024]{2,1,0:T(8,128)(2,1)S(1)}, u32[]{:S(2)}, u32[]{:S(2)}) collective-permute-start(bf16[8,16,1024]{2,1,0:T(8,128)(2,1)S(1)} %constant_dynamic-slice_fusion.10), channel_id=1, source_target_pairs={{0,5},{1,4},{2,7},{3,6},{4,1},{5,0},{6,3},{7,2},{8,13},{9,12},{10,... | collective-permute-start | bytes 786440 | tf_op jit(solution)/shard_map/ppermute | solution.py:67
  384.7 13.2 %collective-permute-start.56 = (f32[16,1024]{1,0:T(8,128)S(1)}, f32[16,1024]{1,0:T(8,128)S(1)}, u32[]{:S(2)}, u32[]{:S(2)}) collective-permute-start(f32[16,1024]{1,0:T(8,128)S(1)} %slice_bitcast_fusion.26), channel_id=1, source_target_pairs={{0,8},{1,9},{2,10},{3,11},{4,12},{5,13},{6,14},{7,15},{8,0},{9,1},... | collective-permute-start | bytes 196616 | tf_op jit(solution)/shard_map/ppermute | solution.py:90
  385.2 18.4 %collective-permute-start.62 = (bf16[8,16,1024]{2,1,0:T(8,128)(2,1)S(1)}, bf16[8,16,1024]{2,1,0:T(8,128)(2,1)S(1)}, u32[]{:S(2)}, u32[]{:S(2)}) collective-permute-start(bf16[8,16,1024]{2,1,0:T(8,128)(2,1)S(1)} %constant_dynamic-slice_fusion.9), channel_id=1, source_target_pairs={{0,6},{1,7},{2,4},{3,5},{4,2},{5,3},{6,0},{7,1},{8,14},{9,15},{10,... | collective-permute-start | bytes 786440 | tf_op jit(solution)/shard_map/ppermute | solution.py:67
  398.0 27.4 %collective-permute-start.71 = (bf16[8,16,1024]{2,1,0:T(8,128)(2,1)S(1)}, bf16[8,16,1024]{2,1,0:T(8,128)(2,1)S(1)}, u32[]{:S(2)}, u32[]{:S(2)}) collective-permute-start(bf16[8,16,1024]{2,1,0:T(8,128)(2,1)S(1)} %constant_dynamic-slice_fusion), channel_id=1, source_target_pairs={{0,15},{1,14},{2,13},{3,12},{4,11},{5,10},{6,9},{7,8},{8,7},{9,6},... | collective-permute-start | bytes 786440 | tf_op jit(solution)/shard_map/ppermute | solution.py:67
  398.3 16.8 %collective-permute-start.63 = (bf16[8,16,1024]{2,1,0:T(8,128)(2,1)S(1)}, bf16[8,16,1024]{2,1,0:T(8,128)(2,1)S(1)}, u32[]{:S(2)}, u32[]{:S(2)}) collective-permute-start(bf16[8,16,1024]{2,1,0:T(8,128)(2,1)S(1)} %constant_dynamic-slice_fusion.8), channel_id=1, source_target_pairs={{0,7},{1,6},{2,5},{3,4},{4,3},{5,2},{6,1},{7,0},{8,15},{9,14},{10,... | collective-permute-start | bytes 786440 | tf_op jit(solution)/shard_map/ppermute | solution.py:67
  399.5 25.9 %collective-permute-start.70 = (bf16[8,16,1024]{2,1,0:T(8,128)(2,1)S(1)}, bf16[8,16,1024]{2,1,0:T(8,128)(2,1)S(1)}, u32[]{:S(2)}, u32[]{:S(2)}) collective-permute-start(bf16[8,16,1024]{2,1,0:T(8,128)(2,1)S(1)} %constant_dynamic-slice_fusion.1), channel_id=1, source_target_pairs={{0,14},{1,15},{2,12},{3,13},{4,10},{5,11},{6,8},{7,9},{8,6},{9,7},... | collective-permute-start | bytes 786440 | tf_op jit(solution)/shard_map/ppermute | solution.py:67
  458.1 13.5 %all-to-all-start = ((f32[16,1,4096]{2,1,0:T(1,128)}), f32[16,1,4096]{2,1,0:T(1,128)S(1)}, u32[]{:S(2)}, u32[]{:S(2)}) async-start(f32[16,1,4096]{2,1,0:T(1,128)} %reshape.71), calls=%async_computation | async-start | bytes 524288 | tf_op jit(solution)/shard_map/all_to_all | solution.py:104
  (20 other events, 264.1 us)

commit v2 on v0

v2 whole, which is shorter than its diff:
```python
import functools
import jax
import jax.numpy as jnp
from jax import lax
from jax.experimental import pallas as pl
from jax.experimental.pallas import tpu as pltpu
from jax.sharding import PartitionSpec as P

AXIS = "vir"
CHUNKS = (24, 16, 16, 8)


def denominator(pair_energy, vir_energy, start, rows):
    mine = lax.dynamic_slice_in_dim(vir_energy, start, rows, 0)
    return pair_energy[None, :, None] - vir_energy[None, None, :] - mine[:, None, None]


def gathered_body(amplitudes, integrals, pair_energy, vir_energy):
    blocks = lax.all_to_all(integrals, AXIS, split_axis=1, concat_axis=2, tiled=True)
    rows = blocks.shape[2] // lax.axis_size(AXIS)
    part = jnp.einsum("lgif,gfh->ilh", blocks, amplitudes, preferred_element_type=jnp.float32)
    cycle = lax.psum_scatter(part, AXIS, scatter_dimension=0, tiled=True)
    swapped = lax.all_to_all(cycle, AXIS, split_axis=2, concat_axis=0, tiled=True)
    paired = cycle + jnp.transpose(swapped, (2, 1, 0))
    return paired / denominator(pair_energy, vir_energy, lax.axis_index(AXIS) * rows, rows)


def after(x, *deps):
    return lax.optimization_barrier((x, *deps))[0] if deps else x


def product_kernel(lhs, amp, out):
    @pl.when(pl.program_id(0) == 0)
    def _():
        out[...] = jnp.zeros_like(out)

    n, _, r, e = lhs.shape
    rows = lhs[:, 0].astype(jnp.float32).reshape(n * r, e).astype(jnp.bfloat16)
    out[...] += jnp.dot(rows, amp[0], preferred_element_type=jnp.float32)


def product(blocks, amplitudes):
    n, own, r, e = blocks.shape
    a = amplitudes.shape[2]
    return pl.pallas_call(
        product_kernel,
        grid=(own,),
        in_specs=[
            pl.BlockSpec((n, 1, r, e), lambda m: (0, m, 0, 0)),
            pl.BlockSpec((1, e, a), lambda m: (m, 0, 0)),
        ],
        out_specs=pl.BlockSpec((n * r, a), lambda m: (0, 0)),
        out_shape=jax.ShapeDtypeStruct((n * r, a), jnp.float32),
        compiler_params=pltpu.CompilerParams(vmem_limit_bytes=40 * 1024 * 1024),
        cost_estimate=pl.CostEstimate(
            flops=2 * n * r * own * e * a,
            bytes_accessed=2 * own * e * (a + n * r) + 4 * n * r * a,
            transcendentals=0,
        ),
    )(blocks, amplitudes)


def exchanged_body(amplitudes, integrals, pair_energy, vir_energy):
    n = lax.axis_size(AXIS)
    me = lax.axis_index(AXIS)
    own, e, a = amplitudes.shape
    rows = integrals.shape[2]
    source = integrals.reshape(n, own, rows, e)
    width = a // n
    starts = [sum(CHUNKS[:q]) for q in range(len(CHUNKS))]

    def exchange(x):
        return lax.all_to_all(x, AXIS, split_axis=0, concat_axis=0, tiled=True)

    def reduced(part, r):
        blocks = part.reshape(n, r, a)
        bit = 1
        while bit < n:
            odd = (me & bit) != 0
            pair = blocks.reshape(-1, 2, r, a)
            mine = jnp.where(odd, pair[:, 1], pair[:, 0])
            other = jnp.where(odd, pair[:, 0], pair[:, 1])
            blocks = mine + lax.ppermute(other, AXIS, [(i, i ^ bit) for i in range(n)])
            bit *= 2
        return blocks[0]

    received, done = [], []
    for q, r in enumerate(CHUNKS):
        x = source
        if q >= 2:
            x = after(x, received[q - 2])
        x = x[:, :, starts[q] : starts[q] + r]
        if q >= 1:
            x = after(x, received[q - 1], *done[q - 2 : q - 1] if q >= 2 else ())
        received.append(exchange(x))
        if q >= 1:
            part = product(received[q - 1], amplitudes)
            done.append(reduced(part, CHUNKS[q - 1]))
    early = jnp.concatenate(done, axis=0)
    er = early.shape[0]
    early_swap = exchange(after(early.reshape(er, n, width).transpose(1, 0, 2), received[-1]))
    late = CHUNKS[-1]
    part = product(received[-1], amplitudes)
    row_part = part.reshape(n, late, a)
    col_part = part.reshape(n * late, n, width).transpose(1, 0, 2)
    got = exchange(after(jnp.concatenate([row_part, col_part.reshape(n, late, a)], axis=1), early_swap))
    got = got.sum(0)
    late_rows = got[:late]
    late_swap = got[late:].reshape(n, late, width)
    cycle = jnp.concatenate([early, late_rows], axis=0)
    swapped = jnp.concatenate([early_swap, late_swap], axis=1).reshape(n * rows, width)
    paired = cycle + swapped.T
    return paired[:, None, :] / denominator(pair_energy, vir_energy, me * rows, rows)


def solution(mesh):
    n = mesh.shape[AXIS]
    body = exchanged_body if n <= 16 else gathered_body
    in_specs = (P(("grp", AXIS), None, None), P("grp", None, AXIS, None), P("grp"), P("grp"))
    out_specs = P(("grp", AXIS), None, None)
    return jax.shard_map(body, mesh=mesh, in_specs=in_specs, out_specs=out_specs, check_vma=False)
```

time: 556 us -> 462 us (0.83)
  blocking collectives: 369 us -> 0 us
  waiting for transfers between devices: 121 us -> 308 us
  starting transfers between devices: 3.63 us -> 78 us
  Pallas kernels: 0 us -> 45 us
  matrix products: 22.3 us -> 0 us
  between operations: 14.8 us -> 1.03 us
  local copies, waits for them, and re-layouts: 18 us -> 23.7 us
    all_to_all x1 -> x0, blocking collectives: 369 us -> none  [body(): lax.all_to_all(integrals, 'vir', split_axis=1, concat_axis=2, tiled=True)]
    ppermute x0 -> x12, waiting for transfers between devices: none -> 177 us  [reduced(): blocks = mine + lax.ppermute(other, AXIS, [(i, i ^ bit) for i in range(n)])]
    all_to_all x1 -> x6, waiting for transfers between devices: 9.31 us -> 131 us  [exchange(): return lax.all_to_all(x, AXIS, split_axis=0, concat_axis=0, tiled=True)]
    unnamed x2 -> x0, waiting for transfers between devices: 112 us -> none
    all_to_all x1 -> x6, starting transfers between devices: 3.62 us -> 53.5 us  [exchange(): return lax.all_to_all(x, AXIS, split_axis=0, concat_axis=0, tiled=True)]
    pallas_call x0 -> x4, Pallas kernels: none -> 45 us  [product(): pl.pallas_call(product_kernel, grid=(own,), in_specs=[pl.BlockSpec((n, 1,...]
    ppermute x0 -> x12, starting transfers between devices: none -> 24.5 us  [reduced(): blocks = mine + lax.ppermute(other, AXIS, [(i, i ^ bit) for i in range(n)])]
    dot_general x1 -> x0, matrix products: 22.3 us -> none  [body(): jnp.einsum('lgif,gfh->ilh', local_row_block, amplitudes, preferred_elemen...]
  transfers between devices with their start and end apart: 2 -> 18, of which waited for: 2 -> 14; matrix products, arithmetic and copies ran while one was open for 0% -> 4% of each run, Pallas kernels for 0% -> 10%
where the time goes in v2:
time: 462 us; the launch traced here: 460 us
  waiting for transfers between devices  308 us (67%)
  starting transfers between devices  78 us (17%)
  Pallas kernels  45 us (10%)
  local copies, waits for them, and re-layouts  23.7 us (5%)
    ppermute x12, waiting for transfers between devices, reduced(): blocks = mine + lax.ppermute(other, AXIS, [(i, i ^ bit) for i in range(n)])  177 us
    all_to_all x6, waiting for transfers between devices, exchange(): return lax.all_to_all(x, AXIS, split_axis=0, concat_axis=0, tiled=True)  131 us
    all_to_all x6, starting transfers between devices, exchange(): return lax.all_to_all(x, AXIS, split_axis=0, concat_axis=0, tiled=True)  53.5 us
    pallas_call x4, Pallas kernels, product(): pl.pallas_call(product_kernel, grid=(own,), in_specs=[pl.BlockSpec((n, 1,...  45 us
    ppermute x12, starting transfers between devices, reduced(): blocks = mine + lax.ppermute(other, AXIS, [(i, i ^ bit) for i in range(n)])  24.5 us
    slice x4, local copies, waits for them, and re-layouts, exchanged_body(): x = x[:, :, starts[q]:starts[q] + r]  19.6 us
  transfers between devices with their start and end apart: 18, of which 14 were waited for; matrix products, arithmetic and copies ran while one was open for 4% of the time, Pallas kernels for 10%

profile of v2, /device:TPU:0, one launch (start us, length us, event | category | flops | bytes accessed | tf_op | source)
XLA Modules:
  0.0 459.8 jit_solution(644109223389584549)
XLA Ops:
  0.0 6.4 %slice.144 = bf16[16,8,24,1024]{3,2,1,0:T(8,128)(2,1)} slice(bf16[16,8,64,1024]{3,2,1,0:T(8,128)(2,1)} %bitcast.209), slice={[0:16], [0:8], [0:24], [0:1024]} | slice | bytes 12582912 | tf_op jit(solution)/shard_map/slice | solution.py:92
  6.4 7.4 %all-to-all-start = ((bf16[16,8,24,1024]{3,2,1,0:T(8,128)(2,1)}), bf16[16,8,24,1024]{3,2,1,0:T(8,128)(2,1)}, u32[]{:S(2)}, u32[]{:S(2)}) async-start(bf16[16,8,24,1024]{3,2,1,0:T(8,128)(2,1)} %slice.144), calls=%async_computation | async-start | bytes 12582912 | tf_op jit(solution)/shard_map/all_to_all | solution.py:73
  13.9 5.0 %slice.153 = bf16[16,8,16,1024]{3,2,1,0:T(8,128)(2,1)} slice(bf16[16,8,64,1024]{3,2,1,0:T(8,128)(2,1)} %bitcast.210), slice={[0:16], [0:8], [24:40], [0:1024]} | slice | bytes 8388608 | tf_op jit(solution)/shard_map/slice | solution.py:92
  18.8 109.2 %all-to-all-done.lhs = bf16[16,8,24,1024]{3,2,1,0:T(8,128)(2,1)} async-done(((bf16[16,8,24,1024]{3,2,1,0:T(8,128)(2,1)}), bf16[16,8,24,1024]{3,2,1,0:T(8,128)(2,1)}, u32[]{:S(2)}, u32[]{:S(2)}) %all-to-all-start) | async-done | bytes 6291488 | tf_op jit(solution)/shard_map/all_to_all | solution.py:73
  128.1 28.1 %all-to-all-start.1 = ((bf16[16,8,16,1024]{3,2,1,0:T(8,128)(2,1)}), bf16[16,8,16,1024]{3,2,1,0:T(8,128)(2,1)}, u32[]{:S(2)}, u32[]{:S(2)}) async-start(bf16[16,8,16,1024]{3,2,1,0:T(8,128)(2,1)} %slice.153), calls=%async_computation.1 | async-start | bytes 8388608 | tf_op jit(solution)/shard_map/all_to_all | solution.py:73
  156.2 12.9 %shard_map.46 = f32[384,1024]{1,0:T(8,128)S(1)} custom-call(bf16[16,8,24,1024]{3,2,1,0:T(8,128)(2,1)} %all-to-all-done.lhs, bf16[8,1024,1024]{2,1,0:T(8,128)(2,1)} %amp.7), custom_call_target="tpu_custom_call" | custom-call | flops 6442450944 | bytes 24641536 | tf_op jit(solution)/shard_map/pallas_call | solution.py:45
  169.1 0.1 select_bitcast_fusion
  169.2 0.4 collective-permute-start
  169.7 1.9 collective-permute-done
  171.6 0.2 bitcast_add_fusion
  171.9 1.9 collective-permute-start.1
  173.8 24.0 %collective-permute-done.1 = f32[4,24,1024]{2,1,0:T(8,128)S(1)} collective-permute-done((f32[4,24,1024]{2,1,0:T(8,128)S(1)}, f32[4,24,1024]{2,1,0:T(8,128)S(1)}, u32[]{:S(2)}, u32[]{:S(2)}) %collective-permute-start.1) | collective-permute-done | bytes 393248 | tf_op jit(solution)/shard_map/ppermute | solution.py:83
  197.7 0.1 fusion.1
  197.8 0.1 collective-permute-start.2
  197.9 31.1 %collective-permute-done.2 = f32[2,24,1024]{2,1,0:T(8,128)S(1)} collective-permute-done((f32[2,24,1024]{2,1,0:T(8,128)S(1)}, f32[2,24,1024]{2,1,0:T(8,128)S(1)}, u32[]{:S(2)}, u32[]{:S(2)}) %collective-permute-start.2) | collective-permute-done | bytes 196640 | tf_op jit(solution)/shard_map/ppermute | solution.py:83
  229.1 4.6 collective-permute-start.3
  233.7 5.0 %slice.132 = bf16[16,8,16,1024]{3,2,1,0:T(8,128)(2,1)} slice(bf16[16,8,64,1024]{3,2,1,0:T(8,128)(2,1)} %bitcast.211), slice={[0:16], [0:8], [40:56], [0:1024]} | slice | bytes 8388608 | tf_op jit(solution)/shard_map/slice | solution.py:92
  238.7 15.8 %collective-permute-done.3 = f32[1,24,1024]{2,1,0:T(8,128)S(1)} collective-permute-done((f32[1,24,1024]{2,1,0:T(8,128)S(1)}, f32[1,24,1024]{2,1,0:T(8,128)S(1)}, u32[]{:S(2)}, u32[]{:S(2)}) %collective-permute-start.3) | collective-permute-done | bytes 98336 | tf_op jit(solution)/shard_map/ppermute | solution.py:83
  254.5 4.6 all-to-all-start.2
  259.0 11.3 %shard_map.47 = f32[256,1024]{1,0:T(8,128)S(1)} custom-call(bf16[16,8,16,1024]{3,2,1,0:T(8,128)(2,1)} %all-to-all-done.1.lhs, bf16[8,1024,1024]{2,1,0:T(8,128)(2,1)} %amp.7), custom_call_target="tpu_custom_call" | custom-call | flops 4294967296 | bytes 22020096 | tf_op jit(solution)/shard_map/pallas_call | solution.py:45
  270.4 0.1 select_bitcast_fusion.2
  270.4 0.3 collective-permute-start.4
  270.7 1.7 collective-permute-done.4
  272.4 0.1 bitcast_add_fusion.2
  272.6 1.8 collective-permute-start.5
  274.4 16.7 %collective-permute-done.5 = f32[4,16,1024]{2,1,0:T(8,128)S(1)} collective-permute-done((f32[4,16,1024]{2,1,0:T(8,128)S(1)}, f32[4,16,1024]{2,1,0:T(8,128)S(1)}, u32[]{:S(2)}, u32[]{:S(2)}) %collective-permute-start.5) | collective-permute-done | bytes 262176 | tf_op jit(solution)/shard_map/ppermute | solution.py:83
  291.2 0.1 collective-permute-start.6
  291.3 39.0 %collective-permute-done.6 = f32[2,16,1024]{2,1,0:T(8,128)S(1)} collective-permute-done((f32[2,16,1024]{2,1,0:T(8,128)S(1)}, f32[2,16,1024]{2,1,0:T(8,128)S(1)}, u32[]{:S(2)}, u32[]{:S(2)}) %collective-permute-start.6) | collective-permute-done | bytes 131104 | tf_op jit(solution)/shard_map/ppermute | solution.py:83
  330.4 4.6 %collective-permute-start.7 = (f32[1,16,1024]{2,1,0:T(8,128)S(1)}, f32[1,16,1024]{2,1,0:T(8,128)S(1)}, u32[]{:S(2)}, u32[]{:S(2)}) collective-permute-start(f32[1,16,1024]{2,1,0:T(8,128)S(1)} %select_bitcast_fusion.11), channel_id=1, source_target_pairs={{0,8},{1,9},{2,10},{3,11},{4,12},{5,13},{6,14},{7,15},{8,0},{9,1},... | collective-permute-start | bytes 196616 | tf_op jit(solution)/shard_map/ppermute | solution.py:83
  335.0 3.2 slice.141
  338.2 17.6 %collective-permute-done.7 = f32[1,16,1024]{2,1,0:T(8,128)S(1)} collective-permute-done((f32[1,16,1024]{2,1,0:T(8,128)S(1)}, f32[1,16,1024]{2,1,0:T(8,128)S(1)}, u32[]{:S(2)}, u32[]{:S(2)}) %collective-permute-start.7) | collective-permute-done | bytes 65568 | tf_op jit(solution)/shard_map/ppermute | solution.py:83
  355.8 3.7 all-to-all-start.3
  359.5 11.3 %shard_map.48 = f32[256,1024]{1,0:T(8,128)S(1)} custom-call(bf16[16,8,16,1024]{3,2,1,0:T(8,128)(2,1)} %all-to-all-done.2.lhs, bf16[8,1024,1024]{2,1,0:T(8,128)(2,1)} %amp.7), custom_call_target="tpu_custom_call" | custom-call | flops 4294967296 | bytes 22020096 | tf_op jit(solution)/shard_map/pallas_call | solution.py:45
  370.9 0.1 select_bitcast_fusion.1
  370.9 0.4 collective-permute-start.8
  371.3 1.6 collective-permute-done.8
  372.9 0.1 bitcast_add_fusion.1
  373.0 1.9 collective-permute-start.9
  374.9 11.2 %collective-permute-done.9 = f32[4,16,1024]{2,1,0:T(8,128)S(1)} collective-permute-done((f32[4,16,1024]{2,1,0:T(8,128)S(1)}, f32[4,16,1024]{2,1,0:T(8,128)S(1)}, u32[]{:S(2)}, u32[]{:S(2)}) %collective-permute-start.9) | collective-permute-done | bytes 262176 | tf_op jit(solution)/shard_map/ppermute | solution.py:83
  386.2 3.9 collective-permute-start.10
  390.1 7.1 %collective-permute-done.10 = f32[2,16,1024]{2,1,0:T(8,128)S(1)} collective-permute-done((f32[2,16,1024]{2,1,0:T(8,128)S(1)}, f32[2,16,1024]{2,1,0:T(8,128)S(1)}, u32[]{:S(2)}, u32[]{:S(2)}) %collective-permute-start.10) | collective-permute-done | bytes 131104 | tf_op jit(solution)/shard_map/ppermute | solution.py:83
  397.3 4.5 collective-permute-start.11
  401.8 0.1 concatenate.21
  401.9 0.1 copy.107
  401.9 0.1 concatenate.22
  402.1 9.2 %collective-permute-done.11 = f32[1,16,1024]{2,1,0:T(8,128)S(1)} collective-permute-done((f32[1,16,1024]{2,1,0:T(8,128)S(1)}, f32[1,16,1024]{2,1,0:T(8,128)S(1)}, u32[]{:S(2)}, u32[]{:S(2)}) %collective-permute-start.11) | collective-permute-done | bytes 65568 | tf_op jit(solution)/shard_map/ppermute | solution.py:83
  411.3 0.1 concatenate.23
  411.5 1.0 reshape.247
  412.5 3.7 all-to-all-start.4
  416.2 9.4 %shard_map.49 = f32[128,1024]{1,0:T(8,128)S(1)} custom-call(bf16[16,8,8,1024]{3,2,1,0:T(8,128)(2,1)S(1)} %all-to-all-done.3.lhs, bf16[8,1024,1024]{2,1,0:T(8,128)(2,1)} %amp.7), custom_call_target="tpu_custom_call" | custom-call | flops 2147483648 | bytes 19398656 | tf_op jit(solution)/shard_map/pallas_call | solution.py:45
  425.6 0.2 copy.105
  425.8 0.3 copy.106
  426.2 0.3 reshape.244
  426.5 1.1 pad_maximum_fusion
  427.5 0.5 broadcast.88
  428.1 1.2 reduce
  429.2 0.1 reshape.248
  429.4 6.0 %all-to-all-start.5 = ((f32[16,16,1024]{2,1,0:T(8,128)}), f32[16,16,1024]{2,1,0:T(8,128)S(1)}, u32[]{:S(2)}, u32[]{:S(2)}) async-start(f32[16,16,1024]{2,1,0:T(8,128)} %pad_maximum_fusion), calls=%async_computation.5 | async-start | bytes 2097152 | tf_op jit(solution)/shard_map/all_to_all | solution.py:73
  436.1 0.1 dynamic_slice.3
  436.1 22.2 %all-to-all-done.5 = f32[16,16,1024]{2,1,0:T(8,128)S(1)} async-done(((f32[16,16,1024]{2,1,0:T(8,128)}), f32[16,16,1024]{2,1,0:T(8,128)S(1)}, u32[]{:S(2)}, u32[]{:S(2)}) %all-to-all-start.5) | async-done | bytes 1048608 | tf_op jit(solution)/shard_map/all_to_all | solution.py:73
  458.4 0.1 reshape.245
  458.5 0.2 copy.112
  458.7 0.1 fusion.3
  458.9 1.0 copy.111
  (30 shorter events, 0.7 us)
Async XLA Ops:
  6.4 121.6 %all-to-all-start = ((bf16[16,8,24,1024]{3,2,1,0:T(8,128)(2,1)}), bf16[16,8,24,1024]{3,2,1,0:T(8,128)(2,1)}, u32[]{:S(2)}, u32[]{:S(2)}) async-start(bf16[16,8,24,1024]{3,2,1,0:T(8,128)(2,1)} %slice.144), calls=%async_computation | async-start | bytes 12582912 | tf_op jit(solution)/shard_map/all_to_all | solution.py:73
  128.1 126.4 %all-to-all-start.1 = ((bf16[16,8,16,1024]{3,2,1,0:T(8,128)(2,1)}), bf16[16,8,16,1024]{3,2,1,0:T(8,128)(2,1)}, u32[]{:S(2)}, u32[]{:S(2)}) async-start(bf16[16,8,16,1024]{3,2,1,0:T(8,128)(2,1)} %slice.153), calls=%async_computation.1 | async-start | bytes 8388608 | tf_op jit(solution)/shard_map/all_to_all | solution.py:73
  169.2 2.4 collective-permute-start
  171.9 25.9 %collective-permute-start.1 = (f32[4,24,1024]{2,1,0:T(8,128)S(1)}, f32[4,24,1024]{2,1,0:T(8,128)S(1)}, u32[]{:S(2)}, u32[]{:S(2)}) collective-permute-start(f32[4,24,1024]{2,1,0:T(8,128)S(1)} %select_bitcast_fusion.3), channel_id=1, source_target_pairs={{0,2},{1,3},{2,0},{3,1},{4,6},{5,7},{6,4},{7,5},{8,10},{9,11},{10,... | collective-permute-start | bytes 1179656 | tf_op jit(solution)/shard_map/ppermute | solution.py:83
  197.8 31.2 %collective-permute-start.2 = (f32[2,24,1024]{2,1,0:T(8,128)S(1)}, f32[2,24,1024]{2,1,0:T(8,128)S(1)}, u32[]{:S(2)}, u32[]{:S(2)}) collective-permute-start(f32[2,24,1024]{2,1,0:T(8,128)S(1)} %select_bitcast_fusion.6), channel_id=1, source_target_pairs={{0,4},{1,5},{2,6},{3,7},{4,0},{5,1},{6,2},{7,3},{8,12},{9,13},{10,... | collective-permute-start | bytes 589832 | tf_op jit(solution)/shard_map/ppermute | solution.py:83
  229.1 25.4 %collective-permute-start.3 = (f32[1,24,1024]{2,1,0:T(8,128)S(1)}, f32[1,24,1024]{2,1,0:T(8,128)S(1)}, u32[]{:S(2)}, u32[]{:S(2)}) collective-permute-start(f32[1,24,1024]{2,1,0:T(8,128)S(1)} %select_bitcast_fusion.9), channel_id=1, source_target_pairs={{0,8},{1,9},{2,10},{3,11},{4,12},{5,13},{6,14},{7,15},{8,0},{9,1},... | collective-permute-start | bytes 294920 | tf_op jit(solution)/shard_map/ppermute | solution.py:83
  254.5 101.3 %all-to-all-start.2 = ((bf16[16,8,16,1024]{3,2,1,0:T(8,128)(2,1)}), bf16[16,8,16,1024]{3,2,1,0:T(8,128)(2,1)}, u32[]{:S(2)}, u32[]{:S(2)}) async-start(bf16[16,8,16,1024]{3,2,1,0:T(8,128)(2,1)} %slice.132), calls=%async_computation.2 | async-start | bytes 8388608 | tf_op jit(solution)/shard_map/all_to_all | solution.py:73
  270.4 2.0 collective-permute-start.4
  272.6 18.6 %collective-permute-start.5 = (f32[4,16,1024]{2,1,0:T(8,128)S(1)}, f32[4,16,1024]{2,1,0:T(8,128)S(1)}, u32[]{:S(2)}, u32[]{:S(2)}) collective-permute-start(f32[4,16,1024]{2,1,0:T(8,128)S(1)} %select_bitcast_fusion.5), channel_id=1, source_target_pairs={{0,2},{1,3},{2,0},{3,1},{4,6},{5,7},{6,4},{7,5},{8,10},{9,11},{10,... | collective-permute-start | bytes 786440 | tf_op jit(solution)/shard_map/ppermute | solution.py:83
  291.2 39.1 %collective-permute-start.6 = (f32[2,16,1024]{2,1,0:T(8,128)S(1)}, f32[2,16,1024]{2,1,0:T(8,128)S(1)}, u32[]{:S(2)}, u32[]{:S(2)}) collective-permute-start(f32[2,16,1024]{2,1,0:T(8,128)S(1)} %select_bitcast_fusion.8), channel_id=1, source_target_pairs={{0,4},{1,5},{2,6},{3,7},{4,0},{5,1},{6,2},{7,3},{8,12},{9,13},{10,... | collective-permute-start | bytes 393224 | tf_op jit(solution)/shard_map/ppermute | solution.py:83
  330.4 25.4 %collective-permute-start.7 = (f32[1,16,1024]{2,1,0:T(8,128)S(1)}, f32[1,16,1024]{2,1,0:T(8,128)S(1)}, u32[]{:S(2)}, u32[]{:S(2)}) collective-permute-start(f32[1,16,1024]{2,1,0:T(8,128)S(1)} %select_bitcast_fusion.11), channel_id=1, source_target_pairs={{0,8},{1,9},{2,10},{3,11},{4,12},{5,13},{6,14},{7,15},{8,0},{9,1},... | collective-permute-start | bytes 196616 | tf_op jit(solution)/shard_map/ppermute | solution.py:83
  355.8 55.7 %all-to-all-start.3 = ((bf16[16,8,8,1024]{3,2,1,0:T(8,128)(2,1)}), bf16[16,8,8,1024]{3,2,1,0:T(8,128)(2,1)S(1)}, u32[]{:S(2)}, u32[]{:S(2)}) async-start(bf16[16,8,8,1024]{3,2,1,0:T(8,128)(2,1)} %slice.141), calls=%async_computation.3 | async-start | bytes 4194304 | tf_op jit(solution)/shard_map/all_to_all | solution.py:73
  370.9 2.0 collective-permute-start.8
  373.0 13.1 %collective-permute-start.9 = (f32[4,16,1024]{2,1,0:T(8,128)S(1)}, f32[4,16,1024]{2,1,0:T(8,128)S(1)}, u32[]{:S(2)}, u32[]{:S(2)}) collective-permute-start(f32[4,16,1024]{2,1,0:T(8,128)S(1)} %select_bitcast_fusion.4), channel_id=1, source_target_pairs={{0,2},{1,3},{2,0},{3,1},{4,6},{5,7},{6,4},{7,5},{8,10},{9,11},{10,... | collective-permute-start | bytes 786440 | tf_op jit(solution)/shard_map/ppermute | solution.py:83
  386.2 11.0 %collective-permute-start.10 = (f32[2,16,1024]{2,1,0:T(8,128)S(1)}, f32[2,16,1024]{2,1,0:T(8,128)S(1)}, u32[]{:S(2)}, u32[]{:S(2)}) collective-permute-start(f32[2,16,1024]{2,1,0:T(8,128)S(1)} %select_bitcast_fusion.7), channel_id=1, source_target_pairs={{0,4},{1,5},{2,6},{3,7},{4,0},{5,1},{6,2},{7,3},{8,12},{9,13},{10,... | collective-permute-start | bytes 393224 | tf_op jit(solution)/shard_map/ppermute | solution.py:83
  397.3 14.0 %collective-permute-start.11 = (f32[1,16,1024]{2,1,0:T(8,128)S(1)}, f32[1,16,1024]{2,1,0:T(8,128)S(1)}, u32[]{:S(2)}, u32[]{:S(2)}) collective-permute-start(f32[1,16,1024]{2,1,0:T(8,128)S(1)} %select_bitcast_fusion.10), channel_id=1, source_target_pairs={{0,8},{1,9},{2,10},{3,11},{4,12},{5,13},{6,14},{7,15},{8,0},{9,1},... | collective-permute-start | bytes 196616 | tf_op jit(solution)/shard_map/ppermute | solution.py:83
  412.5 15.1 %all-to-all-start.4 = ((f32[16,1,3584]{2,1,0:T(1,128)}), f32[16,1,3584]{2,1,0:T(1,128)S(1)}, u32[]{:S(2)}, u32[]{:S(2)}) async-start(f32[16,1,3584]{2,1,0:T(1,128)} %reshape.247), calls=%async_computation.4 | async-start | bytes 458752 | tf_op jit(solution)/shard_map/all_to_all | solution.py:73
  425.8 10.2 %copy-start = (f32[1024]{0:T(1024)S(1)}, f32[1024]{0:T(1024)}, u32[]{:S(2)}) copy-start(f32[1024]{0:T(1024)} %param.7) | copy-start | bytes 12292
  429.4 29.0 %all-to-all-start.5 = ((f32[16,16,1024]{2,1,0:T(8,128)}), f32[16,16,1024]{2,1,0:T(8,128)S(1)}, u32[]{:S(2)}, u32[]{:S(2)}) async-start(f32[16,16,1024]{2,1,0:T(8,128)} %pad_maximum_fusion), calls=%async_computation.5 | async-start | bytes 2097152 | tf_op jit(solution)/shard_map/all_to_all | solution.py:73

commit v3 on v2

v3 whole, which is shorter than its diff:
```python
import functools
import jax
import jax.numpy as jnp
from jax import lax
from jax.experimental import pallas as pl
from jax.experimental.pallas import tpu as pltpu
from jax.sharding import PartitionSpec as P

AXIS = "vir"
CHUNKS = (8, 32, 16, 8)
STEPS = (2, 1)


def denominator(pair_energy, vir_energy, start, rows):
    mine = lax.dynamic_slice_in_dim(vir_energy, start, rows, 0)
    return pair_energy[None, :, None] - vir_energy[None, None, :] - mine[:, None, None]


def gathered_body(amplitudes, integrals, pair_energy, vir_energy):
    blocks = lax.all_to_all(integrals, AXIS, split_axis=1, concat_axis=2, tiled=True)
    rows = blocks.shape[2] // lax.axis_size(AXIS)
    part = jnp.einsum("lgif,gfh->ilh", blocks, amplitudes, preferred_element_type=jnp.float32)
    cycle = lax.psum_scatter(part, AXIS, scatter_dimension=0, tiled=True)
    swapped = lax.all_to_all(cycle, AXIS, split_axis=2, concat_axis=0, tiled=True)
    paired = cycle + jnp.transpose(swapped, (2, 1, 0))
    return paired / denominator(pair_energy, vir_energy, lax.axis_index(AXIS) * rows, rows)


def after(x, *deps):
    return lax.optimization_barrier((x, *deps))[0] if deps else x


def product_kernel(blocks, amp, out):
    n, owned, r, e = blocks.shape

    def rows_of(m):
        rows = blocks[:, m]
        if r % 16:
            rows = rows.astype(jnp.float32).reshape(n * r, e).astype(jnp.bfloat16)
        return rows.reshape(n * r, e)

    lhs = jnp.concatenate([rows_of(m) for m in range(owned)], axis=1)
    part = jnp.dot(lhs, amp[...].reshape(owned * e, -1), preferred_element_type=jnp.float32)

    @pl.when(pl.program_id(0) == 0)
    def _():
        out[...] = part

    @pl.when(pl.program_id(0) != 0)
    def _():
        out[...] += part


def product(blocks, amplitudes):
    n, own, r, e = blocks.shape
    a = amplitudes.shape[2]
    step = next(s for s in STEPS if own % s == 0)
    return pl.pallas_call(
        product_kernel,
        grid=(own // step,),
        in_specs=[
            pl.BlockSpec((n, step, r, e), lambda m: (0, m, 0, 0)),
            pl.BlockSpec((step, e, a), lambda m: (m, 0, 0)),
        ],
        out_specs=pl.BlockSpec((n * r, a), lambda m: (0, 0)),
        out_shape=jax.ShapeDtypeStruct((n * r, a), jnp.float32),
        compiler_params=pltpu.CompilerParams(vmem_limit_bytes=48 * 1024 * 1024),
        cost_estimate=pl.CostEstimate(
            flops=2 * n * r * own * e * a,
            bytes_accessed=2 * own * e * (a + n * r) + 4 * n * r * a,
            transcendentals=0,
        ),
    )(blocks, amplitudes)


def exchanged_body(amplitudes, integrals, pair_energy, vir_energy):
    n = lax.axis_size(AXIS)
    chips = n // 2
    me = lax.axis_index(AXIS)
    core = me % 2
    own, e, a = amplitudes.shape
    rows = integrals.shape[2]
    source = integrals.reshape(n, own, rows, e)
    width = a // chips
    same_core = [list(range(c, n, 2)) for c in range(2)]
    starts = [sum(CHUNKS[:q]) for q in range(len(CHUNKS))]

    def exchange(x, groups=None):
        return lax.all_to_all(
            x, AXIS, split_axis=0, concat_axis=0, tiled=True, axis_index_groups=groups
        )

    def halve(blocks, bit):
        odd = (me & bit) != 0
        pair = blocks.reshape(-1, 2, *blocks.shape[1:])
        mine = jnp.where(odd, pair[:, 1], pair[:, 0])
        other = jnp.where(odd, pair[:, 0], pair[:, 1])
        return mine + lax.ppermute(other, AXIS, [(i, i ^ bit) for i in range(n)])

    received, near, done = [], [], []
    for q, r in enumerate(CHUNKS):
        x = source
        if q >= 2:
            x = after(x, received[q - 2])
        x = x[:, :, starts[q] : starts[q] + r]
        if q >= 1:
            x = after(x, received[q - 1], *done[q - 2 : q - 1] if q >= 2 else ())
        received.append(exchange(x))
        if q >= 1:
            blocks = product(received[q - 1], amplitudes).reshape(n, CHUNKS[q - 1], a)
            bit = 1
            while 2 * bit < n:
                blocks = halve(blocks, bit)
                bit *= 2
            near.append(blocks)
            done.append(halve(blocks, bit)[0])
    early = jnp.concatenate(done, axis=0)
    er, late = early.shape[0], CHUNKS[-1]
    part = halve(product(received[-1], amplitudes).reshape(n, late, a), 1)
    row_part = part.reshape(chips, late, chips, width).transpose(0, 2, 1, 3).reshape(chips, -1, width)
    col_part = part.reshape(chips * late, chips, width).transpose(1, 0, 2)
    early_part = early.reshape(er, chips, width).transpose(1, 0, 2)
    got = exchange(jnp.concatenate([row_part, col_part, early_part], axis=1), same_core)
    split = chips * late
    sums = got[:, : 2 * split].sum(0)
    late_rows = sums[:split].reshape(chips, late, width).transpose(1, 0, 2).reshape(late, a)
    late_cols = sums[split:].reshape(chips, late, width)
    cols = jnp.concatenate([got[:, 2 * split :], late_cols], axis=1)
    other = lax.ppermute(cols, AXIS, [(i, i ^ 1) for i in range(n)])
    stacked = jnp.where(core == 0, jnp.stack([cols, other], 1), jnp.stack([other, cols], 1))
    stacked = stacked.reshape(n * rows, 2, width // 2)
    swapped = jnp.where(core == 0, stacked[:, 0], stacked[:, 1])
    paired = jnp.concatenate([early, late_rows], axis=0) + swapped.T
    return paired[:, None, :] / denominator(pair_energy, vir_energy, me * rows, rows)


def solution(mesh):
    n = mesh.shape[AXIS]
    body = exchanged_body if 2 <= n <= 16 and n & (n - 1) == 0 else gathered_body
    in_specs = (P(("grp", AXIS), None, None), P("grp", None, AXIS, None), P("grp"), P("grp"))
    out_specs = P(("grp", AXIS), None, None)
    return jax.shard_map(body, mesh=mesh, in_specs=in_specs, out_specs=out_specs, check_vma=False)
```

time: 462 us -> 445 us (0.963)
  blocking collectives: 0 us -> 31.1 us
  starting transfers between devices: 78 us -> 47.7 us
  Pallas kernels: 45 us -> 37.9 us
  waiting for transfers between devices: 308 us -> 302 us
    all_to_all x6 -> x4, waiting for transfers between devices: 131 us -> 32.6 us  [exchange(): lax.all_to_all(x, AXIS, split_axis=0, concat_axis=0, tiled=True, axis_ind...]
    ppermute x12 -> x14, waiting for transfers between devices: 177 us -> 269 us  [the longest x13 268 us: halve(): return mine + lax.ppermute(other, AXIS, [(i, i ^ bit) for i in range(n)])]
    all_to_all x0 -> x1, blocking collectives: none -> 31.1 us  [exchange(): lax.all_to_all(x, AXIS, split_axis=0, concat_axis=0, tiled=True, axis_ind...]
    all_to_all x6 -> x4, starting transfers between devices: 53.5 us -> 26.9 us  [exchange(): lax.all_to_all(x, AXIS, split_axis=0, concat_axis=0, tiled=True, axis_ind...]
    pallas_call x4, Pallas kernels: 45 us -> 37.9 us  [product(): pl.pallas_call(product_kernel, grid=(own // step,), in_specs=[pl.BlockSpe...]
    ppermute x12 -> x14, starting transfers between devices: 24.5 us -> 20.8 us  [the longest x13 20.7 us: halve(): return mine + lax.ppermute(other, AXIS, [(i, i ^ bit) for i in range(n)])]
  transfers between devices with their start and end apart: 18 -> 18, of which waited for: 14 -> 14; matrix products, arithmetic and copies ran while one was open for 4% -> 4% of each run, Pallas kernels for 10% -> 9%
where the time goes in v3:
time: 445 us; the launch traced here: 444 us
  waiting for transfers between devices  302 us (68%)
  starting transfers between devices  47.7 us (11%)
  Pallas kernels  37.9 us (9%)
  blocking collectives  31.1 us (7%)
  local copies, waits for them, and re-layouts  22.8 us (5%)
    ppermute x13, waiting for transfers between devices, halve(): return mine + lax.ppermute(other, AXIS, [(i, i ^ bit) for i in range(n)])  268 us
    pallas_call x4, Pallas kernels, product(): pl.pallas_call(product_kernel, grid=(own // step,), in_specs=[pl.BlockSpe...  37.9 us
    all_to_all x4, waiting for transfers between devices, exchange(): lax.all_to_all(x, AXIS, split_axis=0, concat_axis=0, tiled=True, axis_ind...  32.6 us
    all_to_all x1, blocking collectives, exchange(): lax.all_to_all(x, AXIS, split_axis=0, concat_axis=0, tiled=True, axis_ind...  31.1 us
    all_to_all x4, starting transfers between devices, exchange(): lax.all_to_all(x, AXIS, split_axis=0, concat_axis=0, tiled=True, axis_ind...  26.9 us
    ppermute x13, starting transfers between devices, halve(): return mine + lax.ppermute(other, AXIS, [(i, i ^ bit) for i in range(n)])  20.7 us
    slice x4, local copies, waits for them, and re-layouts, exchanged_body(): x = x[:, :, starts[q]:starts[q] + r]  19.8 us
  transfers between devices with their start and end apart: 18, of which 14 were waited for; matrix products, arithmetic and copies ran while one was open for 4% of the time, Pallas kernels for 9%

profile of v3, /device:TPU:0, one launch (start us, length us, event | category | flops | bytes accessed | tf_op | source)
XLA Modules:
  0.0 443.9 jit_solution(6407856315259674835)
XLA Ops:
  0.0 3.2 slice.170
  3.2 7.4 %all-to-all-start = ((bf16[16,8,8,1024]{3,2,1,0:T(8,128)(2,1)}), bf16[16,8,8,1024]{3,2,1,0:T(8,128)(2,1)S(1)}, u32[]{:S(2)}, u32[]{:S(2)}) async-start(bf16[16,8,8,1024]{3,2,1,0:T(8,128)(2,1)} %slice.170), calls=%async_computation | async-start | bytes 4194304 | tf_op jit(solution)/shard_map/all_to_all | solution.py:89
  10.5 8.5 %slice.179 = bf16[16,8,32,1024]{3,2,1,0:T(8,128)(2,1)} slice(bf16[16,8,64,1024]{3,2,1,0:T(8,128)(2,1)} %bitcast.268), slice={[0:16], [0:8], [8:40], [0:1024]} | slice | bytes 16777216 | tf_op jit(solution)/shard_map/slice | solution.py:105
  19.0 32.6 %all-to-all-done.blocks = bf16[16,8,8,1024]{3,2,1,0:T(8,128)(2,1)S(1)} async-done(((bf16[16,8,8,1024]{3,2,1,0:T(8,128)(2,1)}), bf16[16,8,8,1024]{3,2,1,0:T(8,128)(2,1)S(1)}, u32[]{:S(2)}, u32[]{:S(2)}) %all-to-all-start) | async-done | bytes 2097184 | tf_op jit(solution)/shard_map/all_to_all | solution.py:89
  51.7 11.3 %all-to-all-start.1 = ((bf16[16,8,32,1024]{3,2,1,0:T(8,128)(2,1)}), bf16[16,8,32,1024]{3,2,1,0:T(8,128)(2,1)}, u32[]{:S(2)}, u32[]{:S(2)}) async-start(bf16[16,8,32,1024]{3,2,1,0:T(8,128)(2,1)} %slice.179), calls=%async_computation.1 | async-start | bytes 16777216 | tf_op jit(solution)/shard_map/all_to_all | solution.py:89
  62.9 7.6 %shard_map.46 = f32[128,1024]{1,0:T(8,128)S(1)} custom-call(bf16[16,8,8,1024]{3,2,1,0:T(8,128)(2,1)S(1)} %all-to-all-done.blocks, bf16[8,1024,1024]{2,1,0:T(8,128)(2,1)} %amp.7), custom_call_target="tpu_custom_call" | custom-call | flops 2147483648 | bytes 19398656 | tf_op jit(solution)/shard_map/pallas_call | solution.py:58
  70.5 0.4 collective-permute-start
  70.9 1.2 collective-permute-done
  72.2 1.9 collective-permute-start.1
  74.1 40.6 %collective-permute-done.1 = f32[4,8,1024]{2,1,0:T(8,128)S(1)} collective-permute-done((f32[4,8,1024]{2,1,0:T(8,128)S(1)}, f32[4,8,1024]{2,1,0:T(8,128)S(1)}, u32[]{:S(2)}, u32[]{:S(2)}) %collective-permute-start.1) | collective-permute-done | bytes 131104 | tf_op jit(solution)/shard_map/ppermute | solution.py:98
  114.8 0.1 collective-permute-start.2
  114.9 85.4 %collective-permute-done.2 = f32[2,8,1024]{2,1,0:T(8,128)S(1)} collective-permute-done((f32[2,8,1024]{2,1,0:T(8,128)S(1)}, f32[2,8,1024]{2,1,0:T(8,128)S(1)}, u32[]{:S(2)}, u32[]{:S(2)}) %collective-permute-start.2) | collective-permute-done | bytes 65568 | tf_op jit(solution)/shard_map/ppermute | solution.py:98
  200.4 4.6 %collective-permute-start.3 = (f32[1,8,1024]{2,1,0:T(8,128)S(1)}, f32[1,8,1024]{2,1,0:T(8,128)S(1)}, u32[]{:S(2)}, u32[]{:S(2)}) collective-permute-start(f32[1,8,1024]{2,1,0:T(8,128)S(1)} %select_bitcast_fusion.12), channel_id=1, source_target_pairs={{0,8},{1,9},{2,10},{3,11},{4,12},{5,13},{6,14},{7,15},{8,0},{9,1},... | collective-permute-start | bytes 98312 | tf_op jit(solution)/shard_map/ppermute | solution.py:98
  204.9 5.0 %slice.152 = bf16[16,8,16,1024]{3,2,1,0:T(8,128)(2,1)} slice(bf16[16,8,64,1024]{3,2,1,0:T(8,128)(2,1)} %bitcast.269), slice={[0:16], [0:8], [40:56], [0:1024]} | slice | bytes 8388608 | tf_op jit(solution)/shard_map/slice | solution.py:105
  209.9 38.3 %collective-permute-done.3 = f32[1,8,1024]{2,1,0:T(8,128)S(1)} collective-permute-done((f32[1,8,1024]{2,1,0:T(8,128)S(1)}, f32[1,8,1024]{2,1,0:T(8,128)S(1)}, u32[]{:S(2)}, u32[]{:S(2)}) %collective-permute-start.3) | collective-permute-done | bytes 32800 | tf_op jit(solution)/shard_map/ppermute | solution.py:98
  248.2 0.0 all-to-all-done.1.blocks
  248.2 4.6 %all-to-all-start.2 = ((bf16[16,8,16,1024]{3,2,1,0:T(8,128)(2,1)}), bf16[16,8,16,1024]{3,2,1,0:T(8,128)(2,1)}, u32[]{:S(2)}, u32[]{:S(2)}) async-start(bf16[16,8,16,1024]{3,2,1,0:T(8,128)(2,1)} %slice.152), calls=%async_computation.2 | async-start | bytes 8388608 | tf_op jit(solution)/shard_map/all_to_all | solution.py:89
  252.8 13.3 %shard_map.47 = f32[512,1024]{1,0:T(8,128)S(1)} custom-call(bf16[16,8,32,1024]{3,2,1,0:T(8,128)(2,1)} %all-to-all-done.1.blocks, bf16[8,1024,1024]{2,1,0:T(8,128)(2,1)} %amp.7), custom_call_target="tpu_custom_call" | custom-call | flops 8589934592 | bytes 27262976 | tf_op jit(solution)/shard_map/pallas_call | solution.py:58
  266.1 0.1 select_bitcast_fusion
  266.2 0.3 collective-permute-start.4
  266.5 2.4 collective-permute-done.4
  269.0 0.3 bitcast_add_fusion
  269.3 0.1 select_bitcast_fusion.2
  269.3 1.8 collective-permute-start.5
  271.2 25.9 %collective-permute-done.5 = f32[4,32,1024]{2,1,0:T(8,128)S(1)} collective-permute-done((f32[4,32,1024]{2,1,0:T(8,128)S(1)}, f32[4,32,1024]{2,1,0:T(8,128)S(1)}, u32[]{:S(2)}, u32[]{:S(2)}) %collective-permute-start.5) | collective-permute-done | bytes 524320 | tf_op jit(solution)/shard_map/ppermute | solution.py:98
  297.1 0.1 fusion.1
  297.2 0.1 collective-permute-start.6
  297.3 29.6 %collective-permute-done.6 = f32[2,32,1024]{2,1,0:T(8,128)S(1)} collective-permute-done((f32[2,32,1024]{2,1,0:T(8,128)S(1)}, f32[2,32,1024]{2,1,0:T(8,128)S(1)}, u32[]{:S(2)}, u32[]{:S(2)}) %collective-permute-start.6) | collective-permute-done | bytes 262176 | tf_op jit(solution)/shard_map/ppermute | solution.py:98
  326.9 0.1 fusion.8
  327.0 4.6 %collective-permute-start.7 = (f32[1,32,1024]{2,1,0:T(8,128)S(1)}, f32[1,32,1024]{2,1,0:T(8,128)S(1)}, u32[]{:S(2)}, u32[]{:S(2)}) collective-permute-start(f32[1,32,1024]{2,1,0:T(8,128)S(1)} %select_bitcast_fusion.8), channel_id=1, source_target_pairs={{0,8},{1,9},{2,10},{3,11},{4,12},{5,13},{6,14},{7,15},{8,0},{9,1},... | collective-permute-start | bytes 393224 | tf_op jit(solution)/shard_map/ppermute | solution.py:98
  331.6 3.1 slice.161
  334.8 17.6 %collective-permute-done.7 = f32[1,32,1024]{2,1,0:T(8,128)S(1)} collective-permute-done((f32[1,32,1024]{2,1,0:T(8,128)S(1)}, f32[1,32,1024]{2,1,0:T(8,128)S(1)}, u32[]{:S(2)}, u32[]{:S(2)}) %collective-permute-start.7) | collective-permute-done | bytes 131104 | tf_op jit(solution)/shard_map/ppermute | solution.py:98
  352.4 0.0 all-to-all-done.2.blocks
  352.4 3.7 all-to-all-start.3
  356.2 9.5 %shard_map.48 = f32[256,1024]{1,0:T(8,128)S(1)} custom-call(bf16[16,8,16,1024]{3,2,1,0:T(8,128)(2,1)} %all-to-all-done.2.blocks, bf16[8,1024,1024]{2,1,0:T(8,128)(2,1)} %amp.7), custom_call_target="tpu_custom_call" | custom-call | flops 4294967296 | bytes 22020096 | tf_op jit(solution)/shard_map/pallas_call | solution.py:58
  365.7 0.1 select_bitcast_fusion.1
  365.8 0.4 collective-permute-start.8
  366.1 1.6 collective-permute-done.8
  367.8 0.1 bitcast_add_fusion.1
  367.9 1.9 collective-permute-start.9
  369.8 12.4 %collective-permute-done.9 = f32[4,16,1024]{2,1,0:T(8,128)S(1)} collective-permute-done((f32[4,16,1024]{2,1,0:T(8,128)S(1)}, f32[4,16,1024]{2,1,0:T(8,128)S(1)}, u32[]{:S(2)}, u32[]{:S(2)}) %collective-permute-start.9) | collective-permute-done | bytes 262176 | tf_op jit(solution)/shard_map/ppermute | solution.py:98
  382.3 0.1 collective-permute-start.10
  382.4 11.4 %collective-permute-done.10 = f32[2,16,1024]{2,1,0:T(8,128)S(1)} collective-permute-done((f32[2,16,1024]{2,1,0:T(8,128)S(1)}, f32[2,16,1024]{2,1,0:T(8,128)S(1)}, u32[]{:S(2)}, u32[]{:S(2)}) %collective-permute-start.10) | collective-permute-done | bytes 131104 | tf_op jit(solution)/shard_map/ppermute | solution.py:98
  393.8 4.6 %collective-permute-start.11 = (f32[1,16,1024]{2,1,0:T(8,128)S(1)}, f32[1,16,1024]{2,1,0:T(8,128)S(1)}, u32[]{:S(2)}, u32[]{:S(2)}) collective-permute-start(f32[1,16,1024]{2,1,0:T(8,128)S(1)} %select_bitcast_fusion.10), channel_id=1, source_target_pairs={{0,8},{1,9},{2,10},{3,11},{4,12},{5,13},{6,14},{7,15},{8,0},{9,1},... | collective-permute-start | bytes 196616 | tf_op jit(solution)/shard_map/ppermute | solution.py:98
  398.4 0.0 all-to-all-done.3.blocks
  398.4 7.5 %shard_map.49 = f32[128,1024]{1,0:T(8,128)S(1)} custom-call(bf16[16,8,8,1024]{3,2,1,0:T(8,128)(2,1)S(1)} %all-to-all-done.3.blocks, bf16[8,1024,1024]{2,1,0:T(8,128)(2,1)} %amp.7), custom_call_target="tpu_custom_call" | custom-call | flops 2147483648 | bytes 19398656 | tf_op jit(solution)/shard_map/pallas_call | solution.py:58
  406.0 0.1 collective-permute-start.12
  406.1 1.9 collective-permute-done.11
  408.0 0.0 collective-permute-done.12
  408.0 0.1 bitcast_add_fusion.2
  408.2 0.1 copy.125
  408.2 0.1 pad_maximum_fusion
  408.3 0.0 copy-start
  408.3 31.1 %all_to_all.25 = f32[8,184,128]{2,1,0:T(8,128)S(1)} all-to-all(f32[8,184,128]{2,1,0:T(8,128)S(1)} %pad_maximum_fusion), channel_id=1, replica_groups={{0,2,4,6,8,10,12,14},{1,3,5,7,9,11,13,15},{16,18,20,22,24,26,28,30},{17..., dimensions={0} | all-to-all | bytes 1507328 | tf_op jit(solution)/shard_map/all_to_all | solution.py:89
  439.5 0.1 collective-permute-start.13
  440.2 0.0 copy-done
  440.2 0.1 dynamic_slice.3
  440.3 0.8 collective-permute-done.13
  441.1 0.8 copy.104
  441.9 0.9 reshape.262
  442.8 0.1 fusion.5
  443.0 1.0 copy.103
  (30 shorter events, 0.7 us)
Async XLA Ops:
  3.2 48.5 %all-to-all-start = ((bf16[16,8,8,1024]{3,2,1,0:T(8,128)(2,1)}), bf16[16,8,8,1024]{3,2,1,0:T(8,128)(2,1)S(1)}, u32[]{:S(2)}, u32[]{:S(2)}) async-start(bf16[16,8,8,1024]{3,2,1,0:T(8,128)(2,1)} %slice.170), calls=%async_computation | async-start | bytes 4194304 | tf_op jit(solution)/shard_map/all_to_all | solution.py:89
  51.7 196.6 %all-to-all-start.1 = ((bf16[16,8,32,1024]{3,2,1,0:T(8,128)(2,1)}), bf16[16,8,32,1024]{3,2,1,0:T(8,128)(2,1)}, u32[]{:S(2)}, u32[]{:S(2)}) async-start(bf16[16,8,32,1024]{3,2,1,0:T(8,128)(2,1)} %slice.179), calls=%async_computation.1 | async-start | bytes 16777216 | tf_op jit(solution)/shard_map/all_to_all | solution.py:89
  70.5 1.6 collective-permute-start
  72.2 42.5 %collective-permute-start.1 = (f32[4,8,1024]{2,1,0:T(8,128)S(1)}, f32[4,8,1024]{2,1,0:T(8,128)S(1)}, u32[]{:S(2)}, u32[]{:S(2)}) collective-permute-start(f32[4,8,1024]{2,1,0:T(8,128)S(1)} %select_bitcast_fusion.9), channel_id=1, source_target_pairs={{0,2},{1,3},{2,0},{3,1},{4,6},{5,7},{6,4},{7,5},{8,10},{9,11},{10,... | collective-permute-start | bytes 393224 | tf_op jit(solution)/shard_map/ppermute | solution.py:98
  114.8 85.5 %collective-permute-start.2 = (f32[2,8,1024]{2,1,0:T(8,128)S(1)}, f32[2,8,1024]{2,1,0:T(8,128)S(1)}, u32[]{:S(2)}, u32[]{:S(2)}) collective-permute-start(f32[2,8,1024]{2,1,0:T(8,128)S(1)} %select_bitcast_fusion.11), channel_id=1, source_target_pairs={{0,4},{1,5},{2,6},{3,7},{4,0},{5,1},{6,2},{7,3},{8,12},{9,13},{10,... | collective-permute-start | bytes 196616 | tf_op jit(solution)/shard_map/ppermute | solution.py:98
  200.4 47.9 %collective-permute-start.3 = (f32[1,8,1024]{2,1,0:T(8,128)S(1)}, f32[1,8,1024]{2,1,0:T(8,128)S(1)}, u32[]{:S(2)}, u32[]{:S(2)}) collective-permute-start(f32[1,8,1024]{2,1,0:T(8,128)S(1)} %select_bitcast_fusion.12), channel_id=1, source_target_pairs={{0,8},{1,9},{2,10},{3,11},{4,12},{5,13},{6,14},{7,15},{8,0},{9,1},... | collective-permute-start | bytes 98312 | tf_op jit(solution)/shard_map/ppermute | solution.py:98
  248.2 104.2 %all-to-all-start.2 = ((bf16[16,8,16,1024]{3,2,1,0:T(8,128)(2,1)}), bf16[16,8,16,1024]{3,2,1,0:T(8,128)(2,1)}, u32[]{:S(2)}, u32[]{:S(2)}) async-start(bf16[16,8,16,1024]{3,2,1,0:T(8,128)(2,1)} %slice.152), calls=%async_computation.2 | async-start | bytes 8388608 | tf_op jit(solution)/shard_map/all_to_all | solution.py:89
  266.2 2.7 collective-permute-start.4
  269.3 27.7 %collective-permute-start.5 = (f32[4,32,1024]{2,1,0:T(8,128)S(1)}, f32[4,32,1024]{2,1,0:T(8,128)S(1)}, u32[]{:S(2)}, u32[]{:S(2)}) collective-permute-start(f32[4,32,1024]{2,1,0:T(8,128)S(1)} %select_bitcast_fusion.2), channel_id=1, source_target_pairs={{0,2},{1,3},{2,0},{3,1},{4,6},{5,7},{6,4},{7,5},{8,10},{9,11},{10,... | collective-permute-start | bytes 1572872 | tf_op jit(solution)/shard_map/ppermute | solution.py:98
  297.2 29.7 %collective-permute-start.6 = (f32[2,32,1024]{2,1,0:T(8,128)S(1)}, f32[2,32,1024]{2,1,0:T(8,128)S(1)}, u32[]{:S(2)}, u32[]{:S(2)}) collective-permute-start(f32[2,32,1024]{2,1,0:T(8,128)S(1)} %select_bitcast_fusion.5), channel_id=1, source_target_pairs={{0,4},{1,5},{2,6},{3,7},{4,0},{5,1},{6,2},{7,3},{8,12},{9,13},{10,... | collective-permute-start | bytes 786440 | tf_op jit(solution)/shard_map/ppermute | solution.py:98
  327.0 25.4 %collective-permute-start.7 = (f32[1,32,1024]{2,1,0:T(8,128)S(1)}, f32[1,32,1024]{2,1,0:T(8,128)S(1)}, u32[]{:S(2)}, u32[]{:S(2)}) collective-permute-start(f32[1,32,1024]{2,1,0:T(8,128)S(1)} %select_bitcast_fusion.8), channel_id=1, source_target_pairs={{0,8},{1,9},{2,10},{3,11},{4,12},{5,13},{6,14},{7,15},{8,0},{9,1},... | collective-permute-start | bytes 393224 | tf_op jit(solution)/shard_map/ppermute | solution.py:98
  352.4 46.0 %all-to-all-start.3 = ((bf16[16,8,8,1024]{3,2,1,0:T(8,128)(2,1)}), bf16[16,8,8,1024]{3,2,1,0:T(8,128)(2,1)S(1)}, u32[]{:S(2)}, u32[]{:S(2)}) async-start(bf16[16,8,8,1024]{3,2,1,0:T(8,128)(2,1)} %slice.161), calls=%async_computation.3 | async-start | bytes 4194304 | tf_op jit(solution)/shard_map/all_to_all | solution.py:89
  365.8 2.0 collective-permute-start.8
  367.9 14.3 %collective-permute-start.9 = (f32[4,16,1024]{2,1,0:T(8,128)S(1)}, f32[4,16,1024]{2,1,0:T(8,128)S(1)}, u32[]{:S(2)}, u32[]{:S(2)}) collective-permute-start(f32[4,16,1024]{2,1,0:T(8,128)S(1)} %select_bitcast_fusion.4), channel_id=1, source_target_pairs={{0,2},{1,3},{2,0},{3,1},{4,6},{5,7},{6,4},{7,5},{8,10},{9,11},{10,... | collective-permute-start | bytes 786440 | tf_op jit(solution)/shard_map/ppermute | solution.py:98
  382.3 11.5 %collective-permute-start.10 = (f32[2,16,1024]{2,1,0:T(8,128)S(1)}, f32[2,16,1024]{2,1,0:T(8,128)S(1)}, u32[]{:S(2)}, u32[]{:S(2)}) collective-permute-start(f32[2,16,1024]{2,1,0:T(8,128)S(1)} %select_bitcast_fusion.7), channel_id=1, source_target_pairs={{0,4},{1,5},{2,6},{3,7},{4,0},{5,1},{6,2},{7,3},{8,12},{9,13},{10,... | collective-permute-start | bytes 393224 | tf_op jit(solution)/shard_map/ppermute | solution.py:98
  393.8 14.1 %collective-permute-start.11 = (f32[1,16,1024]{2,1,0:T(8,128)S(1)}, f32[1,16,1024]{2,1,0:T(8,128)S(1)}, u32[]{:S(2)}, u32[]{:S(2)}) collective-permute-start(f32[1,16,1024]{2,1,0:T(8,128)S(1)} %select_bitcast_fusion.10), channel_id=1, source_target_pairs={{0,8},{1,9},{2,10},{3,11},{4,12},{5,13},{6,14},{7,15},{8,0},{9,1},... | collective-permute-start | bytes 196616 | tf_op jit(solution)/shard_map/ppermute | solution.py:98
  406.0 2.0 collective-permute-start.12
  408.3 31.9 %copy-start = (f32[1024]{0:T(1024)S(1)}, f32[1024]{0:T(1024)}, u32[]{:S(2)}) copy-start(f32[1024]{0:T(1024)} %param.7) | copy-start | bytes 12292
  439.5 1.6 collective-permute-start.13

commit v4 on v3

--- a/solution.py
+++ b/solution.py
@@ -9,6 +9,7 @@
 AXIS = "vir"
 CHUNKS = (8, 32, 16, 8)
 STEPS = (2, 1)
+SUBLANES = 8
 
 
 def denominator(pair_energy, vir_energy, start, rows):
@@ -24,6 +25,10 @@
     swapped = lax.all_to_all(cycle, AXIS, split_axis=2, concat_axis=0, tiled=True)
     paired = cycle + jnp.transpose(swapped, (2, 1, 0))
     return paired / denominator(pair_energy, vir_energy, lax.axis_index(AXIS) * rows, rows)
+
+
+def exponent_of(largest):
+    return jnp.ceil(jnp.log2(jnp.maximum(largest, 2.0**-100))) - 14.0
 
 
 def after(x, *deps):
@@ -120,7 +125,12 @@
     row_part = part.reshape(chips, late, chips, width).transpose(0, 2, 1, 3).reshape(chips, -1, width)
     col_part = part.reshape(chips * late, chips, width).transpose(1, 0, 2)
     early_part = early.reshape(er, chips, width).transpose(1, 0, 2)
-    got = exchange(jnp.concatenate([row_part, col_part, early_part], axis=1), same_core)
+    exponent = exponent_of(jnp.maximum(jnp.max(jnp.abs(part)), jnp.max(jnp.abs(early))))
+    parts = jnp.concatenate([row_part, col_part, early_part], axis=1) * jnp.exp2(-exponent)
+    tag = jnp.full((chips, SUBLANES, width), exponent, jnp.float32)
+    sent = jnp.concatenate([parts, tag], axis=1).astype(jnp.float16)
+    got = exchange(sent, same_core).astype(jnp.float32)
+    got = got[:, :-SUBLANES] * jnp.exp2(got[:, -1:, :])
     split = chips * late
     sums = got[:, : 2 * split].sum(0)
     late_rows = sums[:split].reshape(chips, late, width).transpose(1, 0, 2).reshape(late, a)

time: 445 us -> 439 us (0.987)
  blocking collectives: 31.1 us -> 23.1 us
    all_to_all x1, blocking collectives: 31.1 us -> 23.1 us  [exchange(): lax.all_to_all(x, AXIS, split_axis=0, concat_axis=0, tiled=True, axis_ind...]
where the time goes in v4:
time: 439 us
  waiting for transfers between devices  302 us (69%)
  starting transfers between devices  47.7 us (11%)
  Pallas kernels  37.9 us (9%)
  blocking collectives  23.1 us (5%)
  local copies, waits for them, and re-layouts  22.9 us (5%)
    ppermute x13, waiting for transfers between devices, halve(): return mine + lax.ppermute(other, AXIS, [(i, i ^ bit) for i in range(n)])  268 us
    pallas_call x4, Pallas kernels, product(): pl.pallas_call(product_kernel, grid=(own // step,), in_specs=[pl.BlockSpe...  37.9 us
    all_to_all x4, waiting for transfers between devices, exchange(): lax.all_to_all(x, AXIS, split_axis=0, concat_axis=0, tiled=True, axis_ind...  32.6 us
    all_to_all x4, starting transfers between devices, exchange(): lax.all_to_all(x, AXIS, split_axis=0, concat_axis=0, tiled=True, axis_ind...  26.9 us
    all_to_all x1, blocking collectives, exchange(): lax.all_to_all(x, AXIS, split_axis=0, concat_axis=0, tiled=True, axis_ind...  23.1 us
    ppermute x13, starting transfers between devices, halve(): return mine + lax.ppermute(other, AXIS, [(i, i ^ bit) for i in range(n)])  20.7 us
    slice x4, local copies, waits for them, and re-layouts, exchanged_body(): x = x[:, :, starts[q]:starts[q] + r]  19.9 us
  transfers between devices with their start and end apart: 18, of which 14 were waited for; matrix products, arithmetic and copies ran while one was open for 4% of the time, Pallas kernels for 9%

profile of v4, /device:TPU:0, one launch (start us, length us, event | category | flops | bytes accessed | tf_op | source)
XLA Modules:
  0.0 438.7 jit_solution(17527352528586551804)
XLA Ops:
  0.0 3.2 slice.178
  3.2 7.4 %all-to-all-start = ((bf16[16,8,8,1024]{3,2,1,0:T(8,128)(2,1)}), bf16[16,8,8,1024]{3,2,1,0:T(8,128)(2,1)S(1)}, u32[]{:S(2)}, u32[]{:S(2)}) async-start(bf16[16,8,8,1024]{3,2,1,0:T(8,128)(2,1)} %slice.178), calls=%async_computation | async-start | bytes 4194304 | tf_op jit(solution)/shard_map/all_to_all | solution.py:94
  10.6 8.5 %slice.187 = bf16[16,8,32,1024]{3,2,1,0:T(8,128)(2,1)} slice(bf16[16,8,64,1024]{3,2,1,0:T(8,128)(2,1)} %bitcast.272), slice={[0:16], [0:8], [8:40], [0:1024]} | slice | bytes 16777216 | tf_op jit(solution)/shard_map/slice | solution.py:110
  19.1 32.6 %all-to-all-done.blocks = bf16[16,8,8,1024]{3,2,1,0:T(8,128)(2,1)S(1)} async-done(((bf16[16,8,8,1024]{3,2,1,0:T(8,128)(2,1)}), bf16[16,8,8,1024]{3,2,1,0:T(8,128)(2,1)S(1)}, u32[]{:S(2)}, u32[]{:S(2)}) %all-to-all-start) | async-done | bytes 2097184 | tf_op jit(solution)/shard_map/all_to_all | solution.py:94
  51.7 11.3 %all-to-all-start.1 = ((bf16[16,8,32,1024]{3,2,1,0:T(8,128)(2,1)}), bf16[16,8,32,1024]{3,2,1,0:T(8,128)(2,1)}, u32[]{:S(2)}, u32[]{:S(2)}) async-start(bf16[16,8,32,1024]{3,2,1,0:T(8,128)(2,1)} %slice.187), calls=%async_computation.1 | async-start | bytes 16777216 | tf_op jit(solution)/shard_map/all_to_all | solution.py:94
  62.9 7.6 %shard_map.46 = f32[128,1024]{1,0:T(8,128)S(1)} custom-call(bf16[16,8,8,1024]{3,2,1,0:T(8,128)(2,1)S(1)} %all-to-all-done.blocks, bf16[8,1024,1024]{2,1,0:T(8,128)(2,1)} %amp.7), custom_call_target="tpu_custom_call" | custom-call | flops 2147483648 | bytes 19398656 | tf_op jit(solution)/shard_map/pallas_call | solution.py:63
  70.5 0.4 collective-permute-start
  71.0 1.2 collective-permute-done
  72.2 1.9 collective-permute-start.1
  74.1 40.6 %collective-permute-done.1 = f32[4,8,1024]{2,1,0:T(8,128)S(1)} collective-permute-done((f32[4,8,1024]{2,1,0:T(8,128)S(1)}, f32[4,8,1024]{2,1,0:T(8,128)S(1)}, u32[]{:S(2)}, u32[]{:S(2)}) %collective-permute-start.1) | collective-permute-done | bytes 131104 | tf_op jit(solution)/shard_map/ppermute | solution.py:103
  114.8 0.1 collective-permute-start.2
  114.9 85.4 %collective-permute-done.2 = f32[2,8,1024]{2,1,0:T(8,128)S(1)} collective-permute-done((f32[2,8,1024]{2,1,0:T(8,128)S(1)}, f32[2,8,1024]{2,1,0:T(8,128)S(1)}, u32[]{:S(2)}, u32[]{:S(2)}) %collective-permute-start.2) | collective-permute-done | bytes 65568 | tf_op jit(solution)/shard_map/ppermute | solution.py:103
  200.4 4.6 %collective-permute-start.3 = (f32[1,8,1024]{2,1,0:T(8,128)S(1)}, f32[1,8,1024]{2,1,0:T(8,128)S(1)}, u32[]{:S(2)}, u32[]{:S(2)}) collective-permute-start(f32[1,8,1024]{2,1,0:T(8,128)S(1)} %select_bitcast_fusion.12), channel_id=1, source_target_pairs={{0,8},{1,9},{2,10},{3,11},{4,12},{5,13},{6,14},{7,15},{8,0},{9,1},... | collective-permute-start | bytes 98312 | tf_op jit(solution)/shard_map/ppermute | solution.py:103
  204.9 5.0 %slice.158 = bf16[16,8,16,1024]{3,2,1,0:T(8,128)(2,1)} slice(bf16[16,8,64,1024]{3,2,1,0:T(8,128)(2,1)} %bitcast.273), slice={[0:16], [0:8], [40:56], [0:1024]} | slice | bytes 8388608 | tf_op jit(solution)/shard_map/slice | solution.py:110
  209.9 38.3 %collective-permute-done.3 = f32[1,8,1024]{2,1,0:T(8,128)S(1)} collective-permute-done((f32[1,8,1024]{2,1,0:T(8,128)S(1)}, f32[1,8,1024]{2,1,0:T(8,128)S(1)}, u32[]{:S(2)}, u32[]{:S(2)}) %collective-permute-start.3) | collective-permute-done | bytes 32800 | tf_op jit(solution)/shard_map/ppermute | solution.py:103
  248.2 0.0 all-to-all-done.1.blocks
  248.2 4.5 %all-to-all-start.2 = ((bf16[16,8,16,1024]{3,2,1,0:T(8,128)(2,1)}), bf16[16,8,16,1024]{3,2,1,0:T(8,128)(2,1)}, u32[]{:S(2)}, u32[]{:S(2)}) async-start(bf16[16,8,16,1024]{3,2,1,0:T(8,128)(2,1)} %slice.158), calls=%async_computation.2 | async-start | bytes 8388608 | tf_op jit(solution)/shard_map/all_to_all | solution.py:94
  252.8 13.3 %shard_map.47 = f32[512,1024]{1,0:T(8,128)S(1)} custom-call(bf16[16,8,32,1024]{3,2,1,0:T(8,128)(2,1)} %all-to-all-done.1.blocks, bf16[8,1024,1024]{2,1,0:T(8,128)(2,1)} %amp.7), custom_call_target="tpu_custom_call" | custom-call | flops 8589934592 | bytes 27262976 | tf_op jit(solution)/shard_map/pallas_call | solution.py:63
  266.1 0.1 select_bitcast_fusion
  266.2 0.3 collective-permute-start.4
  266.5 2.4 collective-permute-done.4
  269.0 0.3 bitcast_add_fusion
  269.3 0.1 select_bitcast_fusion.2
  269.3 1.8 collective-permute-start.5
  271.2 25.9 %collective-permute-done.5 = f32[4,32,1024]{2,1,0:T(8,128)S(1)} collective-permute-done((f32[4,32,1024]{2,1,0:T(8,128)S(1)}, f32[4,32,1024]{2,1,0:T(8,128)S(1)}, u32[]{:S(2)}, u32[]{:S(2)}) %collective-permute-start.5) | collective-permute-done | bytes 524320 | tf_op jit(solution)/shard_map/ppermute | solution.py:103
  297.1 0.1 fusion.2
  297.2 0.1 collective-permute-start.6
  297.3 29.6 %collective-permute-done.6 = f32[2,32,1024]{2,1,0:T(8,128)S(1)} collective-permute-done((f32[2,32,1024]{2,1,0:T(8,128)S(1)}, f32[2,32,1024]{2,1,0:T(8,128)S(1)}, u32[]{:S(2)}, u32[]{:S(2)}) %collective-permute-start.6) | collective-permute-done | bytes 262176 | tf_op jit(solution)/shard_map/ppermute | solution.py:103
  326.9 0.1 fusion.9
  327.0 4.6 %collective-permute-start.7 = (f32[1,32,1024]{2,1,0:T(8,128)S(1)}, f32[1,32,1024]{2,1,0:T(8,128)S(1)}, u32[]{:S(2)}, u32[]{:S(2)}) collective-permute-start(f32[1,32,1024]{2,1,0:T(8,128)S(1)} %select_bitcast_fusion.8), channel_id=1, source_target_pairs={{0,8},{1,9},{2,10},{3,11},{4,12},{5,13},{6,14},{7,15},{8,0},{9,1},... | collective-permute-start | bytes 393224 | tf_op jit(solution)/shard_map/ppermute | solution.py:103
  331.6 3.2 slice.167
  334.8 17.6 %collective-permute-done.7 = f32[1,32,1024]{2,1,0:T(8,128)S(1)} collective-permute-done((f32[1,32,1024]{2,1,0:T(8,128)S(1)}, f32[1,32,1024]{2,1,0:T(8,128)S(1)}, u32[]{:S(2)}, u32[]{:S(2)}) %collective-permute-start.7) | collective-permute-done | bytes 131104 | tf_op jit(solution)/shard_map/ppermute | solution.py:103
  352.4 0.0 all-to-all-done.2.blocks
  352.4 3.7 all-to-all-start.3
  356.2 9.5 %shard_map.48 = f32[256,1024]{1,0:T(8,128)S(1)} custom-call(bf16[16,8,16,1024]{3,2,1,0:T(8,128)(2,1)} %all-to-all-done.2.blocks, bf16[8,1024,1024]{2,1,0:T(8,128)(2,1)} %amp.7), custom_call_target="tpu_custom_call" | custom-call | flops 4294967296 | bytes 22020096 | tf_op jit(solution)/shard_map/pallas_call | solution.py:63
  365.7 0.1 select_bitcast_fusion.1
  365.8 0.4 collective-permute-start.8
  366.1 1.6 collective-permute-done.8
  367.8 0.1 bitcast_add_fusion.1
  367.9 1.9 collective-permute-start.9
  369.8 12.4 %collective-permute-done.9 = f32[4,16,1024]{2,1,0:T(8,128)S(1)} collective-permute-done((f32[4,16,1024]{2,1,0:T(8,128)S(1)}, f32[4,16,1024]{2,1,0:T(8,128)S(1)}, u32[]{:S(2)}, u32[]{:S(2)}) %collective-permute-start.9) | collective-permute-done | bytes 262176 | tf_op jit(solution)/shard_map/ppermute | solution.py:103
  382.3 0.1 collective-permute-start.10
  382.4 11.4 %collective-permute-done.10 = f32[2,16,1024]{2,1,0:T(8,128)S(1)} collective-permute-done((f32[2,16,1024]{2,1,0:T(8,128)S(1)}, f32[2,16,1024]{2,1,0:T(8,128)S(1)}, u32[]{:S(2)}, u32[]{:S(2)}) %collective-permute-start.10) | collective-permute-done | bytes 131104 | tf_op jit(solution)/shard_map/ppermute | solution.py:103
  393.8 4.6 %collective-permute-start.11 = (f32[1,16,1024]{2,1,0:T(8,128)S(1)}, f32[1,16,1024]{2,1,0:T(8,128)S(1)}, u32[]{:S(2)}, u32[]{:S(2)}) collective-permute-start(f32[1,16,1024]{2,1,0:T(8,128)S(1)} %select_bitcast_fusion.10), channel_id=1, source_target_pairs={{0,8},{1,9},{2,10},{3,11},{4,12},{5,13},{6,14},{7,15},{8,0},{9,1},... | collective-permute-start | bytes 196616 | tf_op jit(solution)/shard_map/ppermute | solution.py:103
  398.4 0.0 all-to-all-done.3.blocks
  398.4 7.5 %shard_map.49 = f32[128,1024]{1,0:T(8,128)S(1)} custom-call(bf16[16,8,8,1024]{3,2,1,0:T(8,128)(2,1)S(1)} %all-to-all-done.3.blocks, bf16[8,1024,1024]{2,1,0:T(8,128)(2,1)} %amp.7), custom_call_target="tpu_custom_call" | custom-call | flops 2147483648 | bytes 19398656 | tf_op jit(solution)/shard_map/pallas_call | solution.py:63
  406.0 0.1 collective-permute-start.12
  406.1 1.9 collective-permute-done.11
  408.0 0.6 fusion.12
  408.6 0.0 collective-permute-done.12
  408.6 0.6 abs_reduce_fusion
  410.6 0.1 copy.125
  410.7 0.1 fusion
  410.8 0.1 concatenate.31
  410.9 23.1 %all_to_all.25 = f16[8,192,128]{2,1,0:T(8,128)(2,1)S(1)} all-to-all(f16[8,192,128]{2,1,0:T(8,128)(2,1)S(1)} %concatenate.31), channel_id=1, replica_groups={{0,2,4,6,8,10,12,14},{1,3,5,7,9,11,13,15},{16,18,20,22,24,26,28,30},{17..., dimensions={0} | all-to-all | bytes 786432 | tf_op jit(solution)/shard_map/all_to_all | solution.py:94
  434.0 0.1 convert_element_type.4
  434.1 0.1 slice_multiply_fusion
  434.2 0.1 collective-permute-start.13
  435.0 0.1 dynamic_slice.3
  435.1 0.8 collective-permute-done.13
  435.9 0.8 copy.104
  436.7 0.9 reshape.262
  437.6 0.1 fusion.6
  437.8 1.0 copy.103
  (33 shorter events, 0.7 us)
Async XLA Ops:
  3.2 48.5 %all-to-all-start = ((bf16[16,8,8,1024]{3,2,1,0:T(8,128)(2,1)}), bf16[16,8,8,1024]{3,2,1,0:T(8,128)(2,1)S(1)}, u32[]{:S(2)}, u32[]{:S(2)}) async-start(bf16[16,8,8,1024]{3,2,1,0:T(8,128)(2,1)} %slice.178), calls=%async_computation | async-start | bytes 4194304 | tf_op jit(solution)/shard_map/all_to_all | solution.py:94
  51.7 196.6 %all-to-all-start.1 = ((bf16[16,8,32,1024]{3,2,1,0:T(8,128)(2,1)}), bf16[16,8,32,1024]{3,2,1,0:T(8,128)(2,1)}, u32[]{:S(2)}, u32[]{:S(2)}) async-start(bf16[16,8,32,1024]{3,2,1,0:T(8,128)(2,1)} %slice.187), calls=%async_computation.1 | async-start | bytes 16777216 | tf_op jit(solution)/shard_map/all_to_all | solution.py:94
  70.5 1.6 collective-permute-start
  72.2 42.6 %collective-permute-start.1 = (f32[4,8,1024]{2,1,0:T(8,128)S(1)}, f32[4,8,1024]{2,1,0:T(8,128)S(1)}, u32[]{:S(2)}, u32[]{:S(2)}) collective-permute-start(f32[4,8,1024]{2,1,0:T(8,128)S(1)} %select_bitcast_fusion.9), channel_id=1, source_target_pairs={{0,2},{1,3},{2,0},{3,1},{4,6},{5,7},{6,4},{7,5},{8,10},{9,11},{10,... | collective-permute-start | bytes 393224 | tf_op jit(solution)/shard_map/ppermute | solution.py:103
  114.8 85.5 %collective-permute-start.2 = (f32[2,8,1024]{2,1,0:T(8,128)S(1)}, f32[2,8,1024]{2,1,0:T(8,128)S(1)}, u32[]{:S(2)}, u32[]{:S(2)}) collective-permute-start(f32[2,8,1024]{2,1,0:T(8,128)S(1)} %select_bitcast_fusion.11), channel_id=1, source_target_pairs={{0,4},{1,5},{2,6},{3,7},{4,0},{5,1},{6,2},{7,3},{8,12},{9,13},{10,... | collective-permute-start | bytes 196616 | tf_op jit(solution)/shard_map/ppermute | solution.py:103
  200.4 47.9 %collective-permute-start.3 = (f32[1,8,1024]{2,1,0:T(8,128)S(1)}, f32[1,8,1024]{2,1,0:T(8,128)S(1)}, u32[]{:S(2)}, u32[]{:S(2)}) collective-permute-start(f32[1,8,1024]{2,1,0:T(8,128)S(1)} %select_bitcast_fusion.12), channel_id=1, source_target_pairs={{0,8},{1,9},{2,10},{3,11},{4,12},{5,13},{6,14},{7,15},{8,0},{9,1},... | collective-permute-start | bytes 98312 | tf_op jit(solution)/shard_map/ppermute | solution.py:103
  248.2 104.2 %all-to-all-start.2 = ((bf16[16,8,16,1024]{3,2,1,0:T(8,128)(2,1)}), bf16[16,8,16,1024]{3,2,1,0:T(8,128)(2,1)}, u32[]{:S(2)}, u32[]{:S(2)}) async-start(bf16[16,8,16,1024]{3,2,1,0:T(8,128)(2,1)} %slice.158), calls=%async_computation.2 | async-start | bytes 8388608 | tf_op jit(solution)/shard_map/all_to_all | solution.py:94
  266.2 2.7 collective-permute-start.4
  269.3 27.7 %collective-permute-start.5 = (f32[4,32,1024]{2,1,0:T(8,128)S(1)}, f32[4,32,1024]{2,1,0:T(8,128)S(1)}, u32[]{:S(2)}, u32[]{:S(2)}) collective-permute-start(f32[4,32,1024]{2,1,0:T(8,128)S(1)} %select_bitcast_fusion.2), channel_id=1, source_target_pairs={{0,2},{1,3},{2,0},{3,1},{4,6},{5,7},{6,4},{7,5},{8,10},{9,11},{10,... | collective-permute-start | bytes 1572872 | tf_op jit(solution)/shard_map/ppermute | solution.py:103
  297.2 29.7 %collective-permute-start.6 = (f32[2,32,1024]{2,1,0:T(8,128)S(1)}, f32[2,32,1024]{2,1,0:T(8,128)S(1)}, u32[]{:S(2)}, u32[]{:S(2)}) collective-permute-start(f32[2,32,1024]{2,1,0:T(8,128)S(1)} %select_bitcast_fusion.5), channel_id=1, source_target_pairs={{0,4},{1,5},{2,6},{3,7},{4,0},{5,1},{6,2},{7,3},{8,12},{9,13},{10,... | collective-permute-start | bytes 786440 | tf_op jit(solution)/shard_map/ppermute | solution.py:103
  327.0 25.4 %collective-permute-start.7 = (f32[1,32,1024]{2,1,0:T(8,128)S(1)}, f32[1,32,1024]{2,1,0:T(8,128)S(1)}, u32[]{:S(2)}, u32[]{:S(2)}) collective-permute-start(f32[1,32,1024]{2,1,0:T(8,128)S(1)} %select_bitcast_fusion.8), channel_id=1, source_target_pairs={{0,8},{1,9},{2,10},{3,11},{4,12},{5,13},{6,14},{7,15},{8,0},{9,1},... | collective-permute-start | bytes 393224 | tf_op jit(solution)/shard_map/ppermute | solution.py:103
  352.4 46.0 %all-to-all-start.3 = ((bf16[16,8,8,1024]{3,2,1,0:T(8,128)(2,1)}), bf16[16,8,8,1024]{3,2,1,0:T(8,128)(2,1)S(1)}, u32[]{:S(2)}, u32[]{:S(2)}) async-start(bf16[16,8,8,1024]{3,2,1,0:T(8,128)(2,1)} %slice.167), calls=%async_computation.3 | async-start | bytes 4194304 | tf_op jit(solution)/shard_map/all_to_all | solution.py:94
  365.8 2.0 collective-permute-start.8
  367.9 14.3 %collective-permute-start.9 = (f32[4,16,1024]{2,1,0:T(8,128)S(1)}, f32[4,16,1024]{2,1,0:T(8,128)S(1)}, u32[]{:S(2)}, u32[]{:S(2)}) collective-permute-start(f32[4,16,1024]{2,1,0:T(8,128)S(1)} %select_bitcast_fusion.4), channel_id=1, source_target_pairs={{0,2},{1,3},{2,0},{3,1},{4,6},{5,7},{6,4},{7,5},{8,10},{9,11},{10,... | collective-permute-start | bytes 786440 | tf_op jit(solution)/shard_map/ppermute | solution.py:103
  382.3 11.5 %collective-permute-start.10 = (f32[2,16,1024]{2,1,0:T(8,128)S(1)}, f32[2,16,1024]{2,1,0:T(8,128)S(1)}, u32[]{:S(2)}, u32[]{:S(2)}) collective-permute-start(f32[2,16,1024]{2,1,0:T(8,128)S(1)} %select_bitcast_fusion.7), channel_id=1, source_target_pairs={{0,4},{1,5},{2,6},{3,7},{4,0},{5,1},{6,2},{7,3},{8,12},{9,13},{10,... | collective-permute-start | bytes 393224 | tf_op jit(solution)/shard_map/ppermute | solution.py:103
  393.8 14.1 %collective-permute-start.11 = (f32[1,16,1024]{2,1,0:T(8,128)S(1)}, f32[1,16,1024]{2,1,0:T(8,128)S(1)}, u32[]{:S(2)}, u32[]{:S(2)}) collective-permute-start(f32[1,16,1024]{2,1,0:T(8,128)S(1)} %select_bitcast_fusion.10), channel_id=1, source_target_pairs={{0,8},{1,9},{2,10},{3,11},{4,12},{5,13},{6,14},{7,15},{8,0},{9,1},... | collective-permute-start | bytes 196616 | tf_op jit(solution)/shard_map/ppermute | solution.py:103
  406.0 2.6 collective-permute-start.12
  434.0 1.0 copy-start
  434.2 1.6 collective-permute-start.13

commit v5 on v4

--- a/solution.py
+++ b/solution.py
@@ -7,7 +7,7 @@
 from jax.sharding import PartitionSpec as P
 
 AXIS = "vir"
-CHUNKS = (8, 32, 16, 8)
+CHUNKS = (24, 32, 8)
 STEPS = (2, 1)
 SUBLANES = 8
 
@@ -78,6 +78,30 @@
     )(blocks, amplitudes)
 
 
+def combine_kernel(core, cols, other, mine, base, energy, out):
+    first = core[0] == 0
+    half = cols.shape[2] // 2
+    for k in range(cols.shape[0]):
+        even = jnp.where(first, cols[k], other[k])
+        odd = jnp.where(first, other[k], cols[k])
+        both = jnp.concatenate([even, odd], axis=0)
+        block = jnp.where(first, both[:, :half], both[:, half:]).T
+        at = pl.ds(k * block.shape[1], block.shape[1])
+        out[:, 0, at] = (mine[:, at] + block) / (base[...] - energy[:, at])
+
+
+def combined(core, cols, other, mine, base, energy):
+    rows, a = mine.shape
+    return pl.pallas_call(
+        combine_kernel,
+        in_specs=[pl.BlockSpec(memory_space=pltpu.SMEM)]
+        + [pl.BlockSpec(memory_space=pltpu.VMEM)] * 5,
+        out_specs=pl.BlockSpec(memory_space=pltpu.VMEM),
+        out_shape=jax.ShapeDtypeStruct((rows, 1, a), jnp.float32),
+        compiler_params=pltpu.CompilerParams(vmem_limit_bytes=16 * 1024 * 1024),
+    )(core, cols, other, mine, base, energy)
+
+
 def exchanged_body(amplitudes, integrals, pair_energy, vir_energy):
     n = lax.axis_size(AXIS)
     chips = n // 2
@@ -118,6 +142,8 @@
                 blocks = halve(blocks, bit)
                 bit *= 2
             near.append(blocks)
+            if q == len(CHUNKS) - 1:
+                blocks = after(blocks, received[q])
             done.append(halve(blocks, bit)[0])
     early = jnp.concatenate(done, axis=0)
     er, late = early.shape[0], CHUNKS[-1]
@@ -125,10 +151,10 @@
     row_part = part.reshape(chips, late, chips, width).transpose(0, 2, 1, 3).reshape(chips, -1, width)
     col_part = part.reshape(chips * late, chips, width).transpose(1, 0, 2)
     early_part = early.reshape(er, chips, width).transpose(1, 0, 2)
-    exponent = exponent_of(jnp.maximum(jnp.max(jnp.abs(part)), jnp.max(jnp.abs(early))))
-    parts = jnp.concatenate([row_part, col_part, early_part], axis=1) * jnp.exp2(-exponent)
-    tag = jnp.full((chips, SUBLANES, width), exponent, jnp.float32)
-    sent = jnp.concatenate([parts, tag], axis=1).astype(jnp.float16)
+    parts = jnp.concatenate([row_part, col_part, early_part], axis=1)
+    exponent = exponent_of(jnp.max(jnp.abs(parts), axis=(0, 1), keepdims=True))
+    tag = jnp.broadcast_to(exponent, (chips, SUBLANES, width))
+    sent = jnp.concatenate([parts * jnp.exp2(-exponent), tag], axis=1).astype(jnp.float16)
     got = exchange(sent, same_core).astype(jnp.float32)
     got = got[:, :-SUBLANES] * jnp.exp2(got[:, -1:, :])
     split = chips * late
@@ -137,11 +163,9 @@
     late_cols = sums[split:].reshape(chips, late, width)
     cols = jnp.concatenate([got[:, 2 * split :], late_cols], axis=1)
     other = lax.ppermute(cols, AXIS, [(i, i ^ 1) for i in range(n)])
-    stacked = jnp.where(core == 0, jnp.stack([cols, other], 1), jnp.stack([other, cols], 1))
-    stacked = stacked.reshape(n * rows, 2, width // 2)
-    swapped = jnp.where(core == 0, stacked[:, 0], stacked[:, 1])
-    paired = jnp.concatenate([early, late_rows], axis=0) + swapped.T
-    return paired[:, None, :] / denominator(pair_energy, vir_energy, me * rows, rows)
+    mine = jnp.concatenate([early, late_rows], axis=0)
+    base = pair_energy - lax.dynamic_slice_in_dim(vir_energy, me * rows, rows, 0)
+    return combined(core.reshape(1), cols, other, mine, base[:, None], vir_energy[None, :])
 
 
 def solution(mesh):

time: 439 us -> 430 us (0.979)
  starting transfers between devices: 47.7 us -> 57.1 us
  blocking collectives: 23.1 us -> 15.9 us
  Pallas kernels: 37.9 us -> 33.2 us
  local copies, waits for them, and re-layouts: 22.9 us -> 18.5 us
    all_to_all x4 -> x3, waiting for transfers between devices: 32.6 us -> 106 us  [exchange(): lax.all_to_all(x, AXIS, split_axis=0, concat_axis=0, tiled=True, axis_ind...]
    ppermute x13 -> x9, waiting for transfers between devices: 268 us -> 196 us  [halve(): return mine + lax.ppermute(other, AXIS, [(i, i ^ bit) for i in range(n)])]
    all_to_all x4 -> x3, starting transfers between devices: 26.9 us -> 39.3 us  [exchange(): lax.all_to_all(x, AXIS, split_axis=0, concat_axis=0, tiled=True, axis_ind...]
    all_to_all x1, blocking collectives: 23.1 us -> 15.9 us  [exchange(): lax.all_to_all(x, AXIS, split_axis=0, concat_axis=0, tiled=True, axis_ind...]
    pallas_call x4 -> x3, Pallas kernels: 37.9 us -> 32.1 us  [product(): pl.pallas_call(product_kernel, grid=(own // step,), in_specs=[pl.BlockSpe...]
    ppermute x13 -> x9, starting transfers between devices: 20.7 us -> 17.7 us  [halve(): return mine + lax.ppermute(other, AXIS, [(i, i ^ bit) for i in range(n)])]
    slice x4 -> x3, local copies, waits for them, and re-layouts: 19.9 us -> 18.1 us  [exchanged_body(): x = x[:, :, starts[q]:starts[q] + r]]
  transfers between devices with their start and end apart: 18 -> 13, of which waited for: 14 -> 10; matrix products, arithmetic and copies ran while one was open for 4% -> 3% of each run, Pallas kernels for 9% -> 7%
where the time goes in v5:
time: 430 us
  waiting for transfers between devices  302 us (70%)
  starting transfers between devices  57.1 us (13%)
  Pallas kernels  33.2 us (8%)
  local copies, waits for them, and re-layouts  18.5 us (4%)
  blocking collectives  15.9 us (4%)
    ppermute x9, waiting for transfers between devices, halve(): return mine + lax.ppermute(other, AXIS, [(i, i ^ bit) for i in range(n)])  196 us
    all_to_all x3, waiting for transfers between devices, exchange(): lax.all_to_all(x, AXIS, split_axis=0, concat_axis=0, tiled=True, axis_ind...  106 us
    all_to_all x3, starting transfers between devices, exchange(): lax.all_to_all(x, AXIS, split_axis=0, concat_axis=0, tiled=True, axis_ind...  39.3 us
    pallas_call x3, Pallas kernels, product(): pl.pallas_call(product_kernel, grid=(own // step,), in_specs=[pl.BlockSpe...  32.1 us
    slice x3, local copies, waits for them, and re-layouts, exchanged_body(): x = x[:, :, starts[q]:starts[q] + r]  18.1 us
    ppermute x9, starting transfers between devices, halve(): return mine + lax.ppermute(other, AXIS, [(i, i ^ bit) for i in range(n)])  17.7 us
    all_to_all x1, blocking collectives, exchange(): lax.all_to_all(x, AXIS, split_axis=0, concat_axis=0, tiled=True, axis_ind...  15.9 us
  transfers between devices with their start and end apart: 13, of which 10 were waited for; matrix products, arithmetic and copies ran while one was open for 3% of the time, Pallas kernels for 7%

profile of v5, /device:TPU:0, one launch (start us, length us, event | category | flops | bytes accessed | tf_op | source)
XLA Modules:
  0.0 429.8 jit_solution(12142837104632246999)
XLA Ops:
  0.0 6.5 %slice.126 = bf16[16,8,24,1024]{3,2,1,0:T(8,128)(2,1)} slice(bf16[16,8,64,1024]{3,2,1,0:T(8,128)(2,1)} %bitcast.180), slice={[0:16], [0:8], [0:24], [0:1024]} | slice | bytes 12582912 | tf_op jit(solution)/shard_map/slice | solution.py:134
  6.5 7.4 %all-to-all-start = ((bf16[16,8,24,1024]{3,2,1,0:T(8,128)(2,1)}), bf16[16,8,24,1024]{3,2,1,0:T(8,128)(2,1)}, u32[]{:S(2)}, u32[]{:S(2)}) async-start(bf16[16,8,24,1024]{3,2,1,0:T(8,128)(2,1)} %slice.126), calls=%async_computation | async-start | bytes 12582912 | tf_op jit(solution)/shard_map/all_to_all | solution.py:118
  13.9 8.5 %slice.127 = bf16[16,8,32,1024]{3,2,1,0:T(8,128)(2,1)} slice(bf16[16,8,64,1024]{3,2,1,0:T(8,128)(2,1)} %bitcast.181), slice={[0:16], [0:8], [24:56], [0:1024]} | slice | bytes 16777216 | tf_op jit(solution)/shard_map/slice | solution.py:134
  22.4 105.7 %all-to-all-done.blocks = bf16[16,8,24,1024]{3,2,1,0:T(8,128)(2,1)} async-done(((bf16[16,8,24,1024]{3,2,1,0:T(8,128)(2,1)}), bf16[16,8,24,1024]{3,2,1,0:T(8,128)(2,1)}, u32[]{:S(2)}, u32[]{:S(2)}) %all-to-all-start) | async-done | bytes 6291488 | tf_op jit(solution)/shard_map/all_to_all | solution.py:118
  128.1 28.1 %all-to-all-start.1 = ((bf16[16,8,32,1024]{3,2,1,0:T(8,128)(2,1)}), bf16[16,8,32,1024]{3,2,1,0:T(8,128)(2,1)}, u32[]{:S(2)}, u32[]{:S(2)}) async-start(bf16[16,8,32,1024]{3,2,1,0:T(8,128)(2,1)} %slice.127), calls=%async_computation.1 | async-start | bytes 16777216 | tf_op jit(solution)/shard_map/all_to_all | solution.py:118
  156.3 11.3 %shard_map.46 = f32[384,1024]{1,0:T(8,128)S(1)} custom-call(bf16[16,8,24,1024]{3,2,1,0:T(8,128)(2,1)} %all-to-all-done.blocks, bf16[8,1024,1024]{2,1,0:T(8,128)(2,1)} %amp.5), custom_call_target="tpu_custom_call" | custom-call | flops 6442450944 | bytes 24641536 | tf_op jit(solution)/shard_map/pallas_call | solution.py:63
  167.5 0.1 select_bitcast_fusion.1
  167.7 0.4 collective-permute-start
  168.1 1.9 collective-permute-done
  170.0 0.2 bitcast_add_fusion.1
  170.3 1.9 collective-permute-start.1
  172.2 41.5 %collective-permute-done.1 = f32[4,24,1024]{2,1,0:T(8,128)S(1)} collective-permute-done((f32[4,24,1024]{2,1,0:T(8,128)S(1)}, f32[4,24,1024]{2,1,0:T(8,128)S(1)}, u32[]{:S(2)}, u32[]{:S(2)}) %collective-permute-start.1) | collective-permute-done | bytes 393248 | tf_op jit(solution)/shard_map/ppermute | solution.py:127
  213.7 0.1 fusion.3
  213.8 0.1 collective-permute-start.2
  213.9 82.6 %collective-permute-done.2 = f32[2,24,1024]{2,1,0:T(8,128)S(1)} collective-permute-done((f32[2,24,1024]{2,1,0:T(8,128)S(1)}, f32[2,24,1024]{2,1,0:T(8,128)S(1)}, u32[]{:S(2)}, u32[]{:S(2)}) %collective-permute-start.2) | collective-permute-done | bytes 196640 | tf_op jit(solution)/shard_map/ppermute | solution.py:127
  296.5 4.6 %collective-permute-start.3 = (f32[1,24,1024]{2,1,0:T(8,128)S(1)}, f32[1,24,1024]{2,1,0:T(8,128)S(1)}, u32[]{:S(2)}, u32[]{:S(2)}) collective-permute-start(f32[1,24,1024]{2,1,0:T(8,128)S(1)} %select_bitcast_fusion.8), channel_id=1, source_target_pairs={{0,8},{1,9},{2,10},{3,11},{4,12},{5,13},{6,14},{7,15},{8,0},{9,1},... | collective-permute-start | bytes 294920 | tf_op jit(solution)/shard_map/ppermute | solution.py:127
  301.1 3.1 slice.100
  304.2 40.1 %collective-permute-done.3 = f32[1,24,1024]{2,1,0:T(8,128)S(1)} collective-permute-done((f32[1,24,1024]{2,1,0:T(8,128)S(1)}, f32[1,24,1024]{2,1,0:T(8,128)S(1)}, u32[]{:S(2)}, u32[]{:S(2)}) %collective-permute-start.3) | collective-permute-done | bytes 98336 | tf_op jit(solution)/shard_map/ppermute | solution.py:127
  344.4 0.0 all-to-all-done.1.blocks
  344.4 3.7 all-to-all-start.2
  348.1 13.3 %shard_map.48 = f32[512,1024]{1,0:T(8,128)S(1)} custom-call(bf16[16,8,32,1024]{3,2,1,0:T(8,128)(2,1)} %all-to-all-done.1.blocks, bf16[8,1024,1024]{2,1,0:T(8,128)(2,1)} %amp.5), custom_call_target="tpu_custom_call" | custom-call | flops 8589934592 | bytes 27262976 | tf_op jit(solution)/shard_map/pallas_call | solution.py:63
  361.4 0.2 select_bitcast_fusion
  361.6 0.4 collective-permute-start.5
  362.0 2.3 collective-permute-done.5
  364.3 0.3 bitcast_add_fusion
  364.6 0.1 select_bitcast_fusion.2
  364.7 1.9 collective-permute-start.6
  366.6 18.3 %collective-permute-done.6 = f32[4,32,1024]{2,1,0:T(8,128)S(1)} collective-permute-done((f32[4,32,1024]{2,1,0:T(8,128)S(1)}, f32[4,32,1024]{2,1,0:T(8,128)S(1)}, u32[]{:S(2)}, u32[]{:S(2)}) %collective-permute-start.6) | collective-permute-done | bytes 524320 | tf_op jit(solution)/shard_map/ppermute | solution.py:127
  384.9 0.1 fusion.1
  385.1 4.4 %collective-permute-start.7 = (f32[2,32,1024]{2,1,0:T(8,128)S(1)}, f32[2,32,1024]{2,1,0:T(8,128)S(1)}, u32[]{:S(2)}, u32[]{:S(2)}) collective-permute-start(f32[2,32,1024]{2,1,0:T(8,128)S(1)} %select_bitcast_fusion.4), channel_id=1, source_target_pairs={{0,4},{1,5},{2,6},{3,7},{4,0},{5,1},{6,2},{7,3},{8,12},{9,13},{10,... | collective-permute-start | bytes 786440 | tf_op jit(solution)/shard_map/ppermute | solution.py:127
  389.5 7.7 %collective-permute-done.7 = f32[2,32,1024]{2,1,0:T(8,128)S(1)} collective-permute-done((f32[2,32,1024]{2,1,0:T(8,128)S(1)}, f32[2,32,1024]{2,1,0:T(8,128)S(1)}, u32[]{:S(2)}, u32[]{:S(2)}) %collective-permute-start.7) | collective-permute-done | bytes 262176 | tf_op jit(solution)/shard_map/ppermute | solution.py:127
  397.2 0.0 all-to-all-done.2.blocks
  397.2 4.0 collective-permute-start.8
  401.2 7.5 %shard_map.47 = f32[128,1024]{1,0:T(8,128)S(1)} custom-call(bf16[16,8,8,1024]{3,2,1,0:T(8,128)(2,1)S(1)} %all-to-all-done.2.blocks, bf16[8,1024,1024]{2,1,0:T(8,128)(2,1)} %amp.5), custom_call_target="tpu_custom_call" | custom-call | flops 2147483648 | bytes 19398656 | tf_op jit(solution)/shard_map/pallas_call | solution.py:63
  408.8 0.1 collective-permute-start.4
  408.9 0.0 collective-permute-done.8
  409.0 1.4 collective-permute-done.4
  410.5 0.1 copy.84
  410.6 0.1 abs_reduce_fusion
  410.7 0.1 multiply_convert_fusion
  410.8 0.1 pad_maximum_fusion.1
  410.9 15.9 %all_to_all.20 = f16[8,192,128]{2,1,0:T(8,128)(2,1)S(1)} all-to-all(f16[8,192,128]{2,1,0:T(8,128)(2,1)S(1)} %pad_maximum_fusion.1), channel_id=1, replica_groups={{0,2,4,6,8,10,12,14},{1,3,5,7,9,11,13,15},{16,18,20,22,24,26,28,30},{17..., dimensions={0} | all-to-all | bytes 786432 | tf_op jit(solution)/shard_map/all_to_all | solution.py:118
  426.8 0.0 copy-start
  426.8 0.1 convert_element_type.4
  426.9 0.1 slice_multiply_fusion
  427.1 0.1 collective-permute-start.9
  427.8 0.0 copy-done
  427.8 0.1 subtract_bitcast_fusion
  427.9 0.1 copy.67.base
  428.0 0.7 collective-permute-done.9.other
  428.7 1.2 shard_map.49
  (25 shorter events, 0.6 us)
Async XLA Ops:
  6.5 121.6 %all-to-all-start = ((bf16[16,8,24,1024]{3,2,1,0:T(8,128)(2,1)}), bf16[16,8,24,1024]{3,2,1,0:T(8,128)(2,1)}, u32[]{:S(2)}, u32[]{:S(2)}) async-start(bf16[16,8,24,1024]{3,2,1,0:T(8,128)(2,1)} %slice.126), calls=%async_computation | async-start | bytes 12582912 | tf_op jit(solution)/shard_map/all_to_all | solution.py:118
  128.1 216.2 %all-to-all-start.1 = ((bf16[16,8,32,1024]{3,2,1,0:T(8,128)(2,1)}), bf16[16,8,32,1024]{3,2,1,0:T(8,128)(2,1)}, u32[]{:S(2)}, u32[]{:S(2)}) async-start(bf16[16,8,32,1024]{3,2,1,0:T(8,128)(2,1)} %slice.127), calls=%async_computation.1 | async-start | bytes 16777216 | tf_op jit(solution)/shard_map/all_to_all | solution.py:118
  167.7 2.4 collective-permute-start
  170.3 43.4 %collective-permute-start.1 = (f32[4,24,1024]{2,1,0:T(8,128)S(1)}, f32[4,24,1024]{2,1,0:T(8,128)S(1)}, u32[]{:S(2)}, u32[]{:S(2)}) collective-permute-start(f32[4,24,1024]{2,1,0:T(8,128)S(1)} %select_bitcast_fusion.3), channel_id=1, source_target_pairs={{0,2},{1,3},{2,0},{3,1},{4,6},{5,7},{6,4},{7,5},{8,10},{9,11},{10,... | collective-permute-start | bytes 1179656 | tf_op jit(solution)/shard_map/ppermute | solution.py:127
  213.8 82.7 %collective-permute-start.2 = (f32[2,24,1024]{2,1,0:T(8,128)S(1)}, f32[2,24,1024]{2,1,0:T(8,128)S(1)}, u32[]{:S(2)}, u32[]{:S(2)}) collective-permute-start(f32[2,24,1024]{2,1,0:T(8,128)S(1)} %select_bitcast_fusion.6), channel_id=1, source_target_pairs={{0,4},{1,5},{2,6},{3,7},{4,0},{5,1},{6,2},{7,3},{8,12},{9,13},{10,... | collective-permute-start | bytes 589832 | tf_op jit(solution)/shard_map/ppermute | solution.py:127
  296.5 47.8 %collective-permute-start.3 = (f32[1,24,1024]{2,1,0:T(8,128)S(1)}, f32[1,24,1024]{2,1,0:T(8,128)S(1)}, u32[]{:S(2)}, u32[]{:S(2)}) collective-permute-start(f32[1,24,1024]{2,1,0:T(8,128)S(1)} %select_bitcast_fusion.8), channel_id=1, source_target_pairs={{0,8},{1,9},{2,10},{3,11},{4,12},{5,13},{6,14},{7,15},{8,0},{9,1},... | collective-permute-start | bytes 294920 | tf_op jit(solution)/shard_map/ppermute | solution.py:127
  344.4 52.8 %all-to-all-start.2 = ((bf16[16,8,8,1024]{3,2,1,0:T(8,128)(2,1)}), bf16[16,8,8,1024]{3,2,1,0:T(8,128)(2,1)S(1)}, u32[]{:S(2)}, u32[]{:S(2)}) async-start(bf16[16,8,8,1024]{3,2,1,0:T(8,128)(2,1)} %slice.100), calls=%async_computation.2 | async-start | bytes 4194304 | tf_op jit(solution)/shard_map/all_to_all | solution.py:118
  361.6 2.7 collective-permute-start.5
  364.7 20.2 %collective-permute-start.6 = (f32[4,32,1024]{2,1,0:T(8,128)S(1)}, f32[4,32,1024]{2,1,0:T(8,128)S(1)}, u32[]{:S(2)}, u32[]{:S(2)}) collective-permute-start(f32[4,32,1024]{2,1,0:T(8,128)S(1)} %select_bitcast_fusion.2), channel_id=1, source_target_pairs={{0,2},{1,3},{2,0},{3,1},{4,6},{5,7},{6,4},{7,5},{8,10},{9,11},{10,... | collective-permute-start | bytes 1572872 | tf_op jit(solution)/shard_map/ppermute | solution.py:127
  385.1 12.1 %collective-permute-start.7 = (f32[2,32,1024]{2,1,0:T(8,128)S(1)}, f32[2,32,1024]{2,1,0:T(8,128)S(1)}, u32[]{:S(2)}, u32[]{:S(2)}) collective-permute-start(f32[2,32,1024]{2,1,0:T(8,128)S(1)} %select_bitcast_fusion.4), channel_id=1, source_target_pairs={{0,4},{1,5},{2,6},{3,7},{4,0},{5,1},{6,2},{7,3},{8,12},{9,13},{10,... | collective-permute-start | bytes 786440 | tf_op jit(solution)/shard_map/ppermute | solution.py:127
  397.2 11.7 %collective-permute-start.8 = (f32[1,32,1024]{2,1,0:T(8,128)S(1)}, f32[1,32,1024]{2,1,0:T(8,128)S(1)}, u32[]{:S(2)}, u32[]{:S(2)}) collective-permute-start(f32[1,32,1024]{2,1,0:T(8,128)S(1)} %select_bitcast_fusion.7), channel_id=1, source_target_pairs={{0,8},{1,9},{2,10},{3,11},{4,12},{5,13},{6,14},{7,15},{8,0},{9,1},... | collective-permute-start | bytes 393224 | tf_op jit(solution)/shard_map/ppermute | solution.py:127
  408.8 1.6 collective-permute-start.4
  426.8 1.0 copy-start
  427.1 1.6 collective-permute-start.9

commit v6 on v5

--- a/solution.py
+++ b/solution.py
@@ -7,9 +7,10 @@
 from jax.sharding import PartitionSpec as P
 
 AXIS = "vir"
-CHUNKS = (24, 32, 8)
+CHUNKS = (32, 24, 8)
 STEPS = (2, 1)
 SUBLANES = 8
+PIECES = 16
 
 
 def denominator(pair_energy, vir_energy, start, rows):
@@ -33,6 +34,47 @@
 
 def after(x, *deps):
     return lax.optimization_barrier((x, *deps))[0] if deps else x
+
+
+def head_kernel(source, out, held, load_sem, store_sem):
+    m, r, _ = held.shape
+    size = m // load_sem.shape[0]
+    stores = []
+    loads = []
+    for k in range(load_sem.shape[0]):
+        at = pl.ds(k * size, size)
+        loads.append(
+            pltpu.make_async_copy(source.at[at, pl.ds(0, r)], held.at[at], load_sem.at[k])
+        )
+        stores.append(pltpu.make_async_copy(held.at[at], out.at[at], store_sem.at[k]))
+    for load in loads:
+        load.start()
+    for load, store in zip(loads, stores):
+        load.wait()
+        store.start()
+    for store in stores:
+        store.wait()
+
+
+def head(source, r):
+    m, _, e = source.shape
+    shape = (m, r, e)
+    pieces = next(k for k in (PIECES, 8, 4, 2, 1) if m % k == 0)
+    return pl.pallas_call(
+        head_kernel,
+        in_specs=[pl.BlockSpec(memory_space=pl.ANY)],
+        out_specs=pl.BlockSpec(memory_space=pl.ANY),
+        out_shape=jax.ShapeDtypeStruct(shape, source.dtype),
+        scratch_shapes=[
+            pltpu.VMEM(shape, source.dtype),
+            pltpu.SemaphoreType.DMA((pieces,)),
+            pltpu.SemaphoreType.DMA((pieces,)),
+        ],
+        compiler_params=pltpu.CompilerParams(vmem_limit_bytes=60 * 1024 * 1024),
+        cost_estimate=pl.CostEstimate(
+            flops=0, bytes_accessed=4 * m * r * e, transcendentals=0
+        ),
+    )(source)
 
 
 def product_kernel(blocks, amp, out):
@@ -126,14 +168,17 @@
         other = jnp.where(odd, pair[:, 0], pair[:, 1])
         return mine + lax.ppermute(other, AXIS, [(i, i ^ bit) for i in range(n)])
 
-    received, near, done = [], [], []
+    received, near = [], []
     for q, r in enumerate(CHUNKS):
         x = source
         if q >= 2:
             x = after(x, received[q - 2])
-        x = x[:, :, starts[q] : starts[q] + r]
+        if q == 0 and r % 16 == 0:
+            x = head(x.reshape(n * own, rows, e), r).reshape(n, own, r, e)
+        else:
+            x = x[:, :, starts[q] : starts[q] + r]
         if q >= 1:
-            x = after(x, received[q - 1], *done[q - 2 : q - 1] if q >= 2 else ())
+            x = after(x, received[q - 1], *near[q - 2 : q - 1] if q >= 2 else ())
         received.append(exchange(x))
         if q >= 1:
             blocks = product(received[q - 1], amplitudes).reshape(n, CHUNKS[q - 1], a)
@@ -142,10 +187,8 @@
                 blocks = halve(blocks, bit)
                 bit *= 2
             near.append(blocks)
-            if q == len(CHUNKS) - 1:
-                blocks = after(blocks, received[q])
-            done.append(halve(blocks, bit)[0])
-    early = jnp.concatenate(done, axis=0)
+    split = jnp.concatenate(near, axis=1)
+    early = halve(after(split, received[-1]), chips)[0]
     er, late = early.shape[0], CHUNKS[-1]
     part = halve(product(received[-1], amplitudes).reshape(n, late, a), 1)
     row_part = part.reshape(chips, late, chips, width).transpose(0, 2, 1, 3).reshape(chips, -1, width)

time: 430 us -> 425 us (0.988)
  waiting for transfers between devices: 302 us -> 271 us
  starting transfers between devices: 57.1 us -> 83.9 us
  local copies, waits for them, and re-layouts: 18.5 us -> 9.91 us
  Pallas kernels: 33.2 us -> 39.8 us
    ppermute x9 -> x8, waiting for transfers between devices: 196 us -> 119 us  [halve(): return mine + lax.ppermute(other, AXIS, [(i, i ^ bit) for i in range(n)])]
    all_to_all x3, waiting for transfers between devices: 106 us -> 150 us  [exchange(): lax.all_to_all(x, AXIS, split_axis=0, concat_axis=0, tiled=True, axis_ind...]
    all_to_all x3, starting transfers between devices: 39.3 us -> 72.1 us  [exchange(): lax.all_to_all(x, AXIS, split_axis=0, concat_axis=0, tiled=True, axis_ind...]
    slice x3 -> x2, local copies, waits for them, and re-layouts: 18.1 us -> 9.58 us  [exchanged_body(): x = x[:, :, starts[q]:starts[q] + r]]
    pallas_call x0 -> x1, Pallas kernels: none -> 6.59 us  [head(): pl.pallas_call(head_kernel, in_specs=[pl.BlockSpec(memory_space=pl.ANY)],...]
    ppermute x9 -> x8, starting transfers between devices: 17.7 us -> 11.7 us  [halve(): return mine + lax.ppermute(other, AXIS, [(i, i ^ bit) for i in range(n)])]
  transfers between devices with their start and end apart: 13 -> 12, of which waited for: 10 -> 10; matrix products, arithmetic and copies ran while one was open for 3% -> 3% of each run, Pallas kernels for 7% -> 8%
where the time goes in v6:
time: 425 us; the launch traced here: 424 us
  waiting for transfers between devices  271 us (64%)
  starting transfers between devices  83.9 us (20%)
  Pallas kernels  39.8 us (9%)
  blocking collectives  16.1 us (4%)
  local copies, waits for them, and re-layouts  9.91 us (2%)
    all_to_all x3, waiting for transfers between devices, exchange(): lax.all_to_all(x, AXIS, split_axis=0, concat_axis=0, tiled=True, axis_ind...  150 us
    ppermute x8, waiting for transfers between devices, halve(): return mine + lax.ppermute(other, AXIS, [(i, i ^ bit) for i in range(n)])  119 us
    all_to_all x3, starting transfers between devices, exchange(): lax.all_to_all(x, AXIS, split_axis=0, concat_axis=0, tiled=True, axis_ind...  72.1 us
    pallas_call x3, Pallas kernels, product(): pl.pallas_call(product_kernel, grid=(own // step,), in_specs=[pl.BlockSpe...  32.1 us
    all_to_all x1, blocking collectives, exchange(): lax.all_to_all(x, AXIS, split_axis=0, concat_axis=0, tiled=True, axis_ind...  16.1 us
    ppermute x8, starting transfers between devices, halve(): return mine + lax.ppermute(other, AXIS, [(i, i ^ bit) for i in range(n)])  11.7 us
    slice x2, local copies, waits for them, and re-layouts, exchanged_body(): x = x[:, :, starts[q]:starts[q] + r]  9.58 us
  transfers between devices with their start and end apart: 12, of which 10 were waited for; matrix products, arithmetic and copies ran while one was open for 3% of the time, Pallas kernels for 8%

profile of v6, /device:TPU:0, one launch (start us, length us, event | category | flops | bytes accessed | tf_op | source)
XLA Modules:
  0.0 424.4 jit_solution(190050923969404956)
XLA Ops:
  0.0 6.6 %shard_map.46 = bf16[128,32,1024]{2,1,0:T(8,128)(2,1)} custom-call(bf16[128,64,1024]{2,1,0:T(8,128)(2,1)} %bitcast.171), custom_call_target="tpu_custom_call" | custom-call | bytes 16777216 | tf_op jit(solution)/shard_map/pallas_call | solution.py:63
  6.6 7.4 %all-to-all-start = ((bf16[16,8,32,1024]{3,2,1,0:T(8,128)(2,1)}), bf16[16,8,32,1024]{3,2,1,0:T(8,128)(2,1)}, u32[]{:S(2)}, u32[]{:S(2)}) async-start(bf16[16,8,32,1024]{3,2,1,0:T(8,128)(2,1)} %bitcast.174), calls=%async_computation | async-start | bytes 16777216 | tf_op jit(solution)/shard_map/all_to_all | solution.py:160
  14.1 6.5 %slice.112 = bf16[16,8,24,1024]{3,2,1,0:T(8,128)(2,1)} slice(bf16[16,8,64,1024]{3,2,1,0:T(8,128)(2,1)} %bitcast.172), slice={[0:16], [0:8], [32:56], [0:1024]} | slice | bytes 12582912 | tf_op jit(solution)/shard_map/slice | solution.py:179
  20.5 144.2 %all-to-all-done.blocks = bf16[16,8,32,1024]{3,2,1,0:T(8,128)(2,1)} async-done(((bf16[16,8,32,1024]{3,2,1,0:T(8,128)(2,1)}), bf16[16,8,32,1024]{3,2,1,0:T(8,128)(2,1)}, u32[]{:S(2)}, u32[]{:S(2)}) %all-to-all-start) | async-done | bytes 8388640 | tf_op jit(solution)/shard_map/all_to_all | solution.py:160
  164.8 36.5 %all-to-all-start.1 = ((bf16[16,8,24,1024]{3,2,1,0:T(8,128)(2,1)}), bf16[16,8,24,1024]{3,2,1,0:T(8,128)(2,1)}, u32[]{:S(2)}, u32[]{:S(2)}) async-start(bf16[16,8,24,1024]{3,2,1,0:T(8,128)(2,1)} %slice.112), calls=%async_computation.1 | async-start | bytes 12582912 | tf_op jit(solution)/shard_map/all_to_all | solution.py:160
  201.3 13.3 %shard_map.47 = f32[512,1024]{1,0:T(8,128)S(1)} custom-call(bf16[16,8,32,1024]{3,2,1,0:T(8,128)(2,1)} %all-to-all-done.blocks, bf16[8,1024,1024]{2,1,0:T(8,128)(2,1)} %amp.5), custom_call_target="tpu_custom_call" | custom-call | flops 8589934592 | bytes 27262976 | tf_op jit(solution)/shard_map/pallas_call | solution.py:105
  214.6 0.2 select_bitcast_fusion
  214.8 0.4 collective-permute-start
  215.2 2.4 collective-permute-done
  217.6 1.5 bitcast_add_fusion
  219.1 0.1 select_bitcast_fusion.2
  219.2 1.9 collective-permute-start.1
  221.1 38.6 %collective-permute-done.1 = f32[4,32,1024]{2,1,0:T(8,128)S(1)} collective-permute-done((f32[4,32,1024]{2,1,0:T(8,128)S(1)}, f32[4,32,1024]{2,1,0:T(8,128)S(1)}, u32[]{:S(2)}, u32[]{:S(2)}) %collective-permute-start.1) | collective-permute-done | bytes 524320 | tf_op jit(solution)/shard_map/ppermute | solution.py:169
  259.7 0.1 fusion.1
  259.9 0.1 collective-permute-start.2
  259.9 3.1 slice.88
  263.1 46.2 %collective-permute-done.2 = f32[2,32,1024]{2,1,0:T(8,128)S(1)} collective-permute-done((f32[2,32,1024]{2,1,0:T(8,128)S(1)}, f32[2,32,1024]{2,1,0:T(8,128)S(1)}, u32[]{:S(2)}, u32[]{:S(2)}) %collective-permute-start.2) | collective-permute-done | bytes 262176 | tf_op jit(solution)/shard_map/ppermute | solution.py:169
  309.3 6.2 %all-to-all-done.1.blocks = bf16[16,8,24,1024]{3,2,1,0:T(8,128)(2,1)} async-done(((bf16[16,8,24,1024]{3,2,1,0:T(8,128)(2,1)}), bf16[16,8,24,1024]{3,2,1,0:T(8,128)(2,1)}, u32[]{:S(2)}, u32[]{:S(2)}) %all-to-all-start.1) | async-done | bytes 6291488 | tf_op jit(solution)/shard_map/all_to_all | solution.py:160
  315.5 28.1 %all-to-all-start.2 = ((bf16[16,8,8,1024]{3,2,1,0:T(8,128)(2,1)}), bf16[16,8,8,1024]{3,2,1,0:T(8,128)(2,1)S(1)}, u32[]{:S(2)}, u32[]{:S(2)}) async-start(bf16[16,8,8,1024]{3,2,1,0:T(8,128)(2,1)} %slice.88), calls=%async_computation.2 | async-start | bytes 4194304 | tf_op jit(solution)/shard_map/all_to_all | solution.py:160
  343.7 11.3 %shard_map.49 = f32[384,1024]{1,0:T(8,128)S(1)} custom-call(bf16[16,8,24,1024]{3,2,1,0:T(8,128)(2,1)} %all-to-all-done.1.blocks, bf16[8,1024,1024]{2,1,0:T(8,128)(2,1)} %amp.5), custom_call_target="tpu_custom_call" | custom-call | flops 6442450944 | bytes 24641536 | tf_op jit(solution)/shard_map/pallas_call | solution.py:105
  354.9 0.1 select_bitcast_fusion.1
  355.1 0.5 collective-permute-start.4
  355.5 1.9 collective-permute-done.4
  357.4 0.2 bitcast_add_fusion.1
  357.7 2.0 collective-permute-start.5
  359.7 17.1 %collective-permute-done.5 = f32[4,24,1024]{2,1,0:T(8,128)S(1)} collective-permute-done((f32[4,24,1024]{2,1,0:T(8,128)S(1)}, f32[4,24,1024]{2,1,0:T(8,128)S(1)}, u32[]{:S(2)}, u32[]{:S(2)}) %collective-permute-start.5) | collective-permute-done | bytes 393248 | tf_op jit(solution)/shard_map/ppermute | solution.py:169
  376.8 0.1 fusion.3
  376.9 2.3 collective-permute-start.6
  379.2 10.5 %collective-permute-done.6 = f32[2,24,1024]{2,1,0:T(8,128)S(1)} collective-permute-done((f32[2,24,1024]{2,1,0:T(8,128)S(1)}, f32[2,24,1024]{2,1,0:T(8,128)S(1)}, u32[]{:S(2)}, u32[]{:S(2)}) %collective-permute-start.6) | collective-permute-done | bytes 196640 | tf_op jit(solution)/shard_map/ppermute | solution.py:169
  389.7 0.0 all-to-all-done.2.blocks
  389.8 4.5 %collective-permute-start.7 = (f32[1,56,1024]{2,1,0:T(8,128)S(1)}, f32[1,56,1024]{2,1,0:T(8,128)S(1)}, u32[]{:S(2)}, u32[]{:S(2)}) collective-permute-start(f32[1,56,1024]{2,1,0:T(8,128)S(1)} %select_bitcast_fusion.6), channel_id=1, source_target_pairs={{0,8},{1,9},{2,10},{3,11},{4,12},{5,13},{6,14},{7,15},{8,0},{9,1},... | collective-permute-start | bytes 688136 | tf_op jit(solution)/shard_map/ppermute | solution.py:169
  394.2 7.5 %shard_map.48 = f32[128,1024]{1,0:T(8,128)S(1)} custom-call(bf16[16,8,8,1024]{3,2,1,0:T(8,128)(2,1)S(1)} %all-to-all-done.2.blocks, bf16[8,1024,1024]{2,1,0:T(8,128)(2,1)} %amp.5), custom_call_target="tpu_custom_call" | custom-call | flops 2147483648 | bytes 19398656 | tf_op jit(solution)/shard_map/pallas_call | solution.py:105
  401.8 0.1 collective-permute-start.3
  401.9 2.7 collective-permute-done.7
  404.7 0.0 collective-permute-done.3
  404.7 0.1 bitcast_add_fusion.2
  404.8 0.1 copy.81
  404.9 0.1 abs_reduce_fusion
  405.0 0.1 multiply_convert_fusion
  405.1 0.1 pad_maximum_fusion.2
  405.2 16.1 %all_to_all.20 = f16[8,192,128]{2,1,0:T(8,128)(2,1)S(1)} all-to-all(f16[8,192,128]{2,1,0:T(8,128)(2,1)S(1)} %pad_maximum_fusion.2), channel_id=1, replica_groups={{0,2,4,6,8,10,12,14},{1,3,5,7,9,11,13,15},{16,18,20,22,24,26,28,30},{17..., dimensions={0} | all-to-all | bytes 786432 | tf_op jit(solution)/shard_map/all_to_all | solution.py:160
  421.3 0.0 copy-start
  421.3 0.1 convert_element_type.4
  421.4 0.1 slice_multiply_fusion
  421.6 0.1 collective-permute-start.8
  422.3 0.0 copy-done
  422.3 0.1 subtract_bitcast_fusion
  422.4 0.1 copy.64.base
  422.5 0.7 collective-permute-done.8.other
  423.2 1.2 shard_map.50
  (20 shorter events, 0.6 us)
Async XLA Ops:
  6.6 158.2 %all-to-all-start = ((bf16[16,8,32,1024]{3,2,1,0:T(8,128)(2,1)}), bf16[16,8,32,1024]{3,2,1,0:T(8,128)(2,1)}, u32[]{:S(2)}, u32[]{:S(2)}) async-start(bf16[16,8,32,1024]{3,2,1,0:T(8,128)(2,1)} %bitcast.174), calls=%async_computation | async-start | bytes 16777216 | tf_op jit(solution)/shard_map/all_to_all | solution.py:160
  164.8 150.8 %all-to-all-start.1 = ((bf16[16,8,24,1024]{3,2,1,0:T(8,128)(2,1)}), bf16[16,8,24,1024]{3,2,1,0:T(8,128)(2,1)}, u32[]{:S(2)}, u32[]{:S(2)}) async-start(bf16[16,8,24,1024]{3,2,1,0:T(8,128)(2,1)} %slice.112), calls=%async_computation.1 | async-start | bytes 12582912 | tf_op jit(solution)/shard_map/all_to_all | solution.py:160
  214.8 2.9 collective-permute-start
  219.2 40.5 %collective-permute-start.1 = (f32[4,32,1024]{2,1,0:T(8,128)S(1)}, f32[4,32,1024]{2,1,0:T(8,128)S(1)}, u32[]{:S(2)}, u32[]{:S(2)}) collective-permute-start(f32[4,32,1024]{2,1,0:T(8,128)S(1)} %select_bitcast_fusion.2), channel_id=1, source_target_pairs={{0,2},{1,3},{2,0},{3,1},{4,6},{5,7},{6,4},{7,5},{8,10},{9,11},{10,... | collective-permute-start | bytes 1572872 | tf_op jit(solution)/shard_map/ppermute | solution.py:169
  259.9 49.4 %collective-permute-start.2 = (f32[2,32,1024]{2,1,0:T(8,128)S(1)}, f32[2,32,1024]{2,1,0:T(8,128)S(1)}, u32[]{:S(2)}, u32[]{:S(2)}) collective-permute-start(f32[2,32,1024]{2,1,0:T(8,128)S(1)} %select_bitcast_fusion.5), channel_id=1, source_target_pairs={{0,4},{1,5},{2,6},{3,7},{4,0},{5,1},{6,2},{7,3},{8,12},{9,13},{10,... | collective-permute-start | bytes 786440 | tf_op jit(solution)/shard_map/ppermute | solution.py:169
  315.5 74.2 %all-to-all-start.2 = ((bf16[16,8,8,1024]{3,2,1,0:T(8,128)(2,1)}), bf16[16,8,8,1024]{3,2,1,0:T(8,128)(2,1)S(1)}, u32[]{:S(2)}, u32[]{:S(2)}) async-start(bf16[16,8,8,1024]{3,2,1,0:T(8,128)(2,1)} %slice.88), calls=%async_computation.2 | async-start | bytes 4194304 | tf_op jit(solution)/shard_map/all_to_all | solution.py:160
  355.1 2.4 collective-permute-start.4
  357.7 19.1 %collective-permute-start.5 = (f32[4,24,1024]{2,1,0:T(8,128)S(1)}, f32[4,24,1024]{2,1,0:T(8,128)S(1)}, u32[]{:S(2)}, u32[]{:S(2)}) collective-permute-start(f32[4,24,1024]{2,1,0:T(8,128)S(1)} %select_bitcast_fusion.3), channel_id=1, source_target_pairs={{0,2},{1,3},{2,0},{3,1},{4,6},{5,7},{6,4},{7,5},{8,10},{9,11},{10,... | collective-permute-start | bytes 1179656 | tf_op jit(solution)/shard_map/ppermute | solution.py:169
  376.9 12.8 %collective-permute-start.6 = (f32[2,24,1024]{2,1,0:T(8,128)S(1)}, f32[2,24,1024]{2,1,0:T(8,128)S(1)}, u32[]{:S(2)}, u32[]{:S(2)}) collective-permute-start(f32[2,24,1024]{2,1,0:T(8,128)S(1)} %select_bitcast_fusion.7), channel_id=1, source_target_pairs={{0,4},{1,5},{2,6},{3,7},{4,0},{5,1},{6,2},{7,3},{8,12},{9,13},{10,... | collective-permute-start | bytes 589832 | tf_op jit(solution)/shard_map/ppermute | solution.py:169
  389.8 14.8 %collective-permute-start.7 = (f32[1,56,1024]{2,1,0:T(8,128)S(1)}, f32[1,56,1024]{2,1,0:T(8,128)S(1)}, u32[]{:S(2)}, u32[]{:S(2)}) collective-permute-start(f32[1,56,1024]{2,1,0:T(8,128)S(1)} %select_bitcast_fusion.6), channel_id=1, source_target_pairs={{0,8},{1,9},{2,10},{3,11},{4,12},{5,13},{6,14},{7,15},{8,0},{9,1},... | collective-permute-start | bytes 688136 | tf_op jit(solution)/shard_map/ppermute | solution.py:169
  401.8 2.9 collective-permute-start.3
  421.3 1.0 copy-start
  421.6 1.6 collective-permute-start.8
